TPU v7x, 128 devices: a whole 4x4x4 slice. The times are simulated.
128 devices in a mesh: gx: 8 (over x, core), gy: 16 (over z, y).
Axes of the slice: x: 4, y: 4, z: 4, core: 2. Of those that a mesh axis runs over, the one named last changes fastest.
Arguments:
- sources: float32 [3, 2, 2, 64, 512, 128], P(None, None, None, 'gx', 'gy'), may hold values from -15 to 15
- masks: int32 [3, 64, 512, 128], P(None, 'gx', 'gy'), may hold values 0 or 1
- absorption: float32 [64, 512, 128], P('gx', 'gy'), may hold values from 4 to 8
- plane_basis: float32 [8, 64, 512], P(None, 'gx', 'gy'), may hold values from -0.625 to 0.625
- depth_basis: float32 [8, 128], replicated, may hold values from -0.75 to 0.75
- coupling_blocks: bfloat16 [8, 16, 5, 128, 128], P('gx', 'gy'), may hold values from -0.125 to 0.125
- coupling_index: int32 [8, 16, 5], replicated, may hold values from 0 to 127
Outputs:
- solution: float32 [3, 2, 2, 64, 512, 128], P(None, None, None, 'gx', 'gy')
- residual: float32 [3, 2, 2, 64, 512, 128], P(None, None, None, 'gx', 'gy')
Inputs may be any that keep to these rules, and one draw needn't show every extreme that they name: `coupling_index`: tile numbers are p 16 + q for tile (p, q); entries may repeat.
All inputs are finite; a program needn't handle non-finite values. No bound on the sum of `masks` on one device may be relied on, other than what follows from the above.
Results may differ from a plain program's by a relative error of at most 0.0034.
Values may be sent and summed in bfloat16 or wider, within the bound.
No kernel may reach another device: no remote copies, remote signals or barrier semaphores. Data moves between devices by JAX's collectives and lax.ppermute only.
A program may use at most 128 MiB of HBM per device.

v0:
```python
import jax
import jax.numpy as jnp
from jax import lax
from jax.sharding import PartitionSpec as P

OV = 2
LSTEPS = 3
SWEEPS = 3
ITERS = 2


HIGH = lax.Precision.HIGHEST
wave_sq = 0.5
background = 1.0
contrast = 2.0


def with_halo(cells, sides, width):
    for axis, dim in sides:
        count = lax.axis_size(axis)
        ends = count - 1
        head = lax.slice_in_dim(cells, 0, width, axis=dim)
        tail = lax.slice_in_dim(cells, cells.shape[dim] - width, cells.shape[dim], axis=dim)
        cells = jnp.concatenate(
            [
                lax.ppermute(tail, axis, [(i, (i + 1) % count) for i in range(ends)]),
                cells,
                lax.ppermute(head, axis, [((i + 1) % count, i) for i in range(ends)]),
            ],
            axis=dim,
        )
    return cells


def neighbours(field):
    widths = [(0, 0)] * (field.ndim - 3) + [(1, 1)] * 3
    padded = jnp.pad(field, widths)
    total = padded[..., 2:, 1:-1, 1:-1] + padded[..., :-2, 1:-1, 1:-1]
    total = total + padded[..., 1:-1, 2:, 1:-1] + padded[..., 1:-1, :-2, 1:-1]
    total = total + padded[..., 1:-1, 1:-1, 2:] + padded[..., 1:-1, 1:-1, :-2]
    return total


def jacobi(source, inv_re, inv_im):
    field = jnp.zeros_like(source)
    for step in range(LSTEPS):
        total = source + neighbours(field)
        new_re = inv_re[:, None] * total[:, :, 0] - inv_im[:, None] * total[:, :, 1]
        new_im = inv_re[:, None] * total[:, :, 1] + inv_im[:, None] * total[:, :, 0]
        field = jnp.stack([new_re, new_im], axis=2)
    return field


def apply_operator(field, diag_re, diag_im):
    rimmed = with_halo(field, (("gx", 3), ("gy", 4)), 1)
    deep = jnp.pad(rimmed, [(0, 0)] * 5 + [(1, 1)])
    near = deep[..., 2:, 1:-1, 1:-1] + deep[..., :-2, 1:-1, 1:-1]
    near = near + deep[..., 1:-1, 2:, 1:-1] + deep[..., 1:-1, :-2, 1:-1]
    near = near + deep[..., 1:-1, 1:-1, 2:] + deep[..., 1:-1, 1:-1, :-2]
    part_re = diag_re[:, None] * field[:, :, 0] - diag_im * field[:, :, 1] - near[:, :, 0]
    part_im = diag_re[:, None] * field[:, :, 1] + diag_im * field[:, :, 0] - near[:, :, 1]
    return jnp.stack([part_re, part_im], axis=2)


def on_device(
    sources, masks, absorption, plane_basis, depth_basis, coupling_blocks, coupling_index
):
    variants, rhs_count, _, tile_x, tile_y, depth = sources.shape
    links = coupling_blocks.shape[2]
    width = coupling_blocks.shape[3]
    diag_re = 6.0 - wave_sq * (background + contrast * masks.astype(jnp.float32))
    stacked = jnp.concatenate([diag_re, absorption[None]], axis=0)
    widened = with_halo(stacked, (("gx", 1), ("gy", 2)), OV)
    ext_re = widened[:-1]
    ext_im = widened[-1]
    inside = jnp.broadcast_to(ext_im > 1.0, ext_re.shape)
    modulus = jnp.where(inside, ext_re * ext_re + ext_im * ext_im, 1.0)
    inv_re = jnp.where(inside, ext_re / modulus, 0.0)
    inv_im = jnp.where(inside, -ext_im / modulus, 0.0)
    own_tile = lax.axis_index("gx") * lax.axis_size("gy") + lax.axis_index("gy")
    flat_index = coupling_index.reshape(-1, links)
    own_index = lax.dynamic_index_in_dim(flat_index, own_tile, 0, keepdims=False)
    own_blocks = coupling_blocks.reshape(links, width, width)
    solution = jnp.zeros_like(sources)
    residual = sources
    for outer in range(ITERS):
        source = with_halo(residual, (("gx", 3), ("gy", 4)), OV)
        local = jacobi(source, inv_re, inv_im)[:, :, :, OV : OV + tile_x, OV : OV + tile_y]
        depthwise = jnp.einsum("vrcxyz,bz->vrcxyb", residual, depth_basis, precision=HIGH)
        coarse_residual = jnp.einsum("vrcxyb,axy->vrcab", depthwise, plane_basis, precision=HIGH)
        coarse_residual = coarse_residual.reshape(variants * rhs_count, width)
        iterate = coarse_residual
        for sweep in range(SWEEPS):
            rounded = iterate.astype(jnp.bfloat16)
            whole = lax.all_gather(rounded[None], ("gx", "gy"), axis=0, tiled=True)
            chosen = jnp.take(whole, own_index, axis=0)
            iterate = coarse_residual - jnp.einsum(
                "jfi,joi->fo", chosen, own_blocks, preferred_element_type=jnp.float32
            )
        modes = iterate.reshape(variants, rhs_count, 2, plane_basis.shape[0], depth_basis.shape[0])
        planar = jnp.einsum("vrcab,axy->vrcxyb", modes, plane_basis, precision=HIGH)
        direction = local + jnp.einsum("vrcxyb,bz->vrcxyz", planar, depth_basis, precision=HIGH)
        image = apply_operator(direction, diag_re, absorption)
        img_re, img_im = (image[:, :, 0], image[:, :, 1])
        res_re, res_im = (residual[:, :, 0], residual[:, :, 1])
        dot_re = jnp.sum(img_re * res_re + img_im * res_im, axis=(2, 3, 4))
        dot_im = jnp.sum(img_re * res_im - img_im * res_re, axis=(2, 3, 4))
        energy = jnp.sum(img_re * img_re + img_im * img_im, axis=(2, 3, 4))
        dot_re, dot_im, energy = lax.psum((dot_re, dot_im, energy), ("gx", "gy"))
        alpha_re = (dot_re / energy)[:, :, None, None, None]
        alpha_im = (dot_im / energy)[:, :, None, None, None]
        dir_re, dir_im = (direction[:, :, 0], direction[:, :, 1])
        solution = solution + jnp.stack(
            [alpha_re * dir_re - alpha_im * dir_im, alpha_re * dir_im + alpha_im * dir_re], axis=2
        )
        residual = residual - jnp.stack(
            [alpha_re * img_re - alpha_im * img_im, alpha_re * img_im + alpha_im * img_re], axis=2
        )
    return (solution, residual)


def solution(mesh):
    return jax.shard_map(
        on_device,
        mesh=mesh,
        in_specs=(
            P(None, None, None, "gx", "gy", None),
            P(None, "gx", "gy", None),
            P("gx", "gy", None),
            P(None, "gx", "gy"),
            P(),
            P("gx", "gy", None, None, None),
            P(),
        ),
        out_specs=(P(None, None, None, "gx", "gy", None), P(None, None, None, "gx", "gy", None)),
        check_vma=False,
    )
```

profile of v0, /device:TPU:1, one launch (start us, length us, event | category | flops | bytes accessed | tf_op | source)
XLA Modules:
  0.0 663.7 jit_solution(4070937029642708313)
XLA Ops:
  0.7 2.2 fusion.101
  2.9 4.5 collective-permute-start.4
  7.4 1.9 collective-permute-start.5
  10.5 2.1 collective-permute-start.1
  12.6 3.6 collective-permute-start
  16.2 6.2 fusion.86
  23.2 57.8 %all_gather.18 = bf16[128,6,128]{2,1,0:T(8,128)(2,1)S(1)} all-gather(bf16[1,6,128]{2,1,0:T(8,128)(2,1)S(1)} %convert_element_type.53), channel_id=1, replica_groups=mesh['gx'=8,'gy'=16] {'gx','gy'}, dimensions={0}, use_global_device_ids=true | all-gather | bytes 198144 | tf_op jit(solution)/shard_map/all_gather | solution.py:95
  82.0 55.8 %all-gather.4 = bf16[128,6,128]{2,1,0:T(8,128)(2,1)S(1)} all-gather(bf16[1,6,128]{2,1,0:T(8,128)(2,1)S(1)} %fusion.33), channel_id=2, replica_groups=mesh['gx'=8,'gy'=16] {'gx','gy'}, dimensions={0}, use_global_device_ids=true | all-gather | bytes 198144 | tf_op jit(solution)/shard_map/all_gather | solution.py:95
  138.5 55.8 %all-gather.5 = bf16[128,6,128]{2,1,0:T(8,128)(2,1)S(1)} all-gather(bf16[1,6,128]{2,1,0:T(8,128)(2,1)S(1)} %fusion.32), channel_id=3, replica_groups=mesh['gx'=8,'gy'=16] {'gx','gy'}, dimensions={0}, use_global_device_ids=true | all-gather | bytes 198144 | tf_op jit(solution)/shard_map/all_gather | solution.py:95
  197.8 4.0 collective-permute-start.2
  206.7 4.8 collective-permute-start.6
  214.0 2.7 select_maximum_fusion.3
  216.7 4.5 fusion.10
  221.6 2.7 select_maximum_fusion.2
  224.3 4.5 fusion.9
  229.9 2.7 copy_add_fusion
  232.6 4.3 collective-permute-start.8
  237.0 1.9 collective-permute-start.9
  239.6 1.9 collective-permute-done.9
  242.9 4.9 collective-permute-start.11
  248.9 3.1 select_maximum_fusion.8
  252.0 1.5 slice_add_fusion.22
  255.2 73.2 %all-reduce.8 = (f32[3,2]{1,0:T(4,128)S(1)}, f32[3,2]{1,0:T(4,128)S(1)}, f32[3,2]{1,0:T(4,128)S(1)}) all-reduce(f32[3,2]{1,0:T(4,128)S(1)} %get-tuple-element.6, f32[3,2]{1,0:T(4,128)S(1)} %get-tuple-element.8, f32[3,2]{1,0:T(4,128)S(1)} %get-tuple-element.5), channel_id=1, replica_groups=mesh['gx'=8,'gy'=16] {'gx','gy'}, use_global_device_ids=true, to_apply=%region_5.7 | all-reduce | flops 18 | bytes 144 | tf_op jit(solution)/shard_map/psum | solution.py:109
  328.4 3.2 multiply_subtract_fusion.6
  333.1 6.2 fusion.83
  339.3 2.1 collective-permute-start.12
  341.3 3.2 collective-permute-start.13
  346.7 58.9 %all_gather.21 = bf16[128,6,128]{2,1,0:T(8,128)(2,1)} all-gather(bf16[1,6,128]{2,1,0:T(8,128)(2,1)S(1)} %convert_element_type.57), channel_id=1, replica_groups=mesh['gx'=8,'gy'=16] {'gx','gy'}, dimensions={0}, use_global_device_ids=true | all-gather | bytes 198144 | tf_op jit(solution)/shard_map/all_gather | solution.py:95
  405.6 1.6 gather_fusion.3
  408.1 60.0 %all-gather.6 = bf16[128,6,128]{2,1,0:T(8,128)(2,1)} all-gather(bf16[1,6,128]{2,1,0:T(8,128)(2,1)S(1)} %fusion.31), channel_id=4, replica_groups=mesh['gx'=8,'gy'=16] {'gx','gy'}, dimensions={0}, use_global_device_ids=true | all-gather | bytes 198144 | tf_op jit(solution)/shard_map/all_gather | solution.py:95
  468.1 1.6 gather_fusion.4
  470.6 60.5 %all-gather.7 = bf16[128,6,128]{2,1,0:T(8,128)(2,1)} all-gather(bf16[1,6,128]{2,1,0:T(8,128)(2,1)S(1)} %fusion.30), channel_id=5, replica_groups=mesh['gx'=8,'gy'=16] {'gx','gy'}, dimensions={0}, use_global_device_ids=true | all-gather | bytes 198144 | tf_op jit(solution)/shard_map/all_gather | solution.py:95
  531.1 1.6 gather_fusion.5
  537.6 4.2 collective-permute-start.14
  545.5 2.7 select_maximum_fusion.1
  548.2 4.6 fusion.8
  553.1 2.7 select_maximum_fusion
  555.8 4.6 fusion.7
  561.4 2.7 fusion.14
  564.1 3.0 collective-permute-start.16
  567.1 2.6 collective-permute-start.17
  569.7 1.4 collective-permute-done.16
  573.7 5.0 collective-permute-start.19
  579.7 3.1 select_maximum_fusion.4
  582.8 1.5 slice_add_fusion.20
  587.0 69.8 %all-reduce.7 = (f32[3,2]{1,0:T(4,128)S(1)}, f32[3,2]{1,0:T(4,128)S(1)}, f32[3,2]{1,0:T(4,128)S(1)}) all-reduce(f32[3,2]{1,0:T(4,128)S(1)} %get-tuple-element.4, f32[3,2]{1,0:T(4,128)S(1)} %get-tuple-element.7, f32[3,2]{1,0:T(4,128)S(1)} %get-tuple-element.3), channel_id=1, replica_groups=mesh['gx'=8,'gy'=16] {'gx','gy'}, use_global_device_ids=true, to_apply=%region_11.13 | all-reduce | flops 18 | bytes 144 | tf_op jit(solution)/shard_map/psum | solution.py:109
  656.8 2.0 fusion.38
  660.8 2.6 maximum_add_fusion
  (149 shorter events, 43.6 us)
Async XLA Ops:
  0.6 81.2 %copy-start = (bf16[1,1,5,128,128]{4,3,2,1,0:T(8,128)(2,1)S(1)}, bf16[1,1,5,128,128]{4,3,2,1,0:T(8,128)(2,1)}, u32[]{:S(2)}) copy-start(bf16[1,1,5,128,128]{4,3,2,1,0:T(8,128)(2,1)} %param.14) | copy-start | bytes 491524
  0.6 15.6 %copy-start.2 = (f32[3,2,2,8,32,128]{5,4,3,2,1,0:T(8,128)S(1)}, f32[3,2,2,8,32,128]{5,4,3,2,1,0:T(8,128)}, u32[]{:S(2)}) copy-start(f32[3,2,2,8,32,128]{5,4,3,2,1,0:T(8,128)} %param.9) | copy-start | bytes 4718596
  0.7 9.8 %copy-start.19 = (f32[8,32,128]{2,1,0:T(8,128)S(1)}, f32[8,32,128]{2,1,0:T(8,128)}, u32[]{:S(2)}) copy-start(f32[8,32,128]{2,1,0:T(8,128)} %param.11) | copy-start | bytes 393220
  0.7 15.6 %copy-start.27 = (f32[8,128]{1,0:T(8,128)S(1)}, f32[8,128]{1,0:T(8,128)}, u32[]{:S(2)}) copy-start(f32[8,128]{1,0:T(8,128)} %param.13) | copy-start | bytes 12292
  2.9 200.2 %collective-permute-start.4 = (f32[3,2,2,2,32,128]{5,4,3,1,0,2:T(8,128)}, f32[3,2,2,2,32,128]{5,4,3,1,0,2:T(8,128)}, u32[]{:S(2)}, u32[]{:S(2)}) collective-permute-start(f32[3,2,2,2,32,128]{5,4,3,1,0,2:T(8,128)} %get-tuple-element.59), channel_id=1, source_target_pairs={{0,16},{16,32},{32,48},{48,64},{64,80},{80,96},{96,112},{1,17},{17... | collective-permute-start | bytes 1179656 | tf_op jit(solution)/shard_map/ppermute | solution.py:26
  7.4 15.0 %copy-start.26 = (f32[8,8,32]{2,1,0:T(8,128)S(1)}, f32[8,8,32]{2,1,0:T(8,128)}, u32[]{:S(2)}) copy-start(f32[8,8,32]{2,1,0:T(8,128)} %param.12) | copy-start | bytes 24580
  7.4 196.8 %collective-permute-start.5 = (f32[3,2,2,2,32,128]{5,4,3,1,0,2:T(8,128)}, f32[3,2,2,2,32,128]{5,4,3,1,0,2:T(8,128)}, u32[]{:S(2)}, u32[]{:S(2)}) collective-permute-start(f32[3,2,2,2,32,128]{5,4,3,1,0,2:T(8,128)} %get-tuple-element.58), channel_id=1, source_target_pairs={{16,0},{32,16},{48,32},{64,48},{80,64},{96,80},{112,96},{17,1},{33... | collective-permute-start | bytes 1179656 | tf_op jit(solution)/shard_map/ppermute | solution.py:28
  10.4 201.1 %copy-start.7 = (f32[3,8,32,128]{3,2,1,0:T(8,128)}, f32[3,8,32,128]{3,2,1,0:T(8,128)S(1)}, u32[]{:S(2)}) copy-start(f32[3,8,32,128]{3,2,1,0:T(8,128)S(1)} %multiply_subtract_fusion.8) | copy-start | bytes 1179652
  10.5 70.6 %copy-start.29 = (s32[8,16,5]{1,0,2:T(8,128)S(1)}, s32[8,16,5]{1,0,2:T(8,128)}, u32[]{:S(2)}) copy-start(s32[8,16,5]{1,0,2:T(8,128)} %param.15) | copy-start | bytes 7684
  10.5 186.0 %collective-permute-start.1 = (f32[4,2,32,128]{3,2,1,0:T(8,128)S(1)}, f32[4,2,32,128]{3,2,1,0:T(8,128)S(1)}, u32[]{:S(2)}, u32[]{:S(2)}) collective-permute-start(f32[4,2,32,128]{3,2,1,0:T(8,128)S(1)} %get-tuple-element.65), channel_id=1, source_target_pairs={{16,0},{32,16},{48,32},{64,48},{80,64},{96,80},{112,96},{17,1},{33... | collective-permute-start | bytes 393224 | tf_op jit(solution)/shard_map/ppermute | solution.py:28
  12.6 183.9 %collective-permute-start = (f32[4,2,32,128]{3,2,1,0:T(8,128)S(1)}, f32[4,2,32,128]{3,2,1,0:T(8,128)S(1)}, u32[]{:S(2)}, u32[]{:S(2)}) collective-permute-start(f32[4,2,32,128]{3,2,1,0:T(8,128)S(1)} %get-tuple-element.64), channel_id=1, source_target_pairs={{0,16},{16,32},{32,48},{48,64},{64,80},{80,96},{96,112},{1,17},{17... | collective-permute-start | bytes 393224 | tf_op jit(solution)/shard_map/ppermute | solution.py:26
  81.2 116.6 %copy-start.28 = (pred[5]{0:T(512)(128)(4,1)}, pred[5]{0:T(512)(128)(4,1)S(1)}, u32[]{:S(2)}) copy-start(pred[5]{0:T(512)(128)(4,1)S(1)} %get-tuple-element.21) | copy-start | bytes 19
  81.2 113.1 %copy-start.30 = (s32[1024]{0:T(1024)}, s32[1024]{0:T(1024)S(1)}, u32[]{:S(2)}) copy-start(s32[1024]{0:T(1024)S(1)} %pad_clamp_fusion) | copy-start | bytes 12292
  196.5 5.5 collective-permute-start.3
  197.8 5.2 collective-permute-start.2
  202.0 11.1 %copy-start.22 = (f32[12,36,128]{2,1,0:T(8,128)}, f32[12,36,128]{2,1,0:T(8,128)S(1)}, u32[]{:S(2)}) copy-start(f32[12,36,128]{2,1,0:T(8,128)S(1)} %fusion.51) | copy-start | bytes 663556
  205.4 6.5 collective-permute-start.7
  206.7 6.4 collective-permute-start.6
  211.9 17.0 %copy-start.3 = (f32[3,12,36,128]{3,2,1,0:T(8,128)}, f32[3,12,36,128]{3,2,1,0:T(8,128)S(1)}, u32[]{:S(2)}) copy-start(f32[3,12,36,128]{3,2,1,0:T(8,128)S(1)} %get-tuple-element.60) | copy-start | bytes 1990660
  211.9 17.0 %copy-start.5 = (f32[3,12,36,128]{3,2,1,0:T(8,128)}, f32[3,12,36,128]{3,2,1,0:T(8,128)S(1)}, u32[]{:S(2)}) copy-start(f32[3,12,36,128]{3,2,1,0:T(8,128)S(1)} %get-tuple-element.61) | copy-start | bytes 1990660
  232.6 7.0 %collective-permute-start.8 = (f32[3,2,2,1,32,128]{5,4,3,2,1,0:T(8,128)S(1)}, f32[3,2,2,1,32,128]{5,4,3,2,1,0:T(8,128)S(1)}, u32[]{:S(2)}, u32[]{:S(2)}) collective-permute-start(f32[3,2,2,1,32,128]{5,4,3,2,1,0:T(8,128)S(1)} %get-tuple-element.57), channel_id=1, source_target_pairs={{16,0},{32,16},{48,32},{64,48},{80,64},{96,80},{112,96},{17,1},{33... | collective-permute-start | bytes 589832 | tf_op jit(solution)/shard_map/ppermute | solution.py:28
  237.0 4.5 collective-permute-start.9
  241.6 6.2 collective-permute-start.10
  242.9 6.0 collective-permute-start.11
  252.0 1.5 copy-start.8
  253.5 1.1 copy-start.17
  331.7 1.4 copy-start.10
  331.9 202.8 %copy-start.14 = (f32[3,2,1,8,32,128]{5,4,3,2,1,0:T(8,128)}, f32[3,2,1,8,32,128]{5,4,3,2,1,0:T(8,128)S(1)}, u32[]{:S(2)}) copy-start(f32[3,2,1,8,32,128]{5,4,3,2,1,0:T(8,128)S(1)} %multiply_add_fusion.6) | copy-start | bytes 2359300
  339.3 195.5 %copy-start.11 = (f32[3,2,1,8,32,128]{5,4,3,2,1,0:T(8,128)S(1)}, f32[3,2,1,8,32,128]{5,4,3,2,1,0:T(8,128)}, u32[]{:S(2)}) copy-start(f32[3,2,1,8,32,128]{5,4,3,2,1,0:T(8,128)} %copy-done.10) | copy-start | bytes 2359300
  339.3 194.4 %collective-permute-start.12 = (f32[3,2,2,2,32,128]{5,4,3,1,0,2:T(8,128)}, f32[3,2,2,2,32,128]{5,4,3,1,0,2:T(8,128)}, u32[]{:S(2)}, u32[]{:S(2)}) collective-permute-start(f32[3,2,2,2,32,128]{5,4,3,1,0,2:T(8,128)} %get-tuple-element.55), channel_id=1, source_target_pairs={{0,16},{16,32},{32,48},{48,64},{64,80},{80,96},{96,112},{1,17},{17... | collective-permute-start | bytes 1179656 | tf_op jit(solution)/shard_map/ppermute | solution.py:26
  341.3 193.8 %collective-permute-start.13 = (f32[3,2,2,2,32,128]{5,4,3,1,0,2:T(8,128)}, f32[3,2,2,2,32,128]{5,4,3,1,0,2:T(8,128)}, u32[]{:S(2)}, u32[]{:S(2)}) collective-permute-start(f32[3,2,2,2,32,128]{5,4,3,1,0,2:T(8,128)} %get-tuple-element.54), channel_id=1, source_target_pairs={{16,0},{32,16},{48,32},{64,48},{80,64},{96,80},{112,96},{17,1},{33... | collective-permute-start | bytes 1179656 | tf_op jit(solution)/shard_map/ppermute | solution.py:28
  535.1 9.5 %copy-start.23 = (f32[12,36,128]{2,1,0:T(8,128)S(1)}, f32[12,36,128]{2,1,0:T(8,128)}, u32[]{:S(2)}) copy-start(f32[12,36,128]{2,1,0:T(8,128)} %copy-done.22) | copy-start | bytes 663556
  536.3 7.4 %collective-permute-start.15 = (f32[3,2,2,12,2,128]{5,4,3,1,0,2:T(2,128)S(1)}, f32[3,2,2,12,2,128]{5,4,3,1,0,2:T(2,128)S(1)}, u32[]{:S(2)}, u32[]{:S(2)}) collective-permute-start(f32[3,2,2,12,2,128]{5,4,3,1,0,2:T(2,128)S(1)} %get-tuple-element.42), channel_id=1, source_target_pairs={{1,0},{2,1},{3,2},{4,3},{5,4},{6,5},{7,6},{8,7},{9,8},{10,9},{11,1... | collective-permute-start | bytes 442376 | tf_op jit(solution)/shard_map/ppermute | solution.py:28
  537.6 7.0 %collective-permute-start.14 = (f32[3,2,2,12,2,128]{5,4,3,1,0,2:T(2,128)S(1)}, f32[3,2,2,12,2,128]{5,4,3,1,0,2:T(2,128)S(1)}, u32[]{:S(2)}, u32[]{:S(2)}) collective-permute-start(f32[3,2,2,12,2,128]{5,4,3,1,0,2:T(2,128)S(1)} %get-tuple-element.41), channel_id=1, source_target_pairs={{0,1},{1,2},{2,3},{3,4},{4,5},{5,6},{6,7},{7,8},{8,9},{9,10},{10,1... | collective-permute-start | bytes 442376 | tf_op jit(solution)/shard_map/ppermute | solution.py:26
  543.1 2.0 copy-start.4
  543.1 2.0 copy-start.6
  564.1 7.0 %collective-permute-start.16 = (f32[3,2,2,1,32,128]{5,4,3,1,0,2:T(8,128)S(1)}, f32[3,2,2,1,32,128]{5,4,3,1,0,2:T(8,128)S(1)}, u32[]{:S(2)}, u32[]{:S(2)}) collective-permute-start(f32[3,2,2,1,32,128]{5,4,3,1,0,2:T(8,128)S(1)} %get-tuple-element.53), channel_id=1, source_target_pairs={{16,0},{32,16},{48,32},{64,48},{80,64},{96,80},{112,96},{17,1},{33... | collective-permute-start | bytes 589832 | tf_op jit(solution)/shard_map/ppermute | solution.py:28
  567.1 5.2 collective-permute-start.17
  572.4 6.3 collective-permute-start.18
  573.7 6.0 collective-permute-start.19
  582.8 1.5 copy-start.9
  584.3 1.1 copy-start.18
  584.3 1.7 copy-start.12
  584.3 1.9 copy-start.15
  659.1 1.2 copy-start.13
  659.1 1.4 copy-start.16
  659.1 1.6 copy-start.20
  660.8 2.6 copy-start.1
  (3 other events, 3.1 us)
where the time goes:
time: 671 us; the launch traced here: 664 us
  blocking collectives  492 us (73%)
  starting transfers between devices  58.5 us (9%)
  other arithmetic  55.6 us (8%)
  matrix products  24.8 us (4%)
  local copies, waits for them, and re-layouts  20.2 us (3%)
  waiting for transfers between devices  10.9 us (2%)
    all_gather x6, blocking collectives, on_device(): whole = lax.all_gather(rounded[None], ('gx', 'gy'), axis=0, tiled=True)  349 us
    psum x2, blocking collectives, on_device(): dot_re, dot_im, energy = lax.psum((dot_re, dot_im, energy), ('gx', 'gy'))  143 us
    ppermute x10, starting transfers between devices, with_halo(): lax.ppermute(tail, axis, [(i, (i + 1) % count) for i in range(ends)])  37.6 us
    ppermute x10, starting transfers between devices, with_halo(): lax.ppermute(head, axis, [((i + 1) % count, i) for i in range(ends)])  20.9 us
    add x6, other arithmetic, jacobi(): total = source + neighbours(field)  19.2 us
  transfers between devices with their start and end apart: 20, of which 10 were waited for; matrix products, arithmetic and copies ran while one was open for 4% of the time, Pallas kernels for 0%

commit v1 on v0

v1 whole, which is shorter than its diff:
```python
import functools

import jax
import jax.numpy as jnp
from jax import lax
from jax.experimental import pallas as pl
from jax.experimental.pallas import tpu as pltpu
from jax.sharding import PartitionSpec as P

F32 = jnp.float32
BF16 = jnp.bfloat16
TX, TY, NZ = 8, 32, 128
CELLS = TX * TY
TILES = 128
NNZ = 5
FIELDS = 6
VMEM = 60 * 1024 * 1024
BOTH = ("gx", "gy")


def params(**more):
    return pltpu.CompilerParams(vmem_limit_bytes=VMEM, **more)


def iota(shape, dim):
    return lax.broadcasted_iota(jnp.int32, shape, dim)


def split(x):
    hi = x.astype(BF16)
    return hi, (x - hi.astype(F32)).astype(BF16)


def mm(a, b):
    return lax.dot_general(a, b, (((1,), (0,)), ((), ())), preferred_element_type=F32)


def mm_nt(a, b):
    return lax.dot_general(a, b, (((1,), (1,)), ((), ())), preferred_element_type=F32)


def depth_matrix(depth):
    tall = jnp.concatenate([depth] * 8, axis=0)
    none = jnp.zeros_like(tall)
    return jnp.concatenate(
        [jnp.concatenate([tall, none], axis=1), jnp.concatenate([none, tall], axis=1)], axis=0
    )


def restrict_rows(re, im, pe, rows):
    cells = jnp.concatenate([re.reshape(CELLS, NZ), im.reshape(CELLS, NZ)], axis=1)
    hi, lo = split(cells)
    both = mm_nt(hi, rows)
    part = both[:, :128] + both[:, 128:] + mm_nt(lo, rows[:128])
    return jnp.sum(pe * part, axis=0, keepdims=True)


def pack_low(cells):
    sub = iota((4, 8, NZ), 1)
    return jnp.where(sub < 4, cells[0:4, 0:8], pltpu.roll(cells[4:8, 0:8], 4, 1))


def pack_high(cells):
    sub = iota((4, 8, NZ), 1)
    return jnp.where(sub >= 4, cells[0:4, 24:32], pltpu.roll(cells[4:8, 24:32], 4, 1))


def halo_rows(low, high, x):
    sub = iota((8, NZ), 0)
    if x < 4:
        return jnp.where(sub < 4, low[x], high[x])
    return jnp.where(sub < 4, pltpu.roll(low[x - 4], 4, 0), pltpu.roll(high[x - 4], 4, 0))


def wide_plane(cells, low, high, x):
    return jnp.concatenate([cells[x], halo_rows(low, high, x)], axis=0)


def first_kernel(src, masks, absorb, plane, depth, y0b, y0, pe, ylo, yhi, rows):
    f = pl.program_id(0)

    @pl.when(f == 0)
    def _():
        pick = (iota((8, 128), 1) // 8) % 8 == iota((8, 128), 0)
        pick = jnp.where(pick, 1.0, 0.0)
        p = plane[...]
        hi = p.astype(BF16).astype(F32)
        mid = (p - hi).astype(BF16).astype(F32)
        low = p - hi - mid
        parts = jnp.concatenate([hi, mid, low], axis=0).astype(BF16)
        picks = jnp.concatenate([pick] * 3, axis=0).astype(BF16)
        pe[...] = lax.dot_general(parts, picks, (((0,), (0,)), ((), ())), preferred_element_type=F32)
        hi, lo = split(depth_matrix(depth[...]))
        rows[...] = jnp.concatenate([hi, lo], axis=0)
        y0[...] = jnp.zeros_like(y0)
        for v in range(3):
            m = masks[v].astype(F32)
            ylo[12 + v] = pack_low(m)
            yhi[12 + v] = pack_high(m)
        ylo[15] = pack_low(absorb[...])
        yhi[15] = pack_high(absorb[...])
        ylo[16] = jnp.zeros((4, 8, NZ), F32)
        yhi[16] = jnp.zeros((4, 8, NZ), F32)
        ylo[16, 0] = pe[pl.ds(0, TX, stride=TY), :]
        yhi[16, 0] = pe[pl.ds(TY - 1, TX, stride=TY), :]

    y0[pl.ds(f, 1), :] = restrict_rows(src[0], src[1], pe[...], rows[...])
    for c in range(2):
        ylo[2 * f + c] = pack_low(src[c])
        yhi[2 * f + c] = pack_high(src[c])

    @pl.when(f == FIELDS - 1)
    def _():
        y0b[...] = jnp.broadcast_to(y0[...][None], y0b.shape)


def fixed(*shape):
    return pl.BlockSpec(shape, lambda f: (0,) * len(shape))


def fields(*shape):
    return pl.BlockSpec((2,) + shape, lambda f: (f,) + (0,) * len(shape))


def whole():
    return pl.BlockSpec(memory_space=pltpu.VMEM)


def shape(*dims, dtype=F32):
    return jax.ShapeDtypeStruct(dims, dtype)


def first(src, masks, absorb, plane, depth):
    return pl.pallas_call(
        first_kernel,
        grid=(FIELDS,),
        in_specs=[fields(TX, TY, NZ), fixed(3, TX, TY, NZ), fixed(TX, TY, NZ), fixed(8, CELLS), fixed(8, NZ)],
        out_specs=[fixed(TILES, 8, 128), fixed(8, 128), fixed(CELLS, 128), fixed(17, 4, 8, NZ), fixed(17, 4, 8, NZ)],
        out_shape=[shape(TILES, 8, 128), shape(8, 128), shape(CELLS, 128), shape(17, 4, 8, NZ), shape(17, 4, 8, NZ)],
        scratch_shapes=[pltpu.VMEM((256, 256), BF16)],
        compiler_params=params(),
        name="first",
    )(src, masks, absorb, plane, depth)


def slabs_kernel(src, masks, absorb, pe, low, high, left, right):
    for out, start in ((left, 0), (right, TX - 3)):
        for i in range(3):
            x = start + i
            for ch in range(16):
                if ch < 12:
                    mid = src[ch, x]
                elif ch < 15:
                    mid = masks[ch - 12, x].astype(F32)
                else:
                    mid = absorb[x]
                out[ch, i, :TY] = mid
                out[ch, i, TY:] = halo_rows(low[ch], high[ch], x)
        out[16] = jnp.zeros((3, TY + 8, NZ), F32)
    left[16, 0, :TY] = pe[:TY]
    right[16, 0, :TY] = pe[CELLS - TY :]


def slabs(src, masks, absorb, pe, low, high):
    return pl.pallas_call(
        slabs_kernel,
        in_specs=[whole()] * 6,
        out_specs=[whole()] * 2,
        out_shape=[shape(17, 3, TY + 8, NZ)] * 2,
        compiler_params=params(),
        name="slabs",
    )(src, masks, absorb, pe, low, high)


def complex_times(are, aim, re, im):
    return are * re - aim * im, are * im + aim * re


def update_kernel(res, img, alpha, low0, high0, low1, high1, out, low, high, left, right):
    for f in range(FIELDS):
        are = alpha[f : f + 1, :]
        aim = alpha[8 + f : 9 + f, :]
        a, b = 2 * f, 2 * f + 1
        pre, pim = complex_times(are, aim, img[a], img[b])
        out[a] = res[a] - pre
        out[b] = res[b] - pim
        pre, pim = complex_times(are, aim, low1[a], low1[b])
        low[a] = low0[a] - pre
        low[b] = low0[b] - pim
        pre, pim = complex_times(are, aim, high1[a], high1[b])
        high[a] = high0[a] - pre
        high[b] = high0[b] - pim
        for ch in (a, b):
            for slab, start in ((left, 0), (right, TX - 3)):
                for i in range(3):
                    x = start + i
                    slab[ch, i, :TY] = out[ch, x]
                    slab[ch, i, TY:] = halo_rows(low[ch], high[ch], x)


def update(res, img, alpha, low0, high0, low1, high1):
    return pl.pallas_call(
        update_kernel,
        in_specs=[whole()] * 7,
        out_specs=[whole()] * 5,
        out_shape=[
            shape(12, TX, TY, NZ),
            shape(12, 4, 8, NZ),
            shape(12, 4, 8, NZ),
            shape(12, 3, TY + 8, NZ),
            shape(12, 3, TY + 8, NZ),
        ],
        compiler_params=params(),
        name="update",
    )(res, img, alpha, low0, high0, low1, high1)


def local_kernel(src, low, high, left, right, mask, mlow, mhigh, mleft, mright, absorb, alow, ahigh, aleft, aright,
                 local, image, inv, r, z1, z2, z3):
    lane = iota((TY + 8, NZ), 1)

    def plane(cells, lo, hi, lft, rgt, p):
        if p < 0:
            return lft[p + 3]
        if p >= TX:
            return rgt[p - TX]
        return wide_plane(cells, lo, hi, p)

    for p in range(-3, TX + 3):
        i = p + 3
        if 0 <= p < TX:
            m = jnp.concatenate([mask[0, p].astype(F32), halo_rows(mlow[0], mhigh[0], p)], axis=0)
        else:
            m = plane(None, None, None, mleft[0], mright[0], p)
        dim = plane(absorb, alow[0], ahigh[0], aleft[0], aright[0], p)
        dre = 5.5 - m
        inside = dim > 1.0
        scale = 1.0 / jnp.where(inside, dre * dre + dim * dim, 1.0)
        ire = jnp.where(inside, dre * scale, 0.0)
        iim = jnp.where(inside, -dim * scale, 0.0)
        inv[0, i] = ire
        inv[1, i] = iim
        re = plane(src[0], low[0], high[0], left[0], right[0], p)
        im = plane(src[1], low[1], high[1], left[1], right[1], p)
        r[0, i] = re
        r[1, i] = im
        z1[0, i], z1[1, i] = complex_times(ire, iim, re, im)

    def near(z, c, i):
        mid = z[c, i]
        total = z[c, i - 1] + z[c, i + 1]
        total = total + pltpu.roll(mid, 1, 0) + pltpu.roll(mid, TY + 7, 0)
        total = total + jnp.where(lane == 0, 0.0, pltpu.roll(mid, 1, 1))
        return total + jnp.where(lane == NZ - 1, 0.0, pltpu.roll(mid, NZ - 1, 1))

    for i in range(1, TX + 5):
        re = r[0, i] + near(z1, 0, i)
        im = r[1, i] + near(z1, 1, i)
        z2[0, i], z2[1, i] = complex_times(inv[0, i], inv[1, i], re, im)
    for i in range(2, TX + 4):
        re = r[0, i] + near(z2, 0, i)
        im = r[1, i] + near(z2, 1, i)
        zre, zim = complex_times(inv[0, i], inv[1, i], re, im)
        z3[0, i], z3[1, i] = zre, zim
        if 3 <= i < TX + 3:
            local[0, i - 3], local[1, i - 3] = zre[:TY], zim[:TY]
            image[0, i - 3], image[1, i - 3] = re[:TY], im[:TY]
    for i in range(3, TX + 3):
        for c in range(2):
            image[c, i - 3] = image[c, i - 3] - near(z3, c, i)[:TY]


def channel(offset, *dims):
    return pl.BlockSpec((1,) + dims, lambda f: (offset(f),) + (0,) * len(dims))


def local_solve(res, low, high, left, right, masks, absorb, dlow, dhigh, dleft, dright):
    of_mask = lambda f: 12 + f // 2
    of_absorb = lambda f: 15
    y = (4, 8, NZ)
    x = (3, TY + 8, NZ)
    planes = pltpu.VMEM((2, TX + 6, TY + 8, NZ), F32)
    return pl.pallas_call(
        local_kernel,
        grid=(FIELDS,),
        in_specs=[
            fields(TX, TY, NZ), fields(*y), fields(*y), fields(*x), fields(*x),
            channel(lambda f: f // 2, TX, TY, NZ),
            channel(of_mask, *y), channel(of_mask, *y), channel(of_mask, *x), channel(of_mask, *x),
            fixed(TX, TY, NZ),
            channel(of_absorb, *y), channel(of_absorb, *y), channel(of_absorb, *x), channel(of_absorb, *x),
        ],
        out_specs=[fields(TX, TY, NZ)] * 2,
        out_shape=[shape(12, TX, TY, NZ)] * 2,
        scratch_shapes=[planes] * 5,
        compiler_params=params(),
        name="local",
    )(res, low, high, left, right, masks, dlow, dhigh, dleft, dright, absorb, dlow, dhigh, dleft, dright)


def own_tile():
    return lax.axis_index("gx") * 16 + lax.axis_index("gy")


def sweep(index, tile, blocks, chosen):
    total = None
    for j in range(NNZ):
        part = mm_nt(chosen(index[tile * NNZ + j]), blocks[j])
        total = part if total is None else total + part
    return total


def sweep_kernel(index, every, y0, blocks, out):
    y = y0[...] - sweep(index, own_tile(), blocks, lambda t: every[t].astype(BF16))
    if len(out.shape) == 3:
        out[...] = jnp.broadcast_to(y.astype(BF16)[None], out.shape)
    else:
        out[...] = y


def sweep_call(index, every, y0, blocks, last):
    return pl.pallas_call(
        sweep_kernel,
        in_specs=[pl.BlockSpec(memory_space=pltpu.SMEM)] + [whole()] * 3,
        out_specs=whole(),
        out_shape=shape(8, 128) if last else shape(TILES, 8, 128, dtype=BF16),
        compiler_params=params(),
        name="sweep",
    )(index, every, y0, blocks)


def alphas(every):
    total = jnp.sum(every[...], axis=0)
    row = jnp.broadcast_to(total[6:7, :], (8, 128))
    sub, lane = iota((8, 128), 0), iota((8, 128), 1)

    def take(first_lane):
        return jnp.sum(jnp.where(lane == sub + first_lane, row, 0.0), axis=1, keepdims=True)

    energy = jnp.where(sub[:, :1] < FIELDS, take(16), 1.0)
    are = jnp.broadcast_to(take(0) / energy, (8, 128))
    aim = jnp.broadcast_to(take(8) / energy, (8, 128))
    return are, aim


def restart_kernel(index, every, before, y0, blocks, out, y0_out, alpha):
    are, aim = alphas(every)
    alpha[:8] = are
    alpha[8:] = aim
    sub, lane = iota((8, 128), 0), iota((8, 128), 1)
    turned = jnp.where(lane < 64, -aim, aim)

    def coarse(y, part):
        part = jnp.where(sub < FIELDS, part, 0.0)
        return y - (are * part + turned * pltpu.roll(part, 64, 1))

    tile = own_tile()
    own = coarse(y0[...], every[tile])
    y0_out[...] = own
    y = own - sweep(index, tile, blocks, lambda t: coarse(before[t], every[t]).astype(BF16))
    out[...] = jnp.broadcast_to(y.astype(BF16)[None], out.shape)


def restart(index, every, before, y0, blocks):
    return pl.pallas_call(
        restart_kernel,
        in_specs=[pl.BlockSpec(memory_space=pltpu.SMEM)] + [whole()] * 4,
        out_specs=[whole()] * 3,
        out_shape=[shape(TILES, 8, 128, dtype=BF16), shape(8, 128), shape(16, 128)],
        compiler_params=params(),
        name="restart",
    )(index, every, before, y0, blocks)


def image_kernel(last, y3, yw, ye, yl, yr, pe, elow, ehigh, eleft, eright, depth, masks, absorb, res, local, part,
                 *refs):
    if last:
        direction, image, pay, mats, rows, edge, acc = refs
    else:
        direction, image, pay, ylo, yhi, mats, rows, edge, acc = refs
    f = pl.program_id(0)
    sub8 = iota((8, NZ), 0)

    @pl.when(f == 0)
    def _():
        d = depth[...]
        lane = iota((8, NZ), 1)
        beside = jnp.where(lane == 0, 0.0, pltpu.roll(d, 1, 1))
        beside = beside + jnp.where(lane == NZ - 1, 0.0, pltpu.roll(d, NZ - 1, 1))
        hi, lo = split(depth_matrix(d))
        nhi, nlo = split(depth_matrix(beside))
        mats[0] = jnp.concatenate([hi, hi], axis=0)
        mats[1] = jnp.concatenate([nhi, nhi], axis=0)
        mats[2] = jnp.concatenate([lo, nlo], axis=0)
        rows[...] = jnp.concatenate([hi, lo], axis=0)
        acc[...] = jnp.zeros_like(acc)
        for x in range(TX):
            low = jnp.broadcast_to(ehigh[0, 0, x : x + 1, :], (8, 128))
            high = jnp.broadcast_to(elow[0, 0, x : x + 1, :], (8, 128))
            edge[0, x] = jnp.where(sub8 == 0, low, 0.0)
            edge[1, x] = jnp.where(sub8 == 7, high, 0.0)

    row = pl.ds(f, 1)
    one = pe[...] * y3[row, :]
    three = one.reshape(TX, TY, 128)
    west = (eleft[0, 0, :TY] * yw[row, :])[None]
    east = (eright[0, 0, :TY] * ye[row, :])[None]
    sub = iota((TX, TY, 128), 1)
    near = jnp.concatenate([west, three[:-1]], axis=0) + jnp.concatenate([three[1:], east], axis=0)
    near = near + jnp.where(sub == 0, 0.0, pltpu.roll(three, 1, 1))
    near = near + jnp.where(sub == TY - 1, 0.0, pltpu.roll(three, TY - 1, 1))
    first_rows = near[:, :8] + edge[0] * yl[row, :]
    last_rows = near[:, TY - 8 :] + edge[1] * yr[row, :]
    near = jnp.concatenate([first_rows, near[:, 8 : TY - 8], last_rows], axis=1).reshape(CELLS, 128)
    ohi, olo = split(one)
    nhi, nlo = split(near)
    o = jnp.concatenate([ohi, olo], axis=1)
    n = jnp.concatenate([nhi, nlo], axis=1)
    fine = mm(o, mats[0]) + mm(ohi, mats[2, :128])
    beside = mm(n, mats[0]) + mm(o, mats[1]) + mm(jnp.concatenate([nhi, ohi], axis=1), mats[2])
    cre, cim = fine[:, :NZ].reshape(TX, TY, NZ), fine[:, NZ:].reshape(TX, TY, NZ)
    bre, bim = beside[:, :NZ].reshape(TX, TY, NZ), beside[:, NZ:].reshape(TX, TY, NZ)
    direction[0] = local[0] + cre
    direction[1] = local[1] + cim
    dre = 5.5 - masks[0].astype(F32)
    dim = absorb[...]
    ire = part[0] + (dre * cre - dim * cim - bre)
    iim = part[1] + (dre * cim + dim * cre - bim)
    image[0] = ire
    image[1] = iim
    rre, rim = res[0], res[1]

    def total(v):
        return jnp.sum(jnp.sum(v, axis=(0, 1)).reshape(1, NZ), axis=1, keepdims=True)

    lane1 = iota((1, 128), 1)
    dots = jnp.where(lane1 == f, total(ire * rre + iim * rim), 0.0)
    dots = dots + jnp.where(lane1 == f + 8, total(ire * rim - iim * rre), 0.0)
    dots = dots + jnp.where(lane1 == f + 16, total(ire * ire + iim * iim), 0.0)
    acc[6:7, :] = acc[6:7, :] + dots
    if not last:
        acc[row, :] = restrict_rows(ire, iim, pe[...], rows[...])
        for c, value in ((0, ire), (1, iim)):
            ylo[c] = pack_low(value)
            yhi[c] = pack_high(value)

    @pl.when(f == FIELDS - 1)
    def _():
        pay[...] = jnp.broadcast_to(acc[...][None], pay.shape)


def image_call(last, y3, sides, pe, dlow, dhigh, dleft, dright, depth, masks, absorb, res, local, part):
    edge_y = channel(lambda f: 16, 4, 8, NZ)
    edge_x = channel(lambda f: 16, 3, TY + 8, NZ)
    cells = fields(TX, TY, NZ)
    out_specs = [cells, cells, fixed(TILES, 8, 128)]
    out_shape = [shape(12, TX, TY, NZ)] * 2 + [shape(TILES, 8, 128)]
    if not last:
        out_specs += [fields(4, 8, NZ)] * 2
        out_shape += [shape(12, 4, 8, NZ)] * 2
    return pl.pallas_call(
        functools.partial(image_kernel, last),
        grid=(FIELDS,),
        in_specs=[fixed(8, 128)] * 5
        + [fixed(CELLS, 128), edge_y, edge_y, edge_x, edge_x, fixed(8, NZ)]
        + [channel(lambda f: f // 2, TX, TY, NZ), fixed(TX, TY, NZ), cells, cells, cells],
        out_specs=out_specs,
        out_shape=out_shape,
        scratch_shapes=[
            pltpu.VMEM((3, 256, 256), BF16),
            pltpu.VMEM((256, 256), BF16),
            pltpu.VMEM((2, TX, 8, 128), F32),
            pltpu.VMEM((8, 128), F32),
        ],
        compiler_params=params(),
        name="image",
    )(y3, *sides, pe, dlow, dhigh, dleft, dright, depth, masks, absorb, res, local, part)


def finish_kernel(every, alpha, dir1, dir2, res, img, solution, residual, two):
    f = pl.program_id(0)

    @pl.when(f == 0)
    def _():
        are, aim = alphas(every)
        two[:8] = are
        two[8:] = aim

    are, aim = alpha[pl.ds(f, 1), :], alpha[pl.ds(f + 8, 1), :]
    bre, bim = two[pl.ds(f, 1), :], two[pl.ds(f + 8, 1), :]
    sre, sim = complex_times(are, aim, dir1[0], dir1[1])
    tre, tim = complex_times(bre, bim, dir2[0], dir2[1])
    solution[0] = sre + tre
    solution[1] = sim + tim
    pre, pim = complex_times(bre, bim, img[0], img[1])
    residual[0] = res[0] - pre
    residual[1] = res[1] - pim


def finish(every, alpha, dir1, dir2, res, img):
    cells = fields(TX, TY, NZ)
    return pl.pallas_call(
        finish_kernel,
        grid=(FIELDS,),
        in_specs=[fixed(TILES, 8, 128), fixed(16, 128), cells, cells, cells, cells],
        out_specs=[cells, cells],
        out_shape=[shape(12, TX, TY, NZ)] * 2,
        scratch_shapes=[pltpu.VMEM((16, 128), F32)],
        compiler_params=params(),
        name="finish",
    )(every, alpha, dir1, dir2, res, img)


def down(value, axis):
    count = lax.axis_size(axis)
    return lax.ppermute(value, axis, [(i + 1, i) for i in range(count - 1)])


def up(value, axis):
    count = lax.axis_size(axis)
    return lax.ppermute(value, axis, [(i, i + 1) for i in range(count - 1)])


def gather(copies):
    return lax.all_to_all(copies, BOTH, 0, 0, tiled=True)


def neighbours_of(y3):
    return up(y3, "gx"), down(y3, "gx"), up(y3, "gy"), down(y3, "gy")


def on_device(sources, masks, absorption, plane_basis, depth_basis, coupling_blocks, coupling_index):
    src = sources.reshape(12, TX, TY, NZ)
    blocks = coupling_blocks.reshape(NNZ, 128, 128)
    index = coupling_index.reshape(-1)
    plane = plane_basis.reshape(8, CELLS)

    y0b, y0, pe, ylo, yhi = first(src, masks, absorption, plane, depth_basis)
    low0, high0 = down(ylo, "gy"), up(yhi, "gy")
    all0 = gather(y0b)
    to_left, to_right = slabs(src, masks, absorption, pe, low0, high0)
    left0, right0 = up(to_right, "gx"), down(to_left, "gx")
    all1 = gather(sweep_call(index, all0, y0, blocks, False))
    all2 = gather(sweep_call(index, all1, y0, blocks, False))
    local, part = local_solve(
        src, low0, high0, left0, right0, masks, absorption, low0, high0, left0, right0
    )
    y3 = sweep_call(index, all2, y0, blocks, True)
    dir1, img1, pay, ylo, yhi = image_call(
        False, y3, neighbours_of(y3), pe, low0, high0, left0, right0, depth_basis, masks, absorption, src, local, part
    )

    low1, high1 = down(ylo, "gy"), up(yhi, "gy")
    all3 = gather(pay)
    y1b, y0, alpha = restart(index, all3, all0, y0, blocks)
    res, low, high, to_left, to_right = update(src, img1, alpha, low0, high0, low1, high1)
    left, right = up(to_right, "gx"), down(to_left, "gx")
    all1 = gather(y1b)
    all2 = gather(sweep_call(index, all1, y0, blocks, False))
    local, part = local_solve(res, low, high, left, right, masks, absorption, low0, high0, left0, right0)
    y3 = sweep_call(index, all2, y0, blocks, True)
    dir2, img2, pay = image_call(
        True, y3, neighbours_of(y3), pe, low0, high0, left0, right0, depth_basis, masks, absorption, res, local, part
    )
    all3 = gather(pay)
    solution, residual = finish(all3, alpha, dir1, dir2, res, img2)
    return solution.reshape(sources.shape), residual.reshape(sources.shape)


def solution(mesh):
    return jax.shard_map(
        on_device,
        mesh=mesh,
        in_specs=(
            P(None, None, None, "gx", "gy", None),
            P(None, "gx", "gy", None),
            P("gx", "gy", None),
            P(None, "gx", "gy"),
            P(),
            P("gx", "gy", None, None, None),
            P(),
        ),
        out_specs=(P(None, None, None, "gx", "gy", None), P(None, None, None, "gx", "gy", None)),
        check_vma=False,
    )
```

time: 671 us -> 251 us (0.37)
  blocking collectives: 492 us -> 87.7 us
  Pallas kernels: 0 us -> 61.9 us
  other arithmetic: 55.6 us -> 0 us
  matrix products: 24.8 us -> 0 us
  waiting for transfers between devices: 10.9 us -> 26.2 us
  local copies, waits for them, and re-layouts: 20.2 us -> 8.51 us
    all_gather x6 -> x0, blocking collectives: 349 us -> none  [on_device(): whole = lax.all_gather(rounded[None], ('gx', 'gy'), axis=0, tiled=True)]
    psum x2 -> x0, blocking collectives: 143 us -> none  [on_device(): dot_re, dot_im, energy = lax.psum((dot_re, dot_im, energy), ('gx', 'gy'))]
    all_to_all x0 -> x5, blocking collectives: none -> 87.7 us  [gather(): return lax.all_to_all(copies, BOTH, 0, 0, tiled=True)]
    pallas_call x0 -> x14, Pallas kernels: none -> 61.9 us  [the longest x2 15.5 us: local_solve(): pl.pallas_call(local_kernel, grid=(FIELDS,), in_specs=[fields(TX, TY, NZ)...]
    add x13 -> x0, other arithmetic: 25.4 us -> none  [the longest x6 19.2 us: jacobi(): total = source + neighbours(field)]
    dot_general x14 -> x0, matrix products: 24.8 us -> none  [the longest x2 12.4 us: on_device(): jnp.einsum('vrcxyz,bz->vrcxyb', residual, depth_basis, precision=HIGH)]
    all_to_all x0 -> x2, waiting for transfers between devices: none -> 20.9 us  [gather(): return lax.all_to_all(copies, BOTH, 0, 0, tiled=True)]
    all_to_all x0 -> x2, starting transfers between devices: none -> 17.9 us  [gather(): return lax.all_to_all(copies, BOTH, 0, 0, tiled=True)]
  transfers between devices with their start and end apart: 20 -> 18, of which waited for: 10 -> 4; matrix products, arithmetic and copies ran while one was open for 4% -> 0% of each run, Pallas kernels for 0% -> 11%
where the time goes in v1:
time: 251 us; the launch traced here: 249 us
  blocking collectives  87.7 us (35%)
  starting transfers between devices  63.5 us (25%)
  Pallas kernels  61.9 us (25%)
  waiting for transfers between devices  26.2 us (10%)
  local copies, waits for them, and re-layouts  8.51 us (3%)
    all_to_all x5, blocking collectives, gather(): return lax.all_to_all(copies, BOTH, 0, 0, tiled=True)  87.7 us
    ppermute x8, starting transfers between devices, up(): return lax.ppermute(value, axis, [(i, i + 1) for i in range(count - 1)])  29.6 us
    all_to_all x2, waiting for transfers between devices, gather(): return lax.all_to_all(copies, BOTH, 0, 0, tiled=True)  20.9 us
    all_to_all x2, starting transfers between devices, gather(): return lax.all_to_all(copies, BOTH, 0, 0, tiled=True)  17.9 us
    ppermute x8, starting transfers between devices, down(): return lax.ppermute(value, axis, [(i + 1, i) for i in range(count - 1)])  16 us
    pallas_call x2, Pallas kernels, local_solve(): pl.pallas_call(local_kernel, grid=(FIELDS,), in_specs=[fields(TX, TY, NZ)...  15.5 us
    pallas_call x2, Pallas kernels, image_call(): pl.pallas_call(functools.partial(image_kernel, last), grid=(FIELDS,), in_...  15.4 us
    pallas_call x5, Pallas kernels, sweep_call(): pl.pallas_call(sweep_kernel, in_specs=[pl.BlockSpec(memory_space=pltpu.SM...  9.54 us
  transfers between devices with their start and end apart: 18, of which 4 were waited for; matrix products, arithmetic and copies ran while one was open for 0% of the time, Pallas kernels for 11%

profile of v1, /device:TPU:1, one launch (start us, length us, event | category | flops | bytes accessed | tf_op | source)
XLA Modules:
  0.0 248.9 jit_solution(13700153482444892583)
XLA Ops:
  0.6 1.4 reshape.24.plane
  2.1 5.5 %first.1 = (f32[128,8,128]{2,1,0:T(8,128)}, f32[8,128]{1,0:T(8,128)}, f32[256,128]{1,0:T(8,128)}, f32[17,4,8,128]{3,2,1,0:T(8,128)}, f32[17,4,8,128]{3,2,1,0:T(8,128)}) custom-call(f32[12,8,32,128]{3,2,1,0:T(8,128)} %bitcast.4, s32[3,8,32,128]{3,2,1,0:T(8,128)} %masks.7, f32[8,32,128]{2,1,0:T(8,128)} %absorb.11, f32[8,256]{1,0:T(8,128)} %reshape.24.plane, ...), custom_call_target="tpu_custom_call" | custom-call | tf_op jit(solution)/shard_map/first/pallas_call | solution.py:134
  7.6 1.3 collective-permute-start.4
  8.8 4.7 %collective-permute-start.5 = (f32[17,4,8,128]{3,2,1,0:T(8,128)}, f32[17,4,8,128]{3,2,1,0:T(8,128)S(1)}, u32[]{:S(2)}, u32[]{:S(2)}) collective-permute-start(f32[17,4,8,128]{3,2,1,0:T(8,128)} %get-tuple-element.35), channel_id=1, source_target_pairs={{0,1},{1,2},{2,3},{3,4},{4,5},{5,6},{6,7},{7,8},{8,9},{9,10},{10,1... | collective-permute-start | bytes 835592 | tf_op jit(solution)/shard_map/ppermute | solution.py:521
  13.5 4.2 %collective-permute-done.4.low.mlow.alow.elow.low0 = f32[17,4,8,128]{3,2,1,0:T(8,128)S(1)} collective-permute-done((f32[17,4,8,128]{3,2,1,0:T(8,128)}, f32[17,4,8,128]{3,2,1,0:T(8,128)S(1)}, u32[]{:S(2)}, u32[]{:S(2)}) %collective-permute-start.4) | collective-permute-done | bytes 278560 | tf_op jit(solution)/shard_map/ppermute | solution.py:516
  17.8 1.0 collective-permute-done.5.high.mhigh.ahigh.ehigh.high0
  18.7 0.7 copy-done.3
  19.5 3.2 %slabs.1 = (f32[17,3,40,128]{3,2,1,0:T(8,128)}, f32[17,3,40,128]{3,2,1,0:T(8,128)}) custom-call(f32[12,8,32,128]{3,2,1,0:T(8,128)} %bitcast.5, s32[3,8,32,128]{3,2,1,0:T(8,128)} %masks.7, f32[8,32,128]{2,1,0:T(8,128)} %absorb.11, f32[256,128]{1,0:T(8,128)} %get-tuple-element.33.pe, f32[17,4,8,128]{3,2,1,0:T(8,128)} %copy-done.2, f32[17,4,8,128]{3,2,1,0:T(8,128)} %copy-done.3), custom_call_target="tpu_custom_call" | custom-call | tf_op jit(solution)/shard_map/slabs/pallas_call | solution.py:165
  22.7 5.1 %collective-permute-start.6 = (f32[17,3,40,128]{3,2,1,0:T(8,128)}, f32[17,3,40,128]{3,2,1,0:T(8,128)S(1)}, u32[]{:S(2)}, u32[]{:S(2)}) collective-permute-start(f32[17,3,40,128]{3,2,1,0:T(8,128)} %get-tuple-element.36), channel_id=1, source_target_pairs={{0,16},{16,32},{32,48},{48,64},{64,80},{80,96},{96,112},{1,17},{17... | collective-permute-start | bytes 3133448 | tf_op jit(solution)/shard_map/ppermute | solution.py:521
  27.8 12.5 %all-to-all-start = ((f32[128,8,128]{2,1,0:T(8,128)}), f32[128,8,128]{2,1,0:T(8,128)S(1)}, u32[]{:S(2)}, u32[]{:S(2)}) async-start(f32[128,8,128]{2,1,0:T(8,128)} %get-tuple-element.31), calls=%async_computation | async-start | bytes 1048576 | tf_op jit(solution)/shard_map/all_to_all | solution.py:525
  40.3 3.0 %collective-permute-start.7 = (f32[17,3,40,128]{3,2,1,0:T(8,128)}, f32[17,3,40,128]{3,2,1,0:T(8,128)S(1)}, u32[]{:S(2)}, u32[]{:S(2)}) collective-permute-start(f32[17,3,40,128]{3,2,1,0:T(8,128)} %get-tuple-element.37), channel_id=1, source_target_pairs={{16,0},{32,16},{48,32},{64,48},{80,64},{96,80},{112,96},{17,1},{33... | collective-permute-start | bytes 3133448 | tf_op jit(solution)/shard_map/ppermute | solution.py:516
  43.4 0.8 reshape.22.index
  44.2 12.2 %all-to-all-done.every.before = f32[128,8,128]{2,1,0:T(8,128)S(1)} async-done(((f32[128,8,128]{2,1,0:T(8,128)}), f32[128,8,128]{2,1,0:T(8,128)S(1)}, u32[]{:S(2)}, u32[]{:S(2)}) %all-to-all-start) | async-done | bytes 524320 | tf_op jit(solution)/shard_map/all_to_all | solution.py:525
  56.3 0.8 copy-done.4
  57.2 2.0 sweep.5
  59.2 17.3 %all_to_all.35.every = bf16[128,8,128]{2,1,0:T(8,128)(2,1)} all-to-all(bf16[128,8,128]{2,1,0:T(8,128)(2,1)} %sweep.5), channel_id=1, replica_groups=mesh['gx'=8,'gy'=16] {'gx','gy'}, dimensions={0} | all-to-all | bytes 524288 | tf_op jit(solution)/shard_map/all_to_all | solution.py:525
  76.5 1.9 sweep.6
  78.4 16.4 %all_to_all.36.every = bf16[128,8,128]{2,1,0:T(8,128)(2,1)} all-to-all(bf16[128,8,128]{2,1,0:T(8,128)(2,1)} %sweep.6), channel_id=1, replica_groups=mesh['gx'=8,'gy'=16] {'gx','gy'}, dimensions={0} | all-to-all | bytes 524288 | tf_op jit(solution)/shard_map/all_to_all | solution.py:525
  94.8 1.8 sweep.7.y3
  96.6 1.3 collective-permute-start.3
  97.9 4.0 %collective-permute-start.2 = (f32[8,128]{1,0:T(8,128)}, f32[8,128]{1,0:T(8,128)S(1)}, u32[]{:S(2)}, u32[]{:S(2)}) collective-permute-start(f32[8,128]{1,0:T(8,128)} %sweep.7.y3), channel_id=1, source_target_pairs={{0,1},{1,2},{2,3},{3,4},{4,5},{5,6},{6,7},{7,8},{8,9},{9,10},{10,1... | collective-permute-start | bytes 12296 | tf_op jit(solution)/shard_map/ppermute | solution.py:521
  101.9 3.0 %collective-permute-start.1 = (f32[8,128]{1,0:T(8,128)}, f32[8,128]{1,0:T(8,128)S(1)}, u32[]{:S(2)}, u32[]{:S(2)}) collective-permute-start(f32[8,128]{1,0:T(8,128)} %sweep.7.y3), channel_id=1, source_target_pairs={{16,0},{32,16},{48,32},{64,48},{80,64},{96,80},{112,96},{17,1},{33... | collective-permute-start | bytes 12296 | tf_op jit(solution)/shard_map/ppermute | solution.py:516
  104.9 2.6 %collective-permute-start = (f32[8,128]{1,0:T(8,128)}, f32[8,128]{1,0:T(8,128)S(1)}, u32[]{:S(2)}, u32[]{:S(2)}) collective-permute-start(f32[8,128]{1,0:T(8,128)} %sweep.7.y3), channel_id=1, source_target_pairs={{0,16},{16,32},{32,48},{48,64},{64,80},{80,96},{96,112},{1,17},{17... | collective-permute-start | bytes 12296 | tf_op jit(solution)/shard_map/ppermute | solution.py:521
  107.5 1.0 copy-done.1
  108.6 7.7 %local.2 = (f32[12,8,32,128]{3,2,1,0:T(8,128)}, f32[12,8,32,128]{3,2,1,0:T(8,128)}) custom-call(f32[12,8,32,128]{3,2,1,0:T(8,128)} %bitcast.6, f32[17,4,8,128]{3,2,1,0:T(8,128)} %copy-done.2, f32[17,4,8,128]{3,2,1,0:T(8,128)} %copy-done.3, f32[17,3,40,128]{3,2,1,0:T(8,128)} %copy-done, f32[17,3,40,128]{3,2,1,0:T(8,128)} %copy-done.1, ...), custom_call_target="tpu_custom_call" | custom-call | tf_op jit(solution)/shard_map/local/pallas_call | solution.py:283
  117.0 8.0 %image.2 = (f32[12,8,32,128]{3,2,1,0:T(8,128)}, f32[12,8,32,128]{3,2,1,0:T(8,128)}, f32[128,8,128]{2,1,0:T(8,128)}, f32[12,4,8,128]{3,2,1,0:T(8,128)}, f32[12,4,8,128]{3,2,1,0:T(8,128)}) custom-call(f32[8,128]{1,0:T(8,128)} %sweep.7.y3, f32[8,128]{1,0:T(8,128)} %copy-done.19, f32[8,128]{1,0:T(8,128)} %copy-done.18, f32[8,128]{1,0:T(8,128)} %copy-done.16, ...), custom_call_target="tpu_custom_call" | custom-call | tf_op jit(solution)/shard_map/image/pallas_call | solution.py:461
  124.9 5.4 %all-to-all-start.3 = ((f32[128,8,128]{2,1,0:T(8,128)}), f32[128,8,128]{2,1,0:T(8,128)S(1)}, u32[]{:S(2)}, u32[]{:S(2)}) async-start(f32[128,8,128]{2,1,0:T(8,128)} %get-tuple-element.40), calls=%async_computation.3 | async-start | bytes 1048576 | tf_op jit(solution)/shard_map/all_to_all | solution.py:525
  130.4 1.3 collective-permute-start.12
  131.7 4.0 %collective-permute-start.13 = (f32[12,4,8,128]{3,2,1,0:T(8,128)}, f32[12,4,8,128]{3,2,1,0:T(8,128)S(1)}, u32[]{:S(2)}, u32[]{:S(2)}) collective-permute-start(f32[12,4,8,128]{3,2,1,0:T(8,128)} %get-tuple-element.46), channel_id=1, source_target_pairs={{0,1},{1,2},{2,3},{3,4},{4,5},{5,6},{6,7},{7,8},{8,9},{9,10},{10,1... | collective-permute-start | bytes 589832 | tf_op jit(solution)/shard_map/ppermute | solution.py:521
  135.7 8.8 %all-to-all-done.3.every = f32[128,8,128]{2,1,0:T(8,128)S(1)} async-done(((f32[128,8,128]{2,1,0:T(8,128)}), f32[128,8,128]{2,1,0:T(8,128)S(1)}, u32[]{:S(2)}, u32[]{:S(2)}) %all-to-all-start.3) | async-done | bytes 524320 | tf_op jit(solution)/shard_map/all_to_all | solution.py:525
  144.4 0.8 copy-done.5
  145.2 2.4 restart.1
  148.4 4.1 %update.1 = (f32[12,8,32,128]{3,2,1,0:T(8,128)}, f32[12,4,8,128]{3,2,1,0:T(8,128)}, f32[12,4,8,128]{3,2,1,0:T(8,128)}, f32[12,3,40,128]{3,2,1,0:T(8,128)}, f32[12,3,40,128]{3,2,1,0:T(8,128)}) custom-call(f32[12,8,32,128]{3,2,1,0:T(8,128)} %bitcast.8, f32[12,8,32,128]{3,2,1,0:T(8,128)} %get-tuple-element.43.img, f32[16,128]{1,0:T(8,128)} %get-tuple-element.44.alpha, ...), custom_call_target="tpu_custom_call" | custom-call | tf_op jit(solution)/shard_map/update/pallas_call | solution.py:202
  152.5 2.7 %collective-permute-start.14 = (f32[12,3,40,128]{3,2,1,0:T(8,128)}, f32[12,3,40,128]{3,2,1,0:T(8,128)S(1)}, u32[]{:S(2)}, u32[]{:S(2)}) collective-permute-start(f32[12,3,40,128]{3,2,1,0:T(8,128)} %get-tuple-element.50), channel_id=1, source_target_pairs={{0,16},{16,32},{32,48},{48,64},{64,80},{80,96},{96,112},{1,17},{17... | collective-permute-start | bytes 2211848 | tf_op jit(solution)/shard_map/ppermute | solution.py:521
  155.2 1.9 collective-permute-start.15
  157.2 17.8 %all_to_all.37.every = bf16[128,8,128]{2,1,0:T(8,128)(2,1)} all-to-all(bf16[128,8,128]{2,1,0:T(8,128)(2,1)S(1)} %copy-done.8), channel_id=1, replica_groups=mesh['gx'=8,'gy'=16] {'gx','gy'}, dimensions={0} | all-to-all | bytes 524288 | tf_op jit(solution)/shard_map/all_to_all | solution.py:525
  175.0 2.0 sweep.8
  176.9 16.6 %all_to_all.38.every = bf16[128,8,128]{2,1,0:T(8,128)(2,1)} all-to-all(bf16[128,8,128]{2,1,0:T(8,128)(2,1)} %sweep.8), channel_id=1, replica_groups=mesh['gx'=8,'gy'=16] {'gx','gy'}, dimensions={0} | all-to-all | bytes 524288 | tf_op jit(solution)/shard_map/all_to_all | solution.py:525
  193.5 1.8 sweep.9.y3
  195.3 1.3 collective-permute-start.11
  196.6 4.0 %collective-permute-start.10 = (f32[8,128]{1,0:T(8,128)}, f32[8,128]{1,0:T(8,128)S(1)}, u32[]{:S(2)}, u32[]{:S(2)}) collective-permute-start(f32[8,128]{1,0:T(8,128)} %sweep.9.y3), channel_id=1, source_target_pairs={{0,1},{1,2},{2,3},{3,4},{4,5},{5,6},{6,7},{7,8},{8,9},{9,10},{10,1... | collective-permute-start | bytes 12296 | tf_op jit(solution)/shard_map/ppermute | solution.py:521
  200.6 3.0 %collective-permute-start.9 = (f32[8,128]{1,0:T(8,128)}, f32[8,128]{1,0:T(8,128)S(1)}, u32[]{:S(2)}, u32[]{:S(2)}) collective-permute-start(f32[8,128]{1,0:T(8,128)} %sweep.9.y3), channel_id=1, source_target_pairs={{16,0},{32,16},{48,32},{64,48},{80,64},{96,80},{112,96},{17,1},{33... | collective-permute-start | bytes 12296 | tf_op jit(solution)/shard_map/ppermute | solution.py:516
  203.6 2.6 %collective-permute-start.8 = (f32[8,128]{1,0:T(8,128)}, f32[8,128]{1,0:T(8,128)S(1)}, u32[]{:S(2)}, u32[]{:S(2)}) collective-permute-start(f32[8,128]{1,0:T(8,128)} %sweep.9.y3), channel_id=1, source_target_pairs={{0,16},{16,32},{32,48},{48,64},{64,80},{80,96},{96,112},{1,17},{17... | collective-permute-start | bytes 12296 | tf_op jit(solution)/shard_map/ppermute | solution.py:521
  206.2 0.8 copy-done.7
  207.1 7.8 %local.3 = (f32[12,8,32,128]{3,2,1,0:T(8,128)}, f32[12,8,32,128]{3,2,1,0:T(8,128)}) custom-call(f32[12,8,32,128]{3,2,1,0:T(8,128)} %get-tuple-element.47.src.res, f32[12,4,8,128]{3,2,1,0:T(8,128)} %get-tuple-element.48.low, f32[12,4,8,128]{3,2,1,0:T(8,128)} %get-tuple-element.49.high, f32[12,3,40,128]{3,2,1,0:T(8,128)} %copy-done.6, ...), custom_call_target="tpu_custom_call" | custom-call | tf_op jit(solution)/shard_map/local/pallas_call | solution.py:283
  215.5 7.4 %image.3 = (f32[12,8,32,128]{3,2,1,0:T(8,128)}, f32[12,8,32,128]{3,2,1,0:T(8,128)}, f32[128,8,128]{2,1,0:T(8,128)}) custom-call(f32[8,128]{1,0:T(8,128)} %sweep.9.y3, f32[8,128]{1,0:T(8,128)} %copy-done.17, f32[8,128]{1,0:T(8,128)} %copy-done.14, f32[8,128]{1,0:T(8,128)} %copy-done.13, f32[8,128]{1,0:T(8,128)} %copy-done.12, ...), custom_call_target="tpu_custom_call" | custom-call | tf_op jit(solution)/shard_map/image/pallas_call | solution.py:461
  222.9 19.6 %all_to_all.39.every = f32[128,8,128]{2,1,0:T(8,128)} all-to-all(f32[128,8,128]{2,1,0:T(8,128)} %get-tuple-element.54), channel_id=1, replica_groups=mesh['gx'=8,'gy'=16] {'gx','gy'}, dimensions={0} | all-to-all | bytes 1048576 | tf_op jit(solution)/shard_map/all_to_all | solution.py:525
  242.6 6.3 %finish.1 = (f32[12,8,32,128]{3,2,1,0:T(8,128)}, f32[12,8,32,128]{3,2,1,0:T(8,128)}) custom-call(f32[128,8,128]{2,1,0:T(8,128)} %all_to_all.39.every, f32[16,128]{1,0:T(8,128)} %get-tuple-element.44.alpha, f32[12,8,32,128]{3,2,1,0:T(8,128)} %get-tuple-element.55.dir1, f32[12,8,32,128]{3,2,1,0:T(8,128)} %get-tuple-element.56.dir2, ...), custom_call_target="tpu_custom_call" | custom-call | tf_op jit(solution)/shard_map/finish/pallas_call | solution.py:502
  (50 shorter events, 2.1 us)
Async XLA Ops:
  7.6 10.2 %collective-permute-start.4 = (f32[17,4,8,128]{3,2,1,0:T(8,128)}, f32[17,4,8,128]{3,2,1,0:T(8,128)S(1)}, u32[]{:S(2)}, u32[]{:S(2)}) collective-permute-start(f32[17,4,8,128]{3,2,1,0:T(8,128)} %get-tuple-element.34), channel_id=1, source_target_pairs={{1,0},{2,1},{3,2},{4,3},{5,4},{6,5},{7,6},{8,7},{9,8},{10,9},{11,1... | collective-permute-start | bytes 835592 | tf_op jit(solution)/shard_map/ppermute | solution.py:516
  8.8 9.9 %collective-permute-start.5 = (f32[17,4,8,128]{3,2,1,0:T(8,128)}, f32[17,4,8,128]{3,2,1,0:T(8,128)S(1)}, u32[]{:S(2)}, u32[]{:S(2)}) collective-permute-start(f32[17,4,8,128]{3,2,1,0:T(8,128)} %get-tuple-element.35), channel_id=1, source_target_pairs={{0,1},{1,2},{2,3},{3,4},{4,5},{5,6},{6,7},{7,8},{8,9},{9,10},{10,1... | collective-permute-start | bytes 835592 | tf_op jit(solution)/shard_map/ppermute | solution.py:521
  17.8 1.0 copy-start.2
  18.7 0.7 copy-start.3
  19.5 23.8 %copy-start.11 = (s32[8,16,5]{1,0,2:T(8,128)S(1)}, s32[8,16,5]{1,0,2:T(8,128)}, u32[]{:S(2)}) copy-start(s32[8,16,5]{1,0,2:T(8,128)} %param.13) | copy-start | bytes 7684
  22.7 82.2 %collective-permute-start.6 = (f32[17,3,40,128]{3,2,1,0:T(8,128)}, f32[17,3,40,128]{3,2,1,0:T(8,128)S(1)}, u32[]{:S(2)}, u32[]{:S(2)}) collective-permute-start(f32[17,3,40,128]{3,2,1,0:T(8,128)} %get-tuple-element.36), channel_id=1, source_target_pairs={{0,16},{16,32},{32,48},{48,64},{64,80},{80,96},{96,112},{1,17},{17... | collective-permute-start | bytes 3133448 | tf_op jit(solution)/shard_map/ppermute | solution.py:521
  27.8 28.6 %all-to-all-start = ((f32[128,8,128]{2,1,0:T(8,128)}), f32[128,8,128]{2,1,0:T(8,128)S(1)}, u32[]{:S(2)}, u32[]{:S(2)}) async-start(f32[128,8,128]{2,1,0:T(8,128)} %get-tuple-element.31), calls=%async_computation | async-start | bytes 1048576 | tf_op jit(solution)/shard_map/all_to_all | solution.py:525
  40.3 67.3 %collective-permute-start.7 = (f32[17,3,40,128]{3,2,1,0:T(8,128)}, f32[17,3,40,128]{3,2,1,0:T(8,128)S(1)}, u32[]{:S(2)}, u32[]{:S(2)}) collective-permute-start(f32[17,3,40,128]{3,2,1,0:T(8,128)} %get-tuple-element.37), channel_id=1, source_target_pairs={{16,0},{32,16},{48,32},{64,48},{80,64},{96,80},{112,96},{17,1},{33... | collective-permute-start | bytes 3133448 | tf_op jit(solution)/shard_map/ppermute | solution.py:516
  56.3 0.8 copy-start.4
  96.6 19.7 %collective-permute-start.3 = (f32[8,128]{1,0:T(8,128)}, f32[8,128]{1,0:T(8,128)S(1)}, u32[]{:S(2)}, u32[]{:S(2)}) collective-permute-start(f32[8,128]{1,0:T(8,128)} %sweep.7.y3), channel_id=1, source_target_pairs={{1,0},{2,1},{3,2},{4,3},{5,4},{6,5},{7,6},{8,7},{9,8},{10,9},{11,1... | collective-permute-start | bytes 12296 | tf_op jit(solution)/shard_map/ppermute | solution.py:516
  97.9 18.4 %collective-permute-start.2 = (f32[8,128]{1,0:T(8,128)}, f32[8,128]{1,0:T(8,128)S(1)}, u32[]{:S(2)}, u32[]{:S(2)}) collective-permute-start(f32[8,128]{1,0:T(8,128)} %sweep.7.y3), channel_id=1, source_target_pairs={{0,1},{1,2},{2,3},{3,4},{4,5},{5,6},{6,7},{7,8},{8,9},{9,10},{10,1... | collective-permute-start | bytes 12296 | tf_op jit(solution)/shard_map/ppermute | solution.py:521
  101.9 14.4 %collective-permute-start.1 = (f32[8,128]{1,0:T(8,128)}, f32[8,128]{1,0:T(8,128)S(1)}, u32[]{:S(2)}, u32[]{:S(2)}) collective-permute-start(f32[8,128]{1,0:T(8,128)} %sweep.7.y3), channel_id=1, source_target_pairs={{16,0},{32,16},{48,32},{64,48},{80,64},{96,80},{112,96},{17,1},{33... | collective-permute-start | bytes 12296 | tf_op jit(solution)/shard_map/ppermute | solution.py:516
  104.9 2.6 %copy-start = (f32[17,3,40,128]{3,2,1,0:T(8,128)}, f32[17,3,40,128]{3,2,1,0:T(8,128)S(1)}, u32[]{:S(2)}) copy-start(f32[17,3,40,128]{3,2,1,0:T(8,128)S(1)} %collective-permute-done.6.left.mleft.aleft.eleft) | copy-start | bytes 3133444
  104.9 11.5 %collective-permute-start = (f32[8,128]{1,0:T(8,128)}, f32[8,128]{1,0:T(8,128)S(1)}, u32[]{:S(2)}, u32[]{:S(2)}) collective-permute-start(f32[8,128]{1,0:T(8,128)} %sweep.7.y3), channel_id=1, source_target_pairs={{0,16},{16,32},{32,48},{48,64},{64,80},{80,96},{96,112},{1,17},{17... | collective-permute-start | bytes 12296 | tf_op jit(solution)/shard_map/ppermute | solution.py:521
  107.5 1.0 copy-start.1
  116.3 0.6 copy-start.15
  116.3 0.6 copy-start.16
  116.4 0.6 copy-start.18
  116.4 0.6 copy-start.19
  124.9 19.5 %all-to-all-start.3 = ((f32[128,8,128]{2,1,0:T(8,128)}), f32[128,8,128]{2,1,0:T(8,128)S(1)}, u32[]{:S(2)}, u32[]{:S(2)}) async-start(f32[128,8,128]{2,1,0:T(8,128)} %get-tuple-element.40), calls=%async_computation.3 | async-start | bytes 1048576 | tf_op jit(solution)/shard_map/all_to_all | solution.py:525
  130.4 17.3 %collective-permute-start.12 = (f32[12,4,8,128]{3,2,1,0:T(8,128)}, f32[12,4,8,128]{3,2,1,0:T(8,128)S(1)}, u32[]{:S(2)}, u32[]{:S(2)}) collective-permute-start(f32[12,4,8,128]{3,2,1,0:T(8,128)} %get-tuple-element.45), channel_id=1, source_target_pairs={{1,0},{2,1},{3,2},{4,3},{5,4},{6,5},{7,6},{8,7},{9,8},{10,9},{11,1... | collective-permute-start | bytes 589832 | tf_op jit(solution)/shard_map/ppermute | solution.py:516
  131.7 16.0 %collective-permute-start.13 = (f32[12,4,8,128]{3,2,1,0:T(8,128)}, f32[12,4,8,128]{3,2,1,0:T(8,128)S(1)}, u32[]{:S(2)}, u32[]{:S(2)}) collective-permute-start(f32[12,4,8,128]{3,2,1,0:T(8,128)} %get-tuple-element.46), channel_id=1, source_target_pairs={{0,1},{1,2},{2,3},{3,4},{4,5},{5,6},{6,7},{7,8},{8,9},{9,10},{10,1... | collective-permute-start | bytes 589832 | tf_op jit(solution)/shard_map/ppermute | solution.py:521
  144.4 0.8 copy-start.5
  147.6 0.7 copy-start.9
  147.7 0.8 copy-start.10
  148.4 8.7 %copy-start.8 = (bf16[128,8,128]{2,1,0:T(8,128)(2,1)S(1)}, bf16[128,8,128]{2,1,0:T(8,128)(2,1)}, u32[]{:S(2)}) copy-start(bf16[128,8,128]{2,1,0:T(8,128)(2,1)} %get-tuple-element.41) | copy-start | bytes 786436
  152.5 51.1 %collective-permute-start.14 = (f32[12,3,40,128]{3,2,1,0:T(8,128)}, f32[12,3,40,128]{3,2,1,0:T(8,128)S(1)}, u32[]{:S(2)}, u32[]{:S(2)}) collective-permute-start(f32[12,3,40,128]{3,2,1,0:T(8,128)} %get-tuple-element.50), channel_id=1, source_target_pairs={{0,16},{16,32},{32,48},{48,64},{64,80},{80,96},{96,112},{1,17},{17... | collective-permute-start | bytes 2211848 | tf_op jit(solution)/shard_map/ppermute | solution.py:521
  155.2 51.0 %collective-permute-start.15 = (f32[12,3,40,128]{3,2,1,0:T(8,128)}, f32[12,3,40,128]{3,2,1,0:T(8,128)S(1)}, u32[]{:S(2)}, u32[]{:S(2)}) collective-permute-start(f32[12,3,40,128]{3,2,1,0:T(8,128)} %get-tuple-element.51), channel_id=1, source_target_pairs={{16,0},{32,16},{48,32},{64,48},{80,64},{96,80},{112,96},{17,1},{33... | collective-permute-start | bytes 2211848 | tf_op jit(solution)/shard_map/ppermute | solution.py:516
  195.3 19.6 %collective-permute-start.11 = (f32[8,128]{1,0:T(8,128)}, f32[8,128]{1,0:T(8,128)S(1)}, u32[]{:S(2)}, u32[]{:S(2)}) collective-permute-start(f32[8,128]{1,0:T(8,128)} %sweep.9.y3), channel_id=1, source_target_pairs={{1,0},{2,1},{3,2},{4,3},{5,4},{6,5},{7,6},{8,7},{9,8},{10,9},{11,1... | collective-permute-start | bytes 12296 | tf_op jit(solution)/shard_map/ppermute | solution.py:516
  196.6 18.3 %collective-permute-start.10 = (f32[8,128]{1,0:T(8,128)}, f32[8,128]{1,0:T(8,128)S(1)}, u32[]{:S(2)}, u32[]{:S(2)}) collective-permute-start(f32[8,128]{1,0:T(8,128)} %sweep.9.y3), channel_id=1, source_target_pairs={{0,1},{1,2},{2,3},{3,4},{4,5},{5,6},{6,7},{7,8},{8,9},{9,10},{10,1... | collective-permute-start | bytes 12296 | tf_op jit(solution)/shard_map/ppermute | solution.py:521
  200.6 14.3 %collective-permute-start.9 = (f32[8,128]{1,0:T(8,128)}, f32[8,128]{1,0:T(8,128)S(1)}, u32[]{:S(2)}, u32[]{:S(2)}) collective-permute-start(f32[8,128]{1,0:T(8,128)} %sweep.9.y3), channel_id=1, source_target_pairs={{16,0},{32,16},{48,32},{64,48},{80,64},{96,80},{112,96},{17,1},{33... | collective-permute-start | bytes 12296 | tf_op jit(solution)/shard_map/ppermute | solution.py:516
  203.6 2.6 %copy-start.6 = (f32[12,3,40,128]{3,2,1,0:T(8,128)}, f32[12,3,40,128]{3,2,1,0:T(8,128)S(1)}, u32[]{:S(2)}) copy-start(f32[12,3,40,128]{3,2,1,0:T(8,128)S(1)} %collective-permute-done.14.left) | copy-start | bytes 2211844
  203.6 11.4 %collective-permute-start.8 = (f32[8,128]{1,0:T(8,128)}, f32[8,128]{1,0:T(8,128)S(1)}, u32[]{:S(2)}, u32[]{:S(2)}) collective-permute-start(f32[8,128]{1,0:T(8,128)} %sweep.9.y3), channel_id=1, source_target_pairs={{0,16},{16,32},{32,48},{48,64},{64,80},{80,96},{96,112},{1,17},{17... | collective-permute-start | bytes 12296 | tf_op jit(solution)/shard_map/ppermute | solution.py:521
  206.2 0.9 copy-start.7
  214.9 0.6 copy-start.12
  214.9 0.6 copy-start.13
  214.9 0.6 copy-start.14
  215.0 0.6 copy-start.17

commit v2 on v1

v2 whole, which is shorter than its diff:
```python
import functools

import jax
import jax.numpy as jnp
from jax import lax
from jax.experimental import pallas as pl
from jax.experimental.pallas import tpu as pltpu
from jax.sharding import PartitionSpec as P

F32 = jnp.float32
BF16 = jnp.bfloat16
TX, TY, NZ = 8, 32, 128
CELLS = TX * TY
GX, GY = 8, 16
TILES = GX * GY
NNZ = 5
FIELDS = 6
VMEM = 12 * 1024 * 1024
BOTH = ("gx", "gy")


def params(**more):
    return pltpu.CompilerParams(vmem_limit_bytes=VMEM, **more)


def iota(shape, dim):
    return lax.broadcasted_iota(jnp.int32, shape, dim)


def split(x):
    hi = x.astype(BF16)
    return hi, (x - hi.astype(F32)).astype(BF16)


def mm(a, b):
    return lax.dot_general(a, b, (((1,), (0,)), ((), ())), preferred_element_type=F32)


def mm_nt(a, b):
    return lax.dot_general(a, b, (((1,), (1,)), ((), ())), preferred_element_type=F32)


def depth_matrix(depth):
    tall = jnp.concatenate([depth] * 8, axis=0)
    none = jnp.zeros_like(tall)
    return jnp.concatenate(
        [jnp.concatenate([tall, none], axis=1), jnp.concatenate([none, tall], axis=1)], axis=0
    )


def restrict_rows(re, im, pe, rows):
    cells = jnp.concatenate([re.reshape(CELLS, NZ), im.reshape(CELLS, NZ)], axis=1)
    hi, lo = split(cells)
    both = mm_nt(hi, rows)
    part = both[:, :128] + both[:, 128:] + mm_nt(lo, rows[:128])
    return jnp.sum(pe * part, axis=0, keepdims=True)


def pack_low(cells):
    sub = iota((4, 8, NZ), 1)
    return jnp.where(sub < 4, cells[0:4, 0:8], pltpu.roll(cells[4:8, 0:8], 4, 1))


def pack_high(cells):
    sub = iota((4, 8, NZ), 1)
    return jnp.where(sub >= 4, cells[0:4, 24:32], pltpu.roll(cells[4:8, 24:32], 4, 1))


def halo_rows(low, high, x):
    sub = iota((8, NZ), 0)
    if x < 4:
        return jnp.where(sub < 4, low[x], high[x])
    return jnp.where(sub < 4, pltpu.roll(low[x - 4], 4, 0), pltpu.roll(high[x - 4], 4, 0))


def wide_plane(cells, low, high, x):
    return jnp.concatenate([cells[x], halo_rows(low, high, x)], axis=0)


def first_kernel(
    src_far, masks_far, absorb_far, plane_far, depth_far, y0b_far, pe, ylo_far, yhi_far,
    src, masks, absorb, plane, depth, y0b, ylo, yhi, rows, y0, sems,
):
    copies = []
    for f in range(FIELDS):
        two = pl.ds(2 * f, 2)
        copies.append(pltpu.make_async_copy(src_far.at[two], src.at[two], sems.at[f]))
    copies.append(pltpu.make_async_copy(masks_far, masks, sems.at[FIELDS]))
    copies.append(pltpu.make_async_copy(absorb_far, absorb, sems.at[FIELDS + 1]))
    copies.append(pltpu.make_async_copy(plane_far, plane, sems.at[FIELDS + 2]))
    copies.append(pltpu.make_async_copy(depth_far, depth, sems.at[FIELDS + 3]))
    for copy in copies[::-1]:
        copy.start()
    copies[FIELDS + 2].wait()
    copies[FIELDS + 3].wait()

    pick = (iota((8, 128), 1) // 8) % 8 == iota((8, 128), 0)
    pick = jnp.where(pick, 1.0, 0.0)
    picks = jnp.concatenate([pick] * 3, axis=0).astype(BF16)
    for x in range(TX):
        p = plane[:, x, :]
        hi = p.astype(BF16).astype(F32)
        mid = (p - hi).astype(BF16).astype(F32)
        low = p - hi - mid
        parts = jnp.concatenate([hi, mid, low], axis=0).astype(BF16)
        pe[x * TY : (x + 1) * TY, :] = lax.dot_general(
            parts, picks, (((0,), (0,)), ((), ())), preferred_element_type=F32
        )
    hi, lo = split(depth_matrix(depth[...]))
    rows[...] = jnp.concatenate([hi, lo], axis=0)
    y0[...] = jnp.zeros_like(y0)
    ylo[16] = jnp.zeros((4, 8, NZ), F32)
    yhi[16] = jnp.zeros((4, 8, NZ), F32)
    ylo[16, 0] = pe[pl.ds(0, TX, stride=TY), :]
    yhi[16, 0] = pe[pl.ds(TY - 1, TX, stride=TY), :]

    for f in range(FIELDS):
        copies[f].wait()
        y0[f : f + 1, :] = restrict_rows(src[2 * f], src[2 * f + 1], pe[...], rows[...])
        for ch in (2 * f, 2 * f + 1):
            ylo[ch] = pack_low(src[ch])
            yhi[ch] = pack_high(src[ch])
    y0b[...] = jnp.broadcast_to(y0[...][None], y0b.shape)
    results = [pltpu.make_async_copy(y0b, y0b_far, sems.at[FIELDS + 4])]
    results[0].start()
    copies[FIELDS].wait()
    copies[FIELDS + 1].wait()
    for v in range(3):
        m = masks[v].astype(F32)
        ylo[12 + v] = pack_low(m)
        yhi[12 + v] = pack_high(m)
    ylo[15] = pack_low(absorb[...])
    yhi[15] = pack_high(absorb[...])
    results.append(pltpu.make_async_copy(ylo, ylo_far, sems.at[FIELDS + 5]))
    results.append(pltpu.make_async_copy(yhi, yhi_far, sems.at[FIELDS + 6]))
    results[1].start()
    results[2].start()
    for copy in results:
        copy.wait()


def fixed(*shape):
    return pl.BlockSpec(shape, lambda f: (0,) * len(shape))


def fields(*shape):
    return pl.BlockSpec((2,) + shape, lambda f: (f,) + (0,) * len(shape))


def whole():
    return pl.BlockSpec(memory_space=pltpu.VMEM)


def shape(*dims, dtype=F32):
    return jax.ShapeDtypeStruct(dims, dtype)


def far_shape(*dims, dtype=F32):
    return pltpu.HBM(dims, dtype)


def far(value):
    return pltpu.with_memory_space_constraint(value, pltpu.HBM)


def anywhere():
    return pl.BlockSpec(memory_space=pl.ANY)


def first(src, masks, absorb, plane, depth):
    return pl.pallas_call(
        first_kernel,
        in_specs=[anywhere()] * 5,
        out_specs=[anywhere(), whole(), anywhere(), anywhere()],
        out_shape=[far_shape(TILES, 8, 128), shape(CELLS, 128), far_shape(17, 4, 8, NZ), far_shape(17, 4, 8, NZ)],
        scratch_shapes=[
            pltpu.VMEM((12, TX, TY, NZ), F32),
            pltpu.VMEM((3, TX, TY, NZ), jnp.int32),
            pltpu.VMEM((TX, TY, NZ), F32),
            pltpu.VMEM((8, TX, TY), F32),
            pltpu.VMEM((8, NZ), F32),
            pltpu.VMEM((TILES, 8, 128), F32),
            pltpu.VMEM((17, 4, 8, NZ), F32),
            pltpu.VMEM((17, 4, 8, NZ), F32),
            pltpu.VMEM((256, 256), BF16),
            pltpu.VMEM((8, 128), F32),
            pltpu.SemaphoreType.DMA((FIELDS + 7,)),
        ],
        compiler_params=params(),
        name="first",
    )(far(src), far(masks), far(absorb), far(plane), far(depth))


SLAB = 2 * (TY + 8)


def slab_plane(re, im, re_halo, im_halo):
    return jnp.concatenate([re, im, re_halo, im_halo], axis=0).astype(BF16)


def slab_part(slab, i, c):
    start = c * TY if isinstance(c, int) else pl.multiple_of(c * TY, TY)
    own = slab[i, pl.ds(start, TY), :].astype(F32)
    halo = slab[i, 2 * TY :, :].astype(F32)
    return jnp.concatenate([own, jnp.where(c == 1, halo[8:], halo[:8])], axis=0)


def slabs_kernel(src, masks, absorb, pe, low, high, left, right):
    def halo(ch, x):
        return halo_rows(low[ch], high[ch], x)

    for out, start in ((left, 0), (right, TX - 3)):
        for i in range(3):
            x = start + i
            for f in range(FIELDS):
                a, b = 2 * f, 2 * f + 1
                out[f, i] = slab_plane(src[a, x], src[b, x], halo(a, x), halo(b, x))
            out[6, i] = slab_plane(masks[0, x].astype(F32), masks[1, x].astype(F32), halo(12, x), halo(13, x))
            out[7, i] = slab_plane(masks[2, x].astype(F32), absorb[x], halo(14, x), halo(15, x))
        none = jnp.zeros((8, 128), F32)
        edge = pe[:TY] if start == 0 else pe[CELLS - TY :]
        hi = edge.astype(BF16).astype(F32)
        out[8, 0] = slab_plane(hi, edge - hi, none, none)
        out[8, 1] = jnp.zeros((SLAB, 128), BF16)
        out[8, 2] = jnp.zeros((SLAB, 128), BF16)


def slabs(src, masks, absorb, pe, low, high):
    return pl.pallas_call(
        slabs_kernel,
        in_specs=[whole()] * 6,
        out_specs=[whole()] * 2,
        out_shape=[shape(9, 3, SLAB, NZ, dtype=BF16)] * 2,
        compiler_params=params(),
        name="slabs",
    )(src, masks, absorb, pe, low, high)


def complex_times(are, aim, re, im):
    return are * re - aim * im, are * im + aim * re


def update_kernel(res, img, alpha, low0, high0, low1, high1, out, low, high, left, right):
    for f in range(FIELDS):
        are = alpha[f : f + 1, :]
        aim = alpha[8 + f : 9 + f, :]
        a, b = 2 * f, 2 * f + 1
        pre, pim = complex_times(are, aim, img[a], img[b])
        out[a] = res[a] - pre
        out[b] = res[b] - pim
        pre, pim = complex_times(are, aim, low1[a], low1[b])
        low[a] = low0[a] - pre
        low[b] = low0[b] - pim
        pre, pim = complex_times(are, aim, high1[a], high1[b])
        high[a] = high0[a] - pre
        high[b] = high0[b] - pim
        for slab, start in ((left, 0), (right, TX - 3)):
            for i in range(3):
                x = start + i
                halos = [halo_rows(low[ch], high[ch], x) for ch in (a, b)]
                slab[f, i] = slab_plane(out[a, x], out[b, x], *halos)


def update(res, img, alpha, low0, high0, low1, high1):
    return pl.pallas_call(
        update_kernel,
        in_specs=[whole()] * 7,
        out_specs=[whole()] * 5,
        out_shape=[
            shape(12, TX, TY, NZ),
            shape(12, 4, 8, NZ),
            shape(12, 4, 8, NZ),
            shape(FIELDS, 3, SLAB, NZ, dtype=BF16),
            shape(FIELDS, 3, SLAB, NZ, dtype=BF16),
        ],
        compiler_params=params(),
        name="update",
    )(res, img, alpha, low0, high0, low1, high1)


def local_kernel(src, low, high, left, right, mask, mlow, mhigh, mleft, mright, absorb, alow, ahigh, aleft, aright,
                 local, image, inv, r, z1, z2, z3):
    lane = iota((TY + 8, NZ), 1)

    def plane(cells, lo, hi, lft, rgt, c, p):
        if p < 0:
            return slab_part(lft, p + 3, c)
        if p >= TX:
            return slab_part(rgt, p - TX, c)
        return wide_plane(cells, lo, hi, p)

    which = (pl.program_id(0) // 2) % 2
    for p in range(-3, TX + 3):
        i = p + 3
        if 0 <= p < TX:
            m = jnp.concatenate([mask[0, p].astype(F32), halo_rows(mlow[0], mhigh[0], p)], axis=0)
        else:
            m = plane(None, None, None, mleft.at[0], mright.at[0], which, p)
        dim = plane(absorb, alow[0], ahigh[0], aleft.at[0], aright.at[0], 1, p)
        dre = 5.5 - m
        inside = dim > 1.0
        scale = 1.0 / jnp.where(inside, dre * dre + dim * dim, 1.0)
        ire = jnp.where(inside, dre * scale, 0.0)
        iim = jnp.where(inside, -dim * scale, 0.0)
        inv[0, i] = ire
        inv[1, i] = iim
        re = plane(src[0], low[0], high[0], left.at[0], right.at[0], 0, p)
        im = plane(src[1], low[1], high[1], left.at[0], right.at[0], 1, p)
        r[0, i] = re
        r[1, i] = im
        z1[0, i], z1[1, i] = complex_times(ire, iim, re, im)

    def near(z, c, i):
        mid = z[c, i]
        total = z[c, i - 1] + z[c, i + 1]
        total = total + pltpu.roll(mid, 1, 0) + pltpu.roll(mid, TY + 7, 0)
        total = total + jnp.where(lane == 0, 0.0, pltpu.roll(mid, 1, 1))
        return total + jnp.where(lane == NZ - 1, 0.0, pltpu.roll(mid, NZ - 1, 1))

    for i in range(1, TX + 5):
        re = r[0, i] + near(z1, 0, i)
        im = r[1, i] + near(z1, 1, i)
        z2[0, i], z2[1, i] = complex_times(inv[0, i], inv[1, i], re, im)
    for i in range(2, TX + 4):
        re = r[0, i] + near(z2, 0, i)
        im = r[1, i] + near(z2, 1, i)
        zre, zim = complex_times(inv[0, i], inv[1, i], re, im)
        z3[0, i], z3[1, i] = zre, zim
        if 3 <= i < TX + 3:
            local[0, i - 3], local[1, i - 3] = zre[:TY], zim[:TY]
            image[0, i - 3], image[1, i - 3] = re[:TY], im[:TY]
    for i in range(3, TX + 3):
        for c in range(2):
            image[c, i - 3] = image[c, i - 3] - near(z3, c, i)[:TY]


def channel(offset, *dims):
    return pl.BlockSpec((1,) + dims, lambda f: (offset(f),) + (0,) * len(dims))


def local_solve(res, low, high, left, right, masks, absorb, dlow, dhigh, dleft, dright):
    of_mask = lambda f: 12 + f // 2
    of_absorb = lambda f: 15
    y = (4, 8, NZ)
    x = (3, SLAB, NZ)
    pair = channel(lambda f: f, *x)
    mask_pair, absorb_pair = channel(lambda f: 6 + f // 4, *x), channel(lambda f: 7, *x)
    planes = pltpu.VMEM((2, TX + 6, TY + 8, NZ), F32)
    return pl.pallas_call(
        local_kernel,
        grid=(FIELDS,),
        in_specs=[
            fields(TX, TY, NZ), fields(*y), fields(*y), pair, pair,
            channel(lambda f: f // 2, TX, TY, NZ),
            channel(of_mask, *y), channel(of_mask, *y), mask_pair, mask_pair,
            fixed(TX, TY, NZ),
            channel(of_absorb, *y), channel(of_absorb, *y), absorb_pair, absorb_pair,
        ],
        out_specs=[fields(TX, TY, NZ)] * 2,
        out_shape=[shape(12, TX, TY, NZ)] * 2,
        scratch_shapes=[planes] * 5,
        compiler_params=params(),
        name="local",
    )(res, low, high, left, right, masks, dlow, dhigh, dleft, dright, absorb, dlow, dhigh, dleft, dright)


def own_place():
    return lax.axis_index("gx"), lax.axis_index("gy")


def sweep(index, p, q, blocks, chosen):
    total = None
    for j in range(NNZ):
        part = mm_nt(chosen(index[(p * GY + q) * NNZ + j]), blocks[j])
        total = part if total is None else total + part
    return total


def smem():
    return pl.BlockSpec(memory_space=pltpu.SMEM)


def tile_sweep_kernel(index, every, blocks, out):
    p, q = own_place()
    y = every[p * GY + q] - sweep(index, p, q, blocks, lambda t: every[t].astype(BF16))
    out[...] = jnp.broadcast_to(y.astype(BF16)[None], out.shape)


def tile_sweep(index, every, blocks):
    return pl.pallas_call(
        tile_sweep_kernel,
        in_specs=[smem()] + [whole()] * 2,
        out_specs=whole(),
        out_shape=shape(TILES, 8, 128, dtype=BF16),
        compiler_params=params(),
        name="tile_sweep",
    )(index, every, blocks)


def column_place(t):
    return (t % GY) * GX + t // GY


def column_sweep(index, y0, chosen, pairs, out):
    p, q = own_place()
    for k in range(GX // 2):
        for c in range(2):
            a = ((p // 2 + GX // 2 - k) % (GX // 2)) * 2 + (p % 2 + c) % 2
            y = y0[a * GY + q] - sweep(index, a, q, pairs[k].at[c], chosen)
            out[:, a] = jnp.broadcast_to(y.astype(BF16)[None], (GY, 8, 128))


def column_sweep_kernel(by_column, index, every, y0, b0, b1, b2, b3, out):
    place = column_place if by_column else lambda t: t
    column_sweep(index, y0, lambda t: every[place(t)], (b0, b1, b2, b3), out)


def column_call(by_column, index, every, y0, pairs):
    return pl.pallas_call(
        functools.partial(column_sweep_kernel, by_column),
        in_specs=[smem()] + [whole()] * 6,
        out_specs=whole(),
        out_shape=shape(GY, GX, 8, 128, dtype=BF16),
        compiler_params=params(),
        name="column_sweep",
    )(index, every, y0, *pairs)


def last_sweep_kernel(index, every, y0, b0, b1, b3, blow, bhigh, out):
    p, q = own_place()
    take = lambda t: every[column_place(t)]
    pw, pe = jnp.maximum(p - 1, 0), jnp.minimum(p + 1, GX - 1)
    ql, qr = jnp.maximum(q - 1, 0), jnp.minimum(q + 1, GY - 1)

    def put(i, a, b, rows):
        out[i] = y0[a * GY + b] - sweep(index, a, b, rows, take)

    put(0, p, q, b0.at[0])
    put(3, p, ql, blow)
    put(4, p, qr, bhigh)

    @pl.when(p % 2 == 0)
    def _():
        put(1, pw, q, b1.at[1])
        put(2, pe, q, b0.at[1])

    @pl.when(p % 2 == 1)
    def _():
        put(1, pw, q, b0.at[1])
        put(2, pe, q, b3.at[1])


def last_sweep(index, every, y0, pairs, blow, bhigh):
    return pl.pallas_call(
        last_sweep_kernel,
        in_specs=[smem()] + [whole()] * 7,
        out_specs=whole(),
        out_shape=shape(5, 8, 128),
        compiler_params=params(),
        name="last_sweep",
    )(index, every, y0, pairs[0], pairs[1], pairs[3], blow, bhigh)


def alphas(total):
    row = jnp.broadcast_to(total, (8, 128))
    sub, lane = iota((8, 128), 0), iota((8, 128), 1)

    def take(first_lane):
        return jnp.sum(jnp.where(lane == sub + first_lane, row, 0.0), axis=1, keepdims=True)

    energy = jnp.where(sub[:, :1] < FIELDS, take(16), 1.0)
    are = jnp.broadcast_to(take(0) / energy, (8, 128))
    aim = jnp.broadcast_to(take(8) / energy, (8, 128))
    return are, aim


def restart_kernel(index, every, before, b0, b1, b2, b3, out, y0, alpha):
    are, aim = alphas(jnp.sum(every[...], axis=0)[6:7])
    alpha[:8] = are
    alpha[8:] = aim
    sub, lane = iota((8, 128), 0), iota((8, 128), 1)
    are = jnp.where(sub < FIELDS, are, 0.0)
    aim = jnp.where(sub < FIELDS, jnp.where(lane < 64, -aim, aim), 0.0)

    def coarse(t, _):
        part = every[t]
        y0[t] = before[t] - (are * part + aim * pltpu.roll(part, 64, 1))

    lax.fori_loop(0, TILES, coarse, None, unroll=8)
    column_sweep(index, y0, lambda t: y0[t].astype(BF16), (b0, b1, b2, b3), out)


def restart(index, every, before, pairs):
    return pl.pallas_call(
        restart_kernel,
        in_specs=[smem()] + [whole()] * 6,
        out_specs=[whole()] * 3,
        out_shape=[shape(GY, GX, 8, 128, dtype=BF16), shape(TILES, 8, 128), shape(16, 128)],
        compiler_params=params(),
        name="restart",
    )(index, every, before, *pairs)


def image_kernel(last, ys, pe, elow, ehigh, eleft, eright, depth, masks, absorb, res, local, part,
                 *refs):
    if last:
        direction, image, pay, mats, rows, edge, sides, acc = refs
    else:
        direction, image, pay, ylo, yhi, mats, rows, edge, sides, acc = refs
    f = pl.program_id(0)
    sub8 = iota((8, NZ), 0)

    @pl.when(f == 0)
    def _():
        d = depth[...]
        lane = iota((8, NZ), 1)
        beside = jnp.where(lane == 0, 0.0, pltpu.roll(d, 1, 1))
        beside = beside + jnp.where(lane == NZ - 1, 0.0, pltpu.roll(d, NZ - 1, 1))
        hi, lo = split(depth_matrix(d))
        nhi, nlo = split(depth_matrix(beside))
        mats[0] = jnp.concatenate([hi, hi], axis=0)
        mats[1] = jnp.concatenate([nhi, nhi], axis=0)
        mats[2] = jnp.concatenate([lo, nlo], axis=0)
        rows[...] = jnp.concatenate([hi, lo], axis=0)
        acc[...] = jnp.zeros_like(acc)
        for i, slab in enumerate((eleft, eright)):
            sides[i] = slab[0, 0, :TY].astype(F32) + slab[0, 0, TY : 2 * TY].astype(F32)
        for x in range(TX):
            low = jnp.broadcast_to(ehigh[0, 0, x : x + 1, :], (8, 128))
            high = jnp.broadcast_to(elow[0, 0, x : x + 1, :], (8, 128))
            edge[0, x] = jnp.where(sub8 == 0, low, 0.0)
            edge[1, x] = jnp.where(sub8 == 7, high, 0.0)

    row = pl.ds(f, 1)
    one = pe[...] * ys[0, row, :]
    three = one.reshape(TX, TY, 128)
    west = (sides[0] * ys[1, row, :])[None]
    east = (sides[1] * ys[2, row, :])[None]
    sub = iota((TX, TY, 128), 1)
    near = jnp.concatenate([west, three[:-1]], axis=0) + jnp.concatenate([three[1:], east], axis=0)
    near = near + jnp.where(sub == 0, 0.0, pltpu.roll(three, 1, 1))
    near = near + jnp.where(sub == TY - 1, 0.0, pltpu.roll(three, TY - 1, 1))
    first_rows = near[:, :8] + edge[0] * ys[3, row, :]
    last_rows = near[:, TY - 8 :] + edge[1] * ys[4, row, :]
    near = jnp.concatenate([first_rows, near[:, 8 : TY - 8], last_rows], axis=1).reshape(CELLS, 128)
    ohi, olo = split(one)
    nhi, nlo = split(near)
    o = jnp.concatenate([ohi, olo], axis=1)
    n = jnp.concatenate([nhi, nlo], axis=1)
    fine = mm(o, mats[0]) + mm(ohi, mats[2, :128])
    beside = mm(n, mats[0]) + mm(o, mats[1]) + mm(jnp.concatenate([nhi, ohi], axis=1), mats[2])
    cre, cim = fine[:, :NZ].reshape(TX, TY, NZ), fine[:, NZ:].reshape(TX, TY, NZ)
    bre, bim = beside[:, :NZ].reshape(TX, TY, NZ), beside[:, NZ:].reshape(TX, TY, NZ)
    direction[0] = local[0] + cre
    direction[1] = local[1] + cim
    dre = 5.5 - masks[0].astype(F32)
    dim = absorb[...]
    ire = part[0] + (dre * cre - dim * cim - bre)
    iim = part[1] + (dre * cim + dim * cre - bim)
    image[0] = ire
    image[1] = iim
    rre, rim = res[0], res[1]

    def total(v):
        return jnp.sum(jnp.sum(v, axis=(0, 1)).reshape(1, NZ), axis=1, keepdims=True)

    lane1 = iota((1, 128), 1)
    dots = jnp.where(lane1 == f, total(ire * rre + iim * rim), 0.0)
    dots = dots + jnp.where(lane1 == f + 8, total(ire * rim - iim * rre), 0.0)
    dots = dots + jnp.where(lane1 == f + 16, total(ire * ire + iim * iim), 0.0)
    acc[6:7, :] = acc[6:7, :] + dots
    if not last:
        acc[row, :] = restrict_rows(ire, iim, pe[...], rows[...])
        for c, value in ((0, ire), (1, iim)):
            ylo[c] = pack_low(value)
            yhi[c] = pack_high(value)

    @pl.when(f == FIELDS - 1)
    def _():
        if last:
            pay[...] = jnp.broadcast_to(acc[6:7, :], pay.shape)
        else:
            pay[...] = jnp.broadcast_to(acc[...][None], pay.shape)


def image_call(last, ys, pe, dlow, dhigh, dleft, dright, depth, masks, absorb, res, local, part):
    edge_y = channel(lambda f: 16, 4, 8, NZ)
    edge_x = channel(lambda f: 8, 3, SLAB, NZ)
    cells = fields(TX, TY, NZ)
    pay = (TILES, 128) if last else (TILES, 8, 128)
    out_specs = [cells, cells, fixed(*pay)]
    out_shape = [(shape if last else far_shape)(12, TX, TY, NZ), shape(12, TX, TY, NZ), shape(*pay)]
    if not last:
        out_specs += [fields(4, 8, NZ)] * 2
        out_shape += [shape(12, 4, 8, NZ)] * 2
    return pl.pallas_call(
        functools.partial(image_kernel, last),
        grid=(FIELDS,),
        in_specs=[fixed(5, 8, 128)]
        + [fixed(CELLS, 128), edge_y, edge_y, edge_x, edge_x, fixed(8, NZ)]
        + [channel(lambda f: f // 2, TX, TY, NZ), fixed(TX, TY, NZ), cells, cells, cells],
        out_specs=out_specs,
        out_shape=out_shape,
        scratch_shapes=[
            pltpu.VMEM((3, 256, 256), BF16),
            pltpu.VMEM((256, 256), BF16),
            pltpu.VMEM((2, TX, 8, 128), F32),
            pltpu.VMEM((2, TY, 128), F32),
            pltpu.VMEM((8, 128), F32),
        ],
        compiler_params=params(),
        name="image",
    )(ys, pe, dlow, dhigh, dleft, dright, depth, masks, absorb, res, local, part)


def finish_kernel(every, alpha, dir1, dir2, res, img, solution, residual, two):
    f = pl.program_id(0)

    @pl.when(f == 0)
    def _():
        are, aim = alphas(jnp.sum(every[...], axis=0, keepdims=True))
        two[:8] = are
        two[8:] = aim

    are, aim = alpha[pl.ds(f, 1), :], alpha[pl.ds(f + 8, 1), :]
    bre, bim = two[pl.ds(f, 1), :], two[pl.ds(f + 8, 1), :]
    sre, sim = complex_times(are, aim, dir1[0], dir1[1])
    tre, tim = complex_times(bre, bim, dir2[0], dir2[1])
    solution[0] = sre + tre
    solution[1] = sim + tim
    pre, pim = complex_times(bre, bim, img[0], img[1])
    residual[0] = res[0] - pre
    residual[1] = res[1] - pim


def finish(every, alpha, dir1, dir2, res, img):
    cells = fields(TX, TY, NZ)
    return pl.pallas_call(
        finish_kernel,
        grid=(FIELDS,),
        in_specs=[fixed(TILES, 128), fixed(16, 128), cells, cells, cells, cells],
        out_specs=[cells, cells],
        out_shape=[shape(12, TX, TY, NZ)] * 2,
        scratch_shapes=[pltpu.VMEM((16, 128), F32)],
        compiler_params=params(),
        name="finish",
    )(every, alpha, dir1, dir2, res, img)


def down(value, axis):
    count = lax.axis_size(axis)
    return lax.ppermute(value, axis, [(i + 1, i) for i in range(count - 1)])


def up(value, axis):
    count = lax.axis_size(axis)
    return lax.ppermute(value, axis, [(i, i + 1) for i in range(count - 1)])


def gather(copies, axes=BOTH):
    return lax.all_to_all(copies, axes, 0, 0, tiled=True)


def swap_cores(value):
    return lax.ppermute(value, "gx", [(i, i ^ 1) for i in range(GX)])


def round_x(value, k):
    return lax.ppermute(value, "gx", [(i, (i + 2 * k) % GX) for i in range(GX)])


def after(value, *others):
    return lax.optimization_barrier((value, *others))[0]


def on_device(sources, masks, absorption, plane_basis, depth_basis, coupling_blocks, coupling_index):
    src = sources.reshape(12, TX, TY, NZ)
    blocks = coupling_blocks.reshape(NNZ, 128, 128)
    index = coupling_index.reshape(-1)

    y0b, pe, ylo, yhi = first(src, masks, absorption, plane_basis, depth_basis)
    all0 = gather(y0b)
    low0, high0 = down(ylo, "gy"), up(yhi, "gy")
    other = swap_cores(blocks)
    own_pair = jnp.stack([blocks, other])
    blow, bhigh = up(blocks, "gy"), down(blocks, "gy")
    y1b = tile_sweep(index, after(all0, other), blocks)
    all1 = gather(y1b)
    to_left, to_right = slabs(src, masks, absorption, after(pe, y1b), low0, high0)
    left0, right0 = up(to_right, "gx"), down(to_left, "gx")
    mine = after(own_pair, y1b)
    pairs = [own_pair] + [round_x(mine, k) for k in (1, 2, 3)]
    y2b = column_call(False, index, after(all1, left0, right0, blow, bhigh), all0, pairs)
    all2 = gather(y2b, "gy").reshape(TILES, 8, 128)
    local, part = local_solve(
        src, low0, high0, after(left0, all2), right0, masks, absorption, low0, high0, left0, right0
    )
    ys = last_sweep(index, after(all2, part), all0, pairs, blow, bhigh)
    dir1, img1, pay, ylo, yhi = image_call(
        False, ys, pe, low0, high0, left0, right0, depth_basis, masks, absorption, src, local, part
    )

    all3 = gather(pay)
    low1, high1 = down(ylo, "gy"), up(yhi, "gy")
    y1b, y0, alpha = restart(index, all3, all0, pairs)
    all1 = gather(y1b, "gy").reshape(TILES, 8, 128)
    res, low, high, to_left, to_right = update(src, img1, alpha, low0, high0, low1, high1)
    left, right = up(to_right, "gx"), down(to_left, "gx")
    y2b = column_call(True, index, after(all1, left, right), y0, pairs)
    all2 = gather(y2b, "gy").reshape(TILES, 8, 128)
    local, part = local_solve(res, low, high, after(left, all2), right, masks, absorption, low0, high0, left0, right0)
    ys = last_sweep(index, after(all2, part), y0, pairs, blow, bhigh)
    dir2, img2, pay = image_call(
        True, ys, pe, low0, high0, left0, right0, depth_basis, masks, absorption, res, local, part
    )
    all3 = gather(pay)
    solution, residual = finish(all3, alpha, dir1, dir2, res, img2)
    return solution.reshape(sources.shape), residual.reshape(sources.shape)


def solution(mesh):
    return jax.shard_map(
        on_device,
        mesh=mesh,
        in_specs=(
            P(None, None, None, "gx", "gy", None),
            P(None, "gx", "gy", None),
            P("gx", "gy", None),
            P(None, "gx", "gy"),
            P(),
            P("gx", "gy", None, None, None),
            P(),
        ),
        out_specs=(P(None, None, None, "gx", "gy", None), P(None, None, None, "gx", "gy", None)),
        check_vma=False,
    )
```

time: 251 us -> 187 us (0.75)
  Pallas kernels: 61.9 us -> 36.1 us
  starting transfers between devices: 63.5 us -> 46.9 us
  waiting for transfers between devices: 26.2 us -> 14.1 us
  blocking collectives: 87.7 us -> 75.7 us
  local copies, waits for them, and re-layouts: 8.51 us -> 11.4 us
    all_to_all x5, blocking collectives: 87.7 us -> 75.7 us  [gather(): return lax.all_to_all(copies, axes, 0, 0, tiled=True)]
    ppermute x8 -> x5, starting transfers between devices: 29.6 us -> 18.1 us  [up(): return lax.ppermute(value, axis, [(i, i + 1) for i in range(count - 1)])]
    ppermute x8 -> x5, starting transfers between devices: 16 us -> 7.72 us  [down(): return lax.ppermute(value, axis, [(i + 1, i) for i in range(count - 1)])]
    all_to_all x2, waiting for transfers between devices: 20.9 us -> 13.1 us  [gather(): return lax.all_to_all(copies, axes, 0, 0, tiled=True)]
    pallas_call x2, Pallas kernels: 15.4 us -> 7.8 us  [image_call(): pl.pallas_call(functools.partial(image_kernel, last), grid=(FIELDS,), in_...]
    pallas_call x8, Pallas kernels: 23.7 us -> 16.7 us  [the longest x1 4.33 us: first(): pl.pallas_call(first_kernel, in_specs=[anywhere()] * 5, out_specs=[anywhe...]
    pallas_call x2, Pallas kernels: 15.5 us -> 9.65 us  [local_solve(): pl.pallas_call(local_kernel, grid=(FIELDS,), in_specs=[fields(TX, TY, NZ)...]
    unnamed x41 -> x69, local copies, waits for them, and re-layouts: 6.29 us -> 10.4 us
  transfers between devices with their start and end apart: 18 -> 16, of which waited for: 4 -> 4; matrix products, arithmetic and copies ran while one was open for 0% -> 1% of each run, Pallas kernels for 11% -> 2%
where the time goes in v2:
time: 187 us; the launch traced here: 186 us
  blocking collectives  75.7 us (40%)
  starting transfers between devices  46.9 us (25%)
  Pallas kernels  36.1 us (19%)
  waiting for transfers between devices  14.1 us (8%)
  local copies, waits for them, and re-layouts  11.4 us (6%)
    all_to_all x5, blocking collectives, gather(): return lax.all_to_all(copies, axes, 0, 0, tiled=True)  75.7 us
    ppermute x5, starting transfers between devices, up(): return lax.ppermute(value, axis, [(i, i + 1) for i in range(count - 1)])  18.1 us
    all_to_all x2, starting transfers between devices, gather(): return lax.all_to_all(copies, axes, 0, 0, tiled=True)  17.4 us
    all_to_all x2, waiting for transfers between devices, gather(): return lax.all_to_all(copies, axes, 0, 0, tiled=True)  13.1 us
    unnamed x69, local copies, waits for them, and re-layouts  10.4 us
    pallas_call x2, Pallas kernels, local_solve(): pl.pallas_call(local_kernel, grid=(FIELDS,), in_specs=[fields(TX, TY, NZ)...  9.65 us
    pallas_call x2, Pallas kernels, image_call(): pl.pallas_call(functools.partial(image_kernel, last), grid=(FIELDS,), in_...  7.8 us
    ppermute x5, starting transfers between devices, down(): return lax.ppermute(value, axis, [(i + 1, i) for i in range(count - 1)])  7.72 us
  transfers between devices with their start and end apart: 16, of which 4 were waited for; matrix products, arithmetic and copies ran while one was open for 1% of the time, Pallas kernels for 2%

profile of v2, /device:TPU:1, one launch (start us, length us, event | category | flops | bytes accessed | tf_op | source)
XLA Modules:
  0.0 186.3 jit_solution(11666438161451312615)
XLA Ops:
  0.7 4.3 %first.1 = (f32[128,8,128]{2,1,0:T(8,128)}, f32[256,128]{1,0:T(8,128)S(1)}, f32[17,4,8,128]{3,2,1,0:T(8,128)}, f32[17,4,8,128]{3,2,1,0:T(8,128)}) custom-call(f32[12,8,32,128]{3,2,1,0:T(8,128)} %bitcast.13, s32[3,8,32,128]{3,2,1,0:T(8,128)} %masks.5, f32[8,32,128]{2,1,0:T(8,128)} %absorb.9, f32[8,8,32]{2,1,0:T(8,128)} %plane_far.1, f32[8,128]{1,0:T(8,128)} %depth.3), custom_call_target="tpu_custom_call" | custom-call | tf_op jit(solution)/shard_map/first/pallas_call | solution.py:171
  5.0 11.5 %all-to-all-start = ((f32[128,8,128]{2,1,0:T(8,128)}), f32[128,8,128]{2,1,0:T(8,128)S(1)}, u32[]{:S(2)}, u32[]{:S(2)}) async-start(f32[128,8,128]{2,1,0:T(8,128)} %get-tuple-element.39), calls=%async_computation | async-start | bytes 1048576 | tf_op jit(solution)/shard_map/all_to_all | solution.py:661
  16.5 1.3 collective-permute-start.1
  17.8 4.0 %collective-permute-start.2 = (f32[17,4,8,128]{3,2,1,0:T(8,128)}, f32[17,4,8,128]{3,2,1,0:T(8,128)S(1)}, u32[]{:S(2)}, u32[]{:S(2)}) collective-permute-start(f32[17,4,8,128]{3,2,1,0:T(8,128)} %get-tuple-element.44), channel_id=1, source_target_pairs={{0,1},{1,2},{2,3},{3,4},{4,5},{5,6},{6,7},{7,8},{8,9},{9,10},{10,1... | collective-permute-start | bytes 835592 | tf_op jit(solution)/shard_map/ppermute | solution.py:657
  21.9 1.7 collective-permute-start
  23.6 0.8 copy.10
  24.3 1.0 reshape.30.index
  25.4 5.2 %all-to-all-done.every.y0.before = f32[128,8,128]{2,1,0:T(8,128)S(1)} async-done(((f32[128,8,128]{2,1,0:T(8,128)}), f32[128,8,128]{2,1,0:T(8,128)S(1)}, u32[]{:S(2)}, u32[]{:S(2)}) %all-to-all-start) | async-done | bytes 524320 | tf_op jit(solution)/shard_map/all_to_all | solution.py:661
  30.6 0.8 tile_sweep.1
  31.7 2.7 %collective-permute-start.3 = (bf16[9,3,80,128]{3,2,1,0:T(8,128)(2,1)S(1)}, bf16[9,3,80,128]{3,2,1,0:T(8,128)(2,1)S(1)}, u32[]{:S(2)}, u32[]{:S(2)}) collective-permute-start(bf16[9,3,80,128]{3,2,1,0:T(8,128)(2,1)S(1)} %get-tuple-element.45), channel_id=1, source_target_pairs={{0,16},{16,32},{32,48},{48,64},{64,80},{80,96},{96,112},{1,17},{17... | collective-permute-start | bytes 1658888 | tf_op jit(solution)/shard_map/ppermute | solution.py:657
  34.4 1.9 %collective-permute-start.4 = (bf16[9,3,80,128]{3,2,1,0:T(8,128)(2,1)S(1)}, bf16[9,3,80,128]{3,2,1,0:T(8,128)(2,1)S(1)}, u32[]{:S(2)}, u32[]{:S(2)}) collective-permute-start(bf16[9,3,80,128]{3,2,1,0:T(8,128)(2,1)S(1)} %get-tuple-element.46), channel_id=1, source_target_pairs={{16,0},{32,16},{48,32},{64,48},{80,64},{96,80},{112,96},{17,1},{33... | collective-permute-start | bytes 1658888 | tf_op jit(solution)/shard_map/ppermute | solution.py:652
  36.3 1.3 collective-permute-start.6
  37.6 4.0 %collective-permute-start.5 = (bf16[5,128,128]{2,1,0:T(8,128)(2,1)S(1)}, bf16[5,128,128]{2,1,0:T(8,128)(2,1)S(1)}, u32[]{:S(2)}, u32[]{:S(2)}) collective-permute-start(bf16[5,128,128]{2,1,0:T(8,128)(2,1)S(1)} %bitcast.24), channel_id=1, source_target_pairs={{0,1},{1,2},{2,3},{3,4},{4,5},{5,6},{6,7},{7,8},{8,9},{9,10},{10,1... | collective-permute-start | bytes 491528 | tf_op jit(solution)/shard_map/ppermute | solution.py:657
  41.6 0.9 pad_maximum_fusion.b0
  42.6 0.8 collective-permute-start.9
  43.7 1.2 collective-permute-start.8
  45.5 26.4 %all_to_all.41.every = bf16[128,8,128]{2,1,0:T(8,128)(2,1)S(1)} all-to-all(bf16[128,8,128]{2,1,0:T(8,128)(2,1)S(1)} %tile_sweep.1), channel_id=1, replica_groups=mesh['gx'=8,'gy'=16] {'gx','gy'}, dimensions={0} | all-to-all | bytes 524288 | tf_op jit(solution)/shard_map/all_to_all | solution.py:661
  72.0 1.3 copy-done.5
  73.3 1.4 column_sweep.2
  74.7 11.7 %all_to_all.42 = bf16[16,8,8,128]{3,2,1,0:T(8,128)(2,1)S(1)} all-to-all(bf16[16,8,8,128]{3,2,1,0:T(8,128)(2,1)S(1)} %column_sweep.2), channel_id=1, replica_groups=mesh['gx'=8,'gy'=16] {'gy'}, dimensions={0} | all-to-all | bytes 524288 | tf_op jit(solution)/shard_map/all_to_all | solution.py:661
  86.4 4.8 %local.2 = (f32[12,8,32,128]{3,2,1,0:T(8,128)S(1)}, f32[12,8,32,128]{3,2,1,0:T(8,128)S(1)}) custom-call(f32[12,8,32,128]{3,2,1,0:T(8,128)S(1)} %bitcast.15, f32[17,4,8,128]{3,2,1,0:T(8,128)S(1)} %collective-permute-done.1.low.mlow.alow.elow.low0, f32[17,4,8,128]{3,2,1,0:T(8,128)S(1)} %collective-permute-done.2.high.mhigh.ahigh.ehigh.high0, ...), custom_call_target="tpu_custom_call" | custom-call | tf_op jit(solution)/shard_map/local/pallas_call | solution.py:349
  91.3 1.2 last_sweep.2.ys
  92.5 4.8 %image.2 = (f32[12,8,32,128]{3,2,1,0:T(8,128)}, f32[12,8,32,128]{3,2,1,0:T(8,128)S(1)}, f32[128,8,128]{2,1,0:T(8,128)S(1)}, f32[12,4,8,128]{3,2,1,0:T(8,128)S(1)}, f32[12,4,8,128]{3,2,1,0:T(8,128)S(1)}) custom-call(f32[5,8,128]{2,1,0:T(8,128)S(1)} %last_sweep.2.ys, f32[256,128]{1,0:T(8,128)S(1)} %get-tuple-element.42.pe, ...), custom_call_target="tpu_custom_call" | custom-call | tf_op jit(solution)/shard_map/image/pallas_call | solution.py:596
  97.3 1.1 copy-done.21
  98.5 0.8 copy-done.29
  99.3 0.7 copy-done.31
  100.0 0.7 copy-done.32
  100.6 5.9 %all-to-all-start.3 = ((f32[128,8,128]{2,1,0:T(8,128)}), f32[128,8,128]{2,1,0:T(8,128)}, u32[]{:S(2)}, u32[]{:S(2)}) async-start(f32[128,8,128]{2,1,0:T(8,128)} %copy-done.29), calls=%async_computation.3 | async-start | bytes 1048576 | tf_op jit(solution)/shard_map/all_to_all | solution.py:661
  106.5 1.3 collective-permute-start.10
  107.8 4.7 %collective-permute-start.11 = (f32[12,4,8,128]{3,2,1,0:T(8,128)}, f32[12,4,8,128]{3,2,1,0:T(8,128)}, u32[]{:S(2)}, u32[]{:S(2)}) collective-permute-start(f32[12,4,8,128]{3,2,1,0:T(8,128)} %copy-done.31), channel_id=1, source_target_pairs={{0,1},{1,2},{2,3},{3,4},{4,5},{5,6},{6,7},{7,8},{8,9},{9,10},{10,1... | collective-permute-start | bytes 589832 | tf_op jit(solution)/shard_map/ppermute | solution.py:657
  112.5 7.9 %all-to-all-done.3.every = f32[128,8,128]{2,1,0:T(8,128)} async-done(((f32[128,8,128]{2,1,0:T(8,128)}), f32[128,8,128]{2,1,0:T(8,128)}, u32[]{:S(2)}, u32[]{:S(2)}) %all-to-all-start.3) | async-done | bytes 524320 | tf_op jit(solution)/shard_map/all_to_all | solution.py:661
  120.4 1.0 copy-done.6
  121.4 1.0 copy-done.8
  122.4 1.0 copy-done.11
  123.4 1.0 copy-done.14
  124.4 1.0 copy-done.18
  125.3 3.4 %restart.1 = (bf16[16,8,8,128]{3,2,1,0:T(8,128)(2,1)S(1)}, f32[128,8,128]{2,1,0:T(8,128)S(1)}, f32[16,128]{1,0:T(8,128)S(1)}) custom-call(s32[640]{0:T(1024)S(1)} %reshape.30.index, f32[128,8,128]{2,1,0:T(8,128)} %all-to-all-done.3.every, f32[128,8,128]{2,1,0:T(8,128)S(1)} %copy-done.6, bf16[2,5,128,128]{3,2,1,0:T(8,128)(2,1)S(1)} %copy-done.8, ...), custom_call_target="tpu_custom_call" | custom-call | tf_op jit(solution)/shard_map/restart/pallas_call | solution.py:494
  128.8 1.7 update.1
  130.6 2.7 %collective-permute-start.12 = (bf16[6,3,80,128]{3,2,1,0:T(8,128)(2,1)S(1)}, bf16[6,3,80,128]{3,2,1,0:T(8,128)(2,1)S(1)}, u32[]{:S(2)}, u32[]{:S(2)}) collective-permute-start(bf16[6,3,80,128]{3,2,1,0:T(8,128)(2,1)S(1)} %get-tuple-element.59), channel_id=1, source_target_pairs={{0,16},{16,32},{32,48},{48,64},{64,80},{80,96},{96,112},{1,17},{17... | collective-permute-start | bytes 1105928 | tf_op jit(solution)/shard_map/ppermute | solution.py:657
  133.3 1.9 %collective-permute-start.13 = (bf16[6,3,80,128]{3,2,1,0:T(8,128)(2,1)S(1)}, bf16[6,3,80,128]{3,2,1,0:T(8,128)(2,1)S(1)}, u32[]{:S(2)}, u32[]{:S(2)}) collective-permute-start(bf16[6,3,80,128]{3,2,1,0:T(8,128)(2,1)S(1)} %get-tuple-element.60), channel_id=1, source_target_pairs={{16,0},{32,16},{48,32},{64,48},{80,64},{96,80},{112,96},{17,1},{33... | collective-permute-start | bytes 1105928 | tf_op jit(solution)/shard_map/ppermute | solution.py:652
  135.3 11.6 %all_to_all.43 = bf16[16,8,8,128]{3,2,1,0:T(8,128)(2,1)S(1)} all-to-all(bf16[16,8,8,128]{3,2,1,0:T(8,128)(2,1)S(1)} %get-tuple-element.54), channel_id=1, replica_groups=mesh['gx'=8,'gy'=16] {'gy'}, dimensions={0} | all-to-all | bytes 524288 | tf_op jit(solution)/shard_map/all_to_all | solution.py:661
  146.9 1.4 column_sweep.3
  148.3 10.6 %all_to_all.44 = bf16[16,8,8,128]{3,2,1,0:T(8,128)(2,1)S(1)} all-to-all(bf16[16,8,8,128]{3,2,1,0:T(8,128)(2,1)S(1)} %column_sweep.3), channel_id=1, replica_groups=mesh['gx'=8,'gy'=16] {'gy'}, dimensions={0} | all-to-all | bytes 524288 | tf_op jit(solution)/shard_map/all_to_all | solution.py:661
  158.8 4.8 %local.3 = (f32[12,8,32,128]{3,2,1,0:T(8,128)S(1)}, f32[12,8,32,128]{3,2,1,0:T(8,128)S(1)}) custom-call(f32[12,8,32,128]{3,2,1,0:T(8,128)S(1)} %get-tuple-element.63.src.res, f32[12,4,8,128]{3,2,1,0:T(8,128)S(1)} %get-tuple-element.64.low, f32[12,4,8,128]{3,2,1,0:T(8,128)S(1)} %get-tuple-element.65.high, ...), custom_call_target="tpu_custom_call" | custom-call | tf_op jit(solution)/shard_map/local/pallas_call | solution.py:349
  163.7 1.2 last_sweep.3.ys
  164.9 3.0 %image.3 = (f32[12,8,32,128]{3,2,1,0:T(8,128)S(1)}, f32[12,8,32,128]{3,2,1,0:T(8,128)S(1)}, f32[128,128]{1,0:T(8,128)S(1)}) custom-call(f32[5,8,128]{2,1,0:T(8,128)S(1)} %last_sweep.3.ys, f32[256,128]{1,0:T(8,128)S(1)} %get-tuple-element.42.pe, f32[17,4,8,128]{3,2,1,0:T(8,128)S(1)} %collective-permute-done.1.low.mlow.alow.elow.low0, ...), custom_call_target="tpu_custom_call" | custom-call | tf_op jit(solution)/shard_map/image/pallas_call | solution.py:596
  167.9 15.5 %all_to_all.45 = f32[128,1,128]{2,1,0:T(1,128)S(1)} all-to-all(f32[128,1,128]{2,1,0:T(1,128)S(1)} %bitcast.27), channel_id=1, replica_groups=mesh['gx'=8,'gy'=16] {'gx','gy'}, dimensions={0} | all-to-all | bytes 131072 | tf_op jit(solution)/shard_map/all_to_all | solution.py:661
  183.4 2.9 %finish.1 = (f32[12,8,32,128]{3,2,1,0:T(8,128)}, f32[12,8,32,128]{3,2,1,0:T(8,128)}) custom-call(f32[128,128]{1,0:T(8,128)S(1)} %bitcast.26, f32[16,128]{1,0:T(8,128)S(1)} %get-tuple-element.56.alpha, f32[12,8,32,128]{3,2,1,0:T(8,128)S(1)} %copy-done.20, f32[12,8,32,128]{3,2,1,0:T(8,128)S(1)} %get-tuple-element.72.dir2, ...), custom_call_target="tpu_custom_call" | custom-call | tf_op jit(solution)/shard_map/finish/pallas_call | solution.py:638
  (74 shorter events, 1.2 us)
Async XLA Ops:
  0.6 21.2 %copy-start.27 = (bf16[1,1,5,128,128]{4,3,2,1,0:T(8,128)(2,1)S(1)}, bf16[1,1,5,128,128]{4,3,2,1,0:T(8,128)(2,1)}, u32[]{:S(2)}) copy-start(bf16[1,1,5,128,128]{4,3,2,1,0:T(8,128)(2,1)} %param.12) | copy-start | bytes 491524
  0.6 22.9 %copy-start.33 = (s32[8,16,5]{1,0,2:T(8,128)S(1)}, s32[8,16,5]{1,0,2:T(8,128)}, u32[]{:S(2)}) copy-start(s32[8,16,5]{1,0,2:T(8,128)} %param.13) | copy-start | bytes 7684
  5.0 26.5 %copy-start = (f32[3,2,2,8,32,128]{5,4,3,2,1,0:T(8,128)S(1)}, f32[3,2,2,8,32,128]{5,4,3,2,1,0:T(8,128)}, u32[]{:S(2)}) copy-start(f32[3,2,2,8,32,128]{5,4,3,2,1,0:T(8,128)} %param.7) | copy-start | bytes 4718596
  5.0 26.5 %copy-start.1 = (s32[3,8,32,128]{3,2,1,0:T(8,128)S(1)}, s32[3,8,32,128]{3,2,1,0:T(8,128)}, u32[]{:S(2)}) copy-start(s32[3,8,32,128]{3,2,1,0:T(8,128)} %masks.5) | copy-start | bytes 1179652
  5.0 26.5 %copy-start.16 = (f32[8,32,128]{2,1,0:T(8,128)S(1)}, f32[8,32,128]{2,1,0:T(8,128)}, u32[]{:S(2)}) copy-start(f32[8,32,128]{2,1,0:T(8,128)} %absorb.9) | copy-start | bytes 393220
  5.0 25.6 %all-to-all-start = ((f32[128,8,128]{2,1,0:T(8,128)}), f32[128,8,128]{2,1,0:T(8,128)S(1)}, u32[]{:S(2)}, u32[]{:S(2)}) async-start(f32[128,8,128]{2,1,0:T(8,128)} %get-tuple-element.39), calls=%async_computation | async-start | bytes 1048576 | tf_op jit(solution)/shard_map/all_to_all | solution.py:661
  16.5 14.9 %collective-permute-start.1 = (f32[17,4,8,128]{3,2,1,0:T(8,128)}, f32[17,4,8,128]{3,2,1,0:T(8,128)S(1)}, u32[]{:S(2)}, u32[]{:S(2)}) collective-permute-start(f32[17,4,8,128]{3,2,1,0:T(8,128)} %get-tuple-element.43), channel_id=1, source_target_pairs={{1,0},{2,1},{3,2},{4,3},{5,4},{6,5},{7,6},{8,7},{9,8},{10,9},{11,1... | collective-permute-start | bytes 835592 | tf_op jit(solution)/shard_map/ppermute | solution.py:652
  17.8 13.6 %collective-permute-start.2 = (f32[17,4,8,128]{3,2,1,0:T(8,128)}, f32[17,4,8,128]{3,2,1,0:T(8,128)S(1)}, u32[]{:S(2)}, u32[]{:S(2)}) collective-permute-start(f32[17,4,8,128]{3,2,1,0:T(8,128)} %get-tuple-element.44), channel_id=1, source_target_pairs={{0,1},{1,2},{2,3},{3,4},{4,5},{5,6},{6,7},{7,8},{8,9},{9,10},{10,1... | collective-permute-start | bytes 835592 | tf_op jit(solution)/shard_map/ppermute | solution.py:657
  21.9 3.5 %collective-permute-start = (bf16[5,128,128]{2,1,0:T(8,128)(2,1)S(1)}, bf16[5,128,128]{2,1,0:T(8,128)(2,1)}, u32[]{:S(2)}, u32[]{:S(2)}) collective-permute-start(bf16[5,128,128]{2,1,0:T(8,128)(2,1)S(1)} %bitcast.21), channel_id=1, source_target_pairs={{0,16},{16,0},{32,48},{48,32},{64,80},{80,64},{96,112},{112,96},{1... | collective-permute-start | bytes 491528 | tf_op jit(solution)/shard_map/ppermute | solution.py:665
  30.6 1.0 copy-start.4
  31.4 4.9 %copy-start.28 = (bf16[1,1,5,128,128]{4,3,2,1,0:T(8,128)(2,1)S(1)}, bf16[1,1,5,128,128]{4,3,2,1,0:T(8,128)(2,1)}, u32[]{:S(2)}) copy-start(bf16[1,1,5,128,128]{4,3,2,1,0:T(8,128)(2,1)} %param.12) | copy-start | bytes 491524
  31.7 40.2 %collective-permute-start.3 = (bf16[9,3,80,128]{3,2,1,0:T(8,128)(2,1)S(1)}, bf16[9,3,80,128]{3,2,1,0:T(8,128)(2,1)S(1)}, u32[]{:S(2)}, u32[]{:S(2)}) collective-permute-start(bf16[9,3,80,128]{3,2,1,0:T(8,128)(2,1)S(1)} %get-tuple-element.45), channel_id=1, source_target_pairs={{0,16},{16,32},{32,48},{48,64},{64,80},{80,96},{96,112},{1,17},{17... | collective-permute-start | bytes 1658888 | tf_op jit(solution)/shard_map/ppermute | solution.py:657
  34.4 37.5 %collective-permute-start.4 = (bf16[9,3,80,128]{3,2,1,0:T(8,128)(2,1)S(1)}, bf16[9,3,80,128]{3,2,1,0:T(8,128)(2,1)S(1)}, u32[]{:S(2)}, u32[]{:S(2)}) collective-permute-start(bf16[9,3,80,128]{3,2,1,0:T(8,128)(2,1)S(1)} %get-tuple-element.46), channel_id=1, source_target_pairs={{16,0},{32,16},{48,32},{64,48},{80,64},{96,80},{112,96},{17,1},{33... | collective-permute-start | bytes 1658888 | tf_op jit(solution)/shard_map/ppermute | solution.py:652
  36.3 7.4 %collective-permute-start.6 = (bf16[5,128,128]{2,1,0:T(8,128)(2,1)S(1)}, bf16[5,128,128]{2,1,0:T(8,128)(2,1)S(1)}, u32[]{:S(2)}, u32[]{:S(2)}) collective-permute-start(bf16[5,128,128]{2,1,0:T(8,128)(2,1)S(1)} %bitcast.23), channel_id=1, source_target_pairs={{1,0},{2,1},{3,2},{4,3},{5,4},{6,5},{7,6},{8,7},{9,8},{10,9},{11,1... | collective-permute-start | bytes 491528 | tf_op jit(solution)/shard_map/ppermute | solution.py:652
  37.6 7.9 %collective-permute-start.5 = (bf16[5,128,128]{2,1,0:T(8,128)(2,1)S(1)}, bf16[5,128,128]{2,1,0:T(8,128)(2,1)S(1)}, u32[]{:S(2)}, u32[]{:S(2)}) collective-permute-start(bf16[5,128,128]{2,1,0:T(8,128)(2,1)S(1)} %bitcast.24), channel_id=1, source_target_pairs={{0,1},{1,2},{2,3},{3,4},{4,5},{5,6},{6,7},{7,8},{8,9},{9,10},{10,1... | collective-permute-start | bytes 491528 | tf_op jit(solution)/shard_map/ppermute | solution.py:657
  42.6 48.7 %copy-start.7 = (bf16[2,5,128,128]{3,2,1,0:T(8,128)(2,1)}, bf16[2,5,128,128]{3,2,1,0:T(8,128)(2,1)S(1)}, u32[]{:S(2)}) copy-start(bf16[2,5,128,128]{3,2,1,0:T(8,128)(2,1)S(1)} %pad_maximum_fusion.b0) | copy-start | bytes 983044
  42.6 29.3 %collective-permute-start.9 = (bf16[2,5,128,128]{3,2,1,0:T(8,128)(2,1)S(1)}, bf16[2,5,128,128]{3,2,1,0:T(8,128)(2,1)S(1)}, u32[]{:S(2)}, u32[]{:S(2)}) collective-permute-start(bf16[2,5,128,128]{3,2,1,0:T(8,128)(2,1)S(1)} %pad_maximum_fusion.b0), channel_id=1, source_target_pairs={{0,96},{16,112},{32,0},{48,16},{64,32},{80,48},{96,64},{112,80},{1... | collective-permute-start | bytes 983048 | tf_op jit(solution)/shard_map/ppermute | solution.py:669
  43.7 47.6 %copy-start.23 = (bf16[5,128,128]{2,1,0:T(8,128)(2,1)}, bf16[5,128,128]{2,1,0:T(8,128)(2,1)S(1)}, u32[]{:S(2)}) copy-start(bf16[5,128,128]{2,1,0:T(8,128)(2,1)S(1)} %collective-permute-done.6.bhigh) | copy-start | bytes 491524
  43.7 28.2 %collective-permute-start.8 = (bf16[2,5,128,128]{3,2,1,0:T(8,128)(2,1)S(1)}, bf16[2,5,128,128]{3,2,1,0:T(8,128)(2,1)S(1)}, u32[]{:S(2)}, u32[]{:S(2)}) collective-permute-start(bf16[2,5,128,128]{3,2,1,0:T(8,128)(2,1)S(1)} %pad_maximum_fusion.b0), channel_id=1, source_target_pairs={{0,64},{16,80},{32,96},{48,112},{64,0},{80,16},{96,32},{112,48},{1... | collective-permute-start | bytes 983048 | tf_op jit(solution)/shard_map/ppermute | solution.py:669
  45.5 45.8 %copy-start.25 = (bf16[5,128,128]{2,1,0:T(8,128)(2,1)}, bf16[5,128,128]{2,1,0:T(8,128)(2,1)S(1)}, u32[]{:S(2)}) copy-start(bf16[5,128,128]{2,1,0:T(8,128)(2,1)S(1)} %collective-permute-done.5.blow) | copy-start | bytes 491524
  45.5 26.4 %collective-permute-start.7 = (bf16[2,5,128,128]{3,2,1,0:T(8,128)(2,1)S(1)}, bf16[2,5,128,128]{3,2,1,0:T(8,128)(2,1)S(1)}, u32[]{:S(2)}, u32[]{:S(2)}) collective-permute-start(bf16[2,5,128,128]{3,2,1,0:T(8,128)(2,1)S(1)} %pad_maximum_fusion.b0), channel_id=1, source_target_pairs={{0,32},{16,48},{32,64},{48,80},{64,96},{80,112},{96,0},{112,16},{1... | collective-permute-start | bytes 983048 | tf_op jit(solution)/shard_map/ppermute | solution.py:669
  71.9 14.5 %copy-start.2 = (s32[3,8,32,128]{3,2,1,0:T(8,128)S(1)}, s32[3,8,32,128]{3,2,1,0:T(8,128)}, u32[]{:S(2)}) copy-start(s32[3,8,32,128]{3,2,1,0:T(8,128)} %masks.5) | copy-start | bytes 1179652
  71.9 19.4 %copy-start.10 = (bf16[2,5,128,128]{3,2,1,0:T(8,128)(2,1)}, bf16[2,5,128,128]{3,2,1,0:T(8,128)(2,1)S(1)}, u32[]{:S(2)}) copy-start(bf16[2,5,128,128]{3,2,1,0:T(8,128)(2,1)S(1)} %collective-permute-done.9.b3) | copy-start | bytes 983044
  71.9 19.3 %copy-start.17 = (bf16[2,5,128,128]{3,2,1,0:T(8,128)(2,1)}, bf16[2,5,128,128]{3,2,1,0:T(8,128)(2,1)S(1)}, u32[]{:S(2)}) copy-start(bf16[2,5,128,128]{3,2,1,0:T(8,128)(2,1)S(1)} %collective-permute-done.8.b2) | copy-start | bytes 983044
  72.0 1.3 copy-start.5
  73.3 18.0 %copy-start.13 = (bf16[2,5,128,128]{3,2,1,0:T(8,128)(2,1)}, bf16[2,5,128,128]{3,2,1,0:T(8,128)(2,1)S(1)}, u32[]{:S(2)}) copy-start(bf16[2,5,128,128]{3,2,1,0:T(8,128)(2,1)S(1)} %collective-permute-done.7.b1) | copy-start | bytes 983044
  91.2 1.3 copy-start.30
  97.3 1.1 copy-start.21
  98.5 0.8 copy-start.29
  100.6 19.8 %all-to-all-start.3 = ((f32[128,8,128]{2,1,0:T(8,128)}), f32[128,8,128]{2,1,0:T(8,128)}, u32[]{:S(2)}, u32[]{:S(2)}) async-start(f32[128,8,128]{2,1,0:T(8,128)} %copy-done.29), calls=%async_computation.3 | async-start | bytes 1048576 | tf_op jit(solution)/shard_map/all_to_all | solution.py:661
  106.5 22.2 %collective-permute-start.10 = (f32[12,4,8,128]{3,2,1,0:T(8,128)}, f32[12,4,8,128]{3,2,1,0:T(8,128)}, u32[]{:S(2)}, u32[]{:S(2)}) collective-permute-start(f32[12,4,8,128]{3,2,1,0:T(8,128)} %copy-done.32), channel_id=1, source_target_pairs={{1,0},{2,1},{3,2},{4,3},{5,4},{6,5},{7,6},{8,7},{9,8},{10,9},{11,1... | collective-permute-start | bytes 589832 | tf_op jit(solution)/shard_map/ppermute | solution.py:652
  107.8 21.0 %collective-permute-start.11 = (f32[12,4,8,128]{3,2,1,0:T(8,128)}, f32[12,4,8,128]{3,2,1,0:T(8,128)}, u32[]{:S(2)}, u32[]{:S(2)}) collective-permute-start(f32[12,4,8,128]{3,2,1,0:T(8,128)} %copy-done.31), channel_id=1, source_target_pairs={{0,1},{1,2},{2,3},{3,4},{4,5},{5,6},{6,7},{7,8},{8,9},{9,10},{10,1... | collective-permute-start | bytes 589832 | tf_op jit(solution)/shard_map/ppermute | solution.py:657
  120.4 1.0 copy-start.6
  121.4 1.0 copy-start.8
  122.4 1.0 copy-start.11
  123.4 1.0 copy-start.14
  124.4 1.0 copy-start.18
  125.3 3.5 %copy-start.22 = (f32[12,8,32,128]{3,2,1,0:T(8,128)S(1)}, f32[12,8,32,128]{3,2,1,0:T(8,128)}, u32[]{:S(2)}) copy-start(f32[12,8,32,128]{3,2,1,0:T(8,128)} %copy-done.21) | copy-start | bytes 4718596
  128.8 18.0 %copy-start.9 = (bf16[2,5,128,128]{3,2,1,0:T(8,128)(2,1)S(1)}, bf16[2,5,128,128]{3,2,1,0:T(8,128)(2,1)}, u32[]{:S(2)}) copy-start(bf16[2,5,128,128]{3,2,1,0:T(8,128)(2,1)} %copy-done.7) | copy-start | bytes 983044
  128.8 18.0 %copy-start.12 = (bf16[2,5,128,128]{3,2,1,0:T(8,128)(2,1)S(1)}, bf16[2,5,128,128]{3,2,1,0:T(8,128)(2,1)}, u32[]{:S(2)}) copy-start(bf16[2,5,128,128]{3,2,1,0:T(8,128)(2,1)} %copy-done.10) | copy-start | bytes 983044
  128.8 18.0 %copy-start.15 = (bf16[2,5,128,128]{3,2,1,0:T(8,128)(2,1)S(1)}, bf16[2,5,128,128]{3,2,1,0:T(8,128)(2,1)}, u32[]{:S(2)}) copy-start(bf16[2,5,128,128]{3,2,1,0:T(8,128)(2,1)} %copy-done.13) | copy-start | bytes 983044
  128.8 18.0 %copy-start.19 = (bf16[2,5,128,128]{3,2,1,0:T(8,128)(2,1)S(1)}, bf16[2,5,128,128]{3,2,1,0:T(8,128)(2,1)}, u32[]{:S(2)}) copy-start(bf16[2,5,128,128]{3,2,1,0:T(8,128)(2,1)} %copy-done.17) | copy-start | bytes 983044
  130.6 16.2 %collective-permute-start.12 = (bf16[6,3,80,128]{3,2,1,0:T(8,128)(2,1)S(1)}, bf16[6,3,80,128]{3,2,1,0:T(8,128)(2,1)S(1)}, u32[]{:S(2)}, u32[]{:S(2)}) collective-permute-start(bf16[6,3,80,128]{3,2,1,0:T(8,128)(2,1)S(1)} %get-tuple-element.59), channel_id=1, source_target_pairs={{0,16},{16,32},{32,48},{48,64},{64,80},{80,96},{96,112},{1,17},{17... | collective-permute-start | bytes 1105928 | tf_op jit(solution)/shard_map/ppermute | solution.py:657
  133.3 13.5 %collective-permute-start.13 = (bf16[6,3,80,128]{3,2,1,0:T(8,128)(2,1)S(1)}, bf16[6,3,80,128]{3,2,1,0:T(8,128)(2,1)S(1)}, u32[]{:S(2)}, u32[]{:S(2)}) collective-permute-start(bf16[6,3,80,128]{3,2,1,0:T(8,128)(2,1)S(1)} %get-tuple-element.60), channel_id=1, source_target_pairs={{16,0},{32,16},{48,32},{64,48},{80,64},{96,80},{112,96},{17,1},{33... | collective-permute-start | bytes 1105928 | tf_op jit(solution)/shard_map/ppermute | solution.py:652
  146.8 12.0 %copy-start.3 = (s32[3,8,32,128]{3,2,1,0:T(8,128)S(1)}, s32[3,8,32,128]{3,2,1,0:T(8,128)}, u32[]{:S(2)}) copy-start(s32[3,8,32,128]{3,2,1,0:T(8,128)} %masks.5) | copy-start | bytes 1179652
  158.8 4.8 %copy-start.24 = (bf16[5,128,128]{2,1,0:T(8,128)(2,1)S(1)}, bf16[5,128,128]{2,1,0:T(8,128)(2,1)}, u32[]{:S(2)}) copy-start(bf16[5,128,128]{2,1,0:T(8,128)(2,1)} %copy-done.23) | copy-start | bytes 491524
  158.8 4.8 %copy-start.26 = (bf16[5,128,128]{2,1,0:T(8,128)(2,1)S(1)}, bf16[5,128,128]{2,1,0:T(8,128)(2,1)}, u32[]{:S(2)}) copy-start(bf16[5,128,128]{2,1,0:T(8,128)(2,1)} %copy-done.25) | copy-start | bytes 491524
  164.9 18.5 %copy-start.20 = (f32[12,8,32,128]{3,2,1,0:T(8,128)S(1)}, f32[12,8,32,128]{3,2,1,0:T(8,128)}, u32[]{:S(2)}) copy-start(f32[12,8,32,128]{3,2,1,0:T(8,128)} %get-tuple-element.71.dir1) | copy-start | bytes 4718596
  (2 other events, 1.3 us)

commit v3 on v2

--- a/solution.py
+++ b/solution.py
@@ -16,6 +16,7 @@
 NNZ = 5
 FIELDS = 6
 VMEM = 12 * 1024 * 1024
+EDGES = (25, 4, 16, NZ)
 BOTH = ("gx", "gy")
 
 
@@ -77,18 +78,26 @@
     return jnp.concatenate([cells[x], halo_rows(low, high, x)], axis=0)
 
 
+def even_row():
+    return lax.axis_index("gy") % 2 == 0
+
+
+def by_pairs(to_last, to_next):
+    even = even_row()
+    return jnp.where(even, to_next, to_last), jnp.where(even, to_last, to_next)
+
+
 def first_kernel(
-    src_far, masks_far, absorb_far, plane_far, depth_far, y0b_far, pe, ylo_far, yhi_far,
-    src, masks, absorb, plane, depth, y0b, ylo, yhi, rows, y0, sems,
+    src_far, masks_far, absorb_far, plane_far, depth_far, blocks_far, y0b_far, pe, in_far, out_far,
+    src, masks, absorb, plane, depth, blocks, y0b, inner, outer, rows, y0, sems,
 ):
     copies = []
     for f in range(FIELDS):
         two = pl.ds(2 * f, 2)
         copies.append(pltpu.make_async_copy(src_far.at[two], src.at[two], sems.at[f]))
-    copies.append(pltpu.make_async_copy(masks_far, masks, sems.at[FIELDS]))
-    copies.append(pltpu.make_async_copy(absorb_far, absorb, sems.at[FIELDS + 1]))
-    copies.append(pltpu.make_async_copy(plane_far, plane, sems.at[FIELDS + 2]))
-    copies.append(pltpu.make_async_copy(depth_far, depth, sems.at[FIELDS + 3]))
+    rest = ((masks_far, masks), (absorb_far, absorb), (plane_far, plane), (depth_far, depth), (blocks_far, blocks))
+    for i, (there, here) in enumerate(rest):
+        copies.append(pltpu.make_async_copy(there, here, sems.at[FIELDS + i]))
     for copy in copies[::-1]:
         copy.start()
     copies[FIELDS + 2].wait()
@@ -109,30 +118,42 @@
     hi, lo = split(depth_matrix(depth[...]))
     rows[...] = jnp.concatenate([hi, lo], axis=0)
     y0[...] = jnp.zeros_like(y0)
-    ylo[16] = jnp.zeros((4, 8, NZ), F32)
-    yhi[16] = jnp.zeros((4, 8, NZ), F32)
-    ylo[16, 0] = pe[pl.ds(0, TX, stride=TY), :]
-    yhi[16, 0] = pe[pl.ds(TY - 1, TX, stride=TY), :]
-
+
+    def edges(re, im):
+        low = jnp.concatenate([pack_low(re), pack_low(im)], axis=1)
+        high = jnp.concatenate([pack_high(re), pack_high(im)], axis=1)
+        return by_pairs(low, high)
+
+    def put(refs, at, values):
+        for ref, value in zip(refs, values):
+            hi, lo = split(value)
+            ref[at[0]] = hi
+            if len(at) > 1:
+                ref[at[1]] = lo
+
+    refs = (inner, outer)
     for f in range(FIELDS):
         copies[f].wait()
-        y0[f : f + 1, :] = restrict_rows(src[2 * f], src[2 * f + 1], pe[...], rows[...])
-        for ch in (2 * f, 2 * f + 1):
-            ylo[ch] = pack_low(src[ch])
-            yhi[ch] = pack_high(src[ch])
+        re, im = src[2 * f], src[2 * f + 1]
+        y0[f : f + 1, :] = restrict_rows(re, im, pe[...], rows[...])
+        put(refs, (f, FIELDS + f), edges(re, im))
     y0b[...] = jnp.broadcast_to(y0[...][None], y0b.shape)
-    results = [pltpu.make_async_copy(y0b, y0b_far, sems.at[FIELDS + 4])]
+    results = [pltpu.make_async_copy(y0b, y0b_far, sems.at[FIELDS + 5])]
     results[0].start()
     copies[FIELDS].wait()
     copies[FIELDS + 1].wait()
-    for v in range(3):
-        m = masks[v].astype(F32)
-        ylo[12 + v] = pack_low(m)
-        yhi[12 + v] = pack_high(m)
-    ylo[15] = pack_low(absorb[...])
-    yhi[15] = pack_high(absorb[...])
-    results.append(pltpu.make_async_copy(ylo, ylo_far, sems.at[FIELDS + 5]))
-    results.append(pltpu.make_async_copy(yhi, yhi_far, sems.at[FIELDS + 6]))
+    put(refs, (12,), edges(masks[0].astype(F32), masks[1].astype(F32)))
+    put(refs, (13,), edges(masks[2].astype(F32), absorb[...]))
+    copies[FIELDS + 4].wait()
+    ends = by_pairs(pe[pl.ds(0, TX, stride=TY), :], pe[pl.ds(TY - 1, TX, stride=TY), :])
+    for ref, end in zip(refs, ends):
+        hi = end.astype(BF16).astype(F32)
+        ref[14] = jnp.zeros((4, 16, NZ), BF16)
+        ref[14, 0] = jnp.concatenate([hi, end - hi], axis=0).astype(BF16)
+        for j in range(NNZ):
+            ref[15 + 2 * j : 17 + 2 * j] = blocks[j].reshape(2, 4, 16, 128)
+    results.append(pltpu.make_async_copy(inner, in_far, sems.at[FIELDS + 6]))
+    results.append(pltpu.make_async_copy(outer, out_far, sems.at[FIELDS + 7]))
     results[1].start()
     results[2].start()
     for copy in results:
@@ -167,28 +188,33 @@
     return pl.BlockSpec(memory_space=pl.ANY)
 
 
-def first(src, masks, absorb, plane, depth):
+def first(src, masks, absorb, plane, depth, blocks):
     return pl.pallas_call(
         first_kernel,
-        in_specs=[anywhere()] * 5,
+        in_specs=[anywhere()] * 6,
         out_specs=[anywhere(), whole(), anywhere(), anywhere()],
-        out_shape=[far_shape(TILES, 8, 128), shape(CELLS, 128), far_shape(17, 4, 8, NZ), far_shape(17, 4, 8, NZ)],
+        out_shape=[far_shape(TILES, 8, 128), shape(CELLS, 128), far_shape(*EDGES, dtype=BF16), far_shape(*EDGES, dtype=BF16)],
         scratch_shapes=[
             pltpu.VMEM((12, TX, TY, NZ), F32),
             pltpu.VMEM((3, TX, TY, NZ), jnp.int32),
             pltpu.VMEM((TX, TY, NZ), F32),
             pltpu.VMEM((8, TX, TY), F32),
             pltpu.VMEM((8, NZ), F32),
+            pltpu.VMEM((NNZ, 128, 128), BF16),
             pltpu.VMEM((TILES, 8, 128), F32),
-            pltpu.VMEM((17, 4, 8, NZ), F32),
-            pltpu.VMEM((17, 4, 8, NZ), F32),
+            pltpu.VMEM(EDGES, BF16),
+            pltpu.VMEM(EDGES, BF16),
             pltpu.VMEM((256, 256), BF16),
             pltpu.VMEM((8, 128), F32),
-            pltpu.SemaphoreType.DMA((FIELDS + 7,)),
+            pltpu.SemaphoreType.DMA((FIELDS + 8,)),
         ],
         compiler_params=params(),
         name="first",
-    )(far(src), far(masks), far(absorb), far(plane), far(depth))
+    )(far(src), far(masks), far(absorb), far(plane), far(depth), far(blocks))
+
+
+def anywhere():
+    return pl.BlockSpec(memory_space=pl.ANY)
 
 
 SLAB = 2 * (TY + 8)
@@ -205,42 +231,78 @@
     return jnp.concatenate([own, jnp.where(c == 1, halo[8:], halo[:8])], axis=0)
 
 
-def slabs_kernel(src, masks, absorb, pe, low, high, left, right):
+def own_core():
+    return lax.axis_index("gx") % 2
+
+
+def fill_sides(fill, core_out, chip_out):
+    @pl.when(own_core() == 0)
+    def _():
+        fill(core_out, TX - 3)
+        fill(chip_out, 0)
+
+    @pl.when(own_core() == 1)
+    def _():
+        fill(core_out, 0)
+        fill(chip_out, TX - 3)
+
+
+def slabs_kernel(src, masks, absorb, pe, inner, outer, b0, b1, b2, b3, core_out, chip_out, low, high):
+    even = even_row()
+    for pair in range(8):
+        sides = []
+        for ref in (inner, outer):
+            value = ref[pair].astype(F32) if pair < FIELDS else ref[FIELDS + pair].astype(F32)
+            sides.append(value + ref[FIELDS + pair].astype(F32) if pair < FIELDS else value)
+        for out, value in ((low, jnp.where(even, sides[0], sides[1])), (high, jnp.where(even, sides[1], sides[0]))):
+            out[2 * pair] = value[:, :8]
+            out[2 * pair + 1] = value[:, 8:]
+    ends = [ref[14, 0].astype(F32) for ref in (inner, outer)]
+    ends = [end[:8] + end[8:] for end in ends]
+    for out, value in ((low, jnp.where(even, *ends)), (high, jnp.where(even, *ends[::-1]))):
+        out[16] = jnp.zeros((4, 8, NZ), F32)
+        out[16, 0] = value
+
     def halo(ch, x):
         return halo_rows(low[ch], high[ch], x)
 
-    for out, start in ((left, 0), (right, TX - 3)):
+    def fill(out, start):
         for i in range(3):
             x = start + i
             for f in range(FIELDS):
                 a, b = 2 * f, 2 * f + 1
-                out[f, i] = slab_plane(src[a, x], src[b, x], halo(a, x), halo(b, x))
-            out[6, i] = slab_plane(masks[0, x].astype(F32), masks[1, x].astype(F32), halo(12, x), halo(13, x))
-            out[7, i] = slab_plane(masks[2, x].astype(F32), absorb[x], halo(14, x), halo(15, x))
+                out[3 * f + i] = slab_plane(src[a, x], src[b, x], halo(a, x), halo(b, x))
+            out[18 + i] = slab_plane(masks[0, x].astype(F32), masks[1, x].astype(F32), halo(12, x), halo(13, x))
+            out[21 + i] = slab_plane(masks[2, x].astype(F32), absorb[x], halo(14, x), halo(15, x))
         none = jnp.zeros((8, 128), F32)
         edge = pe[:TY] if start == 0 else pe[CELLS - TY :]
         hi = edge.astype(BF16).astype(F32)
-        out[8, 0] = slab_plane(hi, edge - hi, none, none)
-        out[8, 1] = jnp.zeros((SLAB, 128), BF16)
-        out[8, 2] = jnp.zeros((SLAB, 128), BF16)
-
-
-def slabs(src, masks, absorb, pe, low, high):
+        out[24] = slab_plane(hi, edge - hi, none, none)
+        out[25] = jnp.zeros((SLAB, 128), BF16)
+        out[26] = jnp.zeros((SLAB, 128), BF16)
+
+    fill_sides(fill, core_out, chip_out)
+    for k, rows in enumerate((b0, b1, b2, b3)):
+        core_out[27 + 8 * k : 35 + 8 * k] = rows[...].reshape(8, SLAB, 128)
+
+
+def slabs(src, masks, absorb, pe, inner, outer, rows):
     return pl.pallas_call(
         slabs_kernel,
-        in_specs=[whole()] * 6,
-        out_specs=[whole()] * 2,
-        out_shape=[shape(9, 3, SLAB, NZ, dtype=BF16)] * 2,
+        in_specs=[whole()] * 10,
+        out_specs=[whole()] * 4,
+        out_shape=[shape(59, SLAB, NZ, dtype=BF16), shape(27, SLAB, NZ, dtype=BF16)] + [shape(17, 4, 8, NZ)] * 2,
         compiler_params=params(),
         name="slabs",
-    )(src, masks, absorb, pe, low, high)
+    )(src, masks, absorb, pe, inner, outer, *rows)
 
 
 def complex_times(are, aim, re, im):
     return are * re - aim * im, are * im + aim * re
 
 
-def update_kernel(res, img, alpha, low0, high0, low1, high1, out, low, high, left, right):
+def update_kernel(res, img, alpha, low0, high0, inner, outer, out, low, high, core_out, chip_out):
+    even = even_row()
     for f in range(FIELDS):
         are = alpha[f : f + 1, :]
         aim = alpha[8 + f : 9 + f, :]
@@ -248,20 +310,25 @@
         pre, pim = complex_times(are, aim, img[a], img[b])
         out[a] = res[a] - pre
         out[b] = res[b] - pim
-        pre, pim = complex_times(are, aim, low1[a], low1[b])
+        pre, pim = complex_times(are, aim, *[jnp.where(even, inner[ch], outer[ch]) for ch in (a, b)])
         low[a] = low0[a] - pre
         low[b] = low0[b] - pim
-        pre, pim = complex_times(are, aim, high1[a], high1[b])
+        pre, pim = complex_times(are, aim, *[jnp.where(even, outer[ch], inner[ch]) for ch in (a, b)])
         high[a] = high0[a] - pre
         high[b] = high0[b] - pim
-        for slab, start in ((left, 0), (right, TX - 3)):
+
+    def fill(slab, start):
+        for f in range(FIELDS):
+            a, b = 2 * f, 2 * f + 1
             for i in range(3):
                 x = start + i
                 halos = [halo_rows(low[ch], high[ch], x) for ch in (a, b)]
-                slab[f, i] = slab_plane(out[a, x], out[b, x], *halos)
-
-
-def update(res, img, alpha, low0, high0, low1, high1):
+                slab[3 * f + i] = slab_plane(out[a, x], out[b, x], *halos)
+
+    fill_sides(fill, core_out, chip_out)
+
+
+def update(res, img, alpha, low0, high0, inner, outer):
     return pl.pallas_call(
         update_kernel,
         in_specs=[whole()] * 7,
@@ -270,24 +337,25 @@
             shape(12, TX, TY, NZ),
             shape(12, 4, 8, NZ),
             shape(12, 4, 8, NZ),
-            shape(FIELDS, 3, SLAB, NZ, dtype=BF16),
-            shape(FIELDS, 3, SLAB, NZ, dtype=BF16),
+            shape(18, SLAB, NZ, dtype=BF16),
+            shape(18, SLAB, NZ, dtype=BF16),
         ],
         compiler_params=params(),
         name="update",
-    )(res, img, alpha, low0, high0, low1, high1)
+    )(res, img, alpha, low0, high0, inner, outer)
 
 
 def local_kernel(src, low, high, left, right, mask, mlow, mhigh, mleft, mright, absorb, alow, ahigh, aleft, aright,
                  local, image, inv, r, z1, z2, z3):
     lane = iota((TY + 8, NZ), 1)
 
-    def plane(cells, lo, hi, lft, rgt, c, p):
-        if p < 0:
-            return slab_part(lft, p + 3, c)
-        if p >= TX:
-            return slab_part(rgt, p - TX, c)
-        return wide_plane(cells, lo, hi, p)
+    core = own_core()
+
+    def plane(cells, lo, hi, by_core, by_chip, c, p):
+        if 0 <= p < TX:
+            return wide_plane(cells, lo, hi, p)
+        i, by_chip_on = (p + 3, 0) if p < 0 else (p - TX, 1)
+        return jnp.where(core == by_chip_on, slab_part(by_chip, i, c), slab_part(by_core, i, c))
 
     which = (pl.program_id(0) // 2) % 2
     for p in range(-3, TX + 3):
@@ -295,8 +363,8 @@
         if 0 <= p < TX:
             m = jnp.concatenate([mask[0, p].astype(F32), halo_rows(mlow[0], mhigh[0], p)], axis=0)
         else:
-            m = plane(None, None, None, mleft.at[0], mright.at[0], which, p)
-        dim = plane(absorb, alow[0], ahigh[0], aleft.at[0], aright.at[0], 1, p)
+            m = plane(None, None, None, mleft, mright, which, p)
+        dim = plane(absorb, alow[0], ahigh[0], aleft, aright, 1, p)
         dre = 5.5 - m
         inside = dim > 1.0
         scale = 1.0 / jnp.where(inside, dre * dre + dim * dim, 1.0)
@@ -304,8 +372,8 @@
         iim = jnp.where(inside, -dim * scale, 0.0)
         inv[0, i] = ire
         inv[1, i] = iim
-        re = plane(src[0], low[0], high[0], left.at[0], right.at[0], 0, p)
-        im = plane(src[1], low[1], high[1], left.at[0], right.at[0], 1, p)
+        re = plane(src[0], low[0], high[0], left, right, 0, p)
+        im = plane(src[1], low[1], high[1], left, right, 1, p)
         r[0, i] = re
         r[1, i] = im
         z1[0, i], z1[1, i] = complex_times(ire, iim, re, im)
@@ -338,13 +406,15 @@
     return pl.BlockSpec((1,) + dims, lambda f: (offset(f),) + (0,) * len(dims))
 
 
+def slab_of(which):
+    return pl.BlockSpec((3, SLAB, NZ), lambda f: (which(f), 0, 0))
+
+
 def local_solve(res, low, high, left, right, masks, absorb, dlow, dhigh, dleft, dright):
     of_mask = lambda f: 12 + f // 2
     of_absorb = lambda f: 15
     y = (4, 8, NZ)
-    x = (3, SLAB, NZ)
-    pair = channel(lambda f: f, *x)
-    mask_pair, absorb_pair = channel(lambda f: 6 + f // 4, *x), channel(lambda f: 7, *x)
+    pair, mask_pair, absorb_pair = slab_of(lambda f: f), slab_of(lambda f: 6 + f // 4), slab_of(lambda f: 7)
     planes = pltpu.VMEM((2, TX + 6, TY + 8, NZ), F32)
     return pl.pallas_call(
         local_kernel,
@@ -401,32 +471,63 @@
     return (t % GY) * GX + t // GY
 
 
-def column_sweep(index, y0, chosen, pairs, out):
+def column_sweep(index, y0, chosen, rows, out):
     p, q = own_place()
-    for k in range(GX // 2):
-        for c in range(2):
-            a = ((p // 2 + GX // 2 - k) % (GX // 2)) * 2 + (p % 2 + c) % 2
-            y = y0[a * GY + q] - sweep(index, a, q, pairs[k].at[c], chosen)
-            out[:, a] = jnp.broadcast_to(y.astype(BF16)[None], (GY, 8, 128))
-
-
-def column_sweep_kernel(by_column, index, every, y0, b0, b1, b2, b3, out):
-    place = column_place if by_column else lambda t: t
-    column_sweep(index, y0, lambda t: every[place(t)], (b0, b1, b2, b3), out)
-
-
-def column_call(by_column, index, every, y0, pairs):
-    return pl.pallas_call(
-        functools.partial(column_sweep_kernel, by_column),
-        in_specs=[smem()] + [whole()] * 6,
+    for i in range(GX):
+        a = ((p // 2 + GX // 2 - i // 2) % (GX // 2)) * 2 + (p % 2 + i % 2) % 2
+        y = y0[a * GY + q] - sweep(index, a, q, rows(i), chosen)
+        out[:, a] = jnp.broadcast_to(y.astype(BF16)[None], (GY, 8, 128))
+
+
+def packed_blocks(slab, k):
+    rows = slab[8 * k : 8 * k + 8].reshape(NNZ * 128, 128)
+    return [rows[128 * j : 128 * j + 128] for j in range(NNZ)]
+
+
+def first_column_kernel(index, every, y0, b0, b1, b2, b3, by_core, out):
+    own = (b0, b1, b2, b3)
+    theirs = by_core.at[27:59]
+    column_sweep(
+        index, y0, lambda t: every[t], lambda i: packed_blocks(theirs, i // 2) if i % 2 else own[i // 2], out
+    )
+
+
+def first_column(index, every, y0, rows, by_core):
+    return pl.pallas_call(
+        first_column_kernel,
+        in_specs=[smem()] + [whole()] * 7,
         out_specs=whole(),
         out_shape=shape(GY, GX, 8, 128, dtype=BF16),
         compiler_params=params(),
         name="column_sweep",
-    )(index, every, y0, *pairs)
-
-
-def last_sweep_kernel(index, every, y0, b0, b1, b3, blow, bhigh, out):
+    )(index, every, y0, *rows, by_core)
+
+
+def column_rows(own, theirs):
+    return lambda i: packed_blocks(theirs, i // 2) if i % 2 else own.at[i // 2]
+
+
+def column_sweep_kernel(index, every, y0, own, theirs, out):
+    column_sweep(index, y0, lambda t: every[column_place(t)], column_rows(own, theirs), out)
+
+
+def column_call(index, every, y0, own, theirs):
+    return pl.pallas_call(
+        column_sweep_kernel,
+        in_specs=[smem()] + [whole()] * 4,
+        out_specs=whole(),
+        out_shape=shape(GY, GX, 8, 128, dtype=BF16),
+        compiler_params=params(),
+        name="column_sweep",
+    )(index, every, y0, own, theirs)
+
+
+def edge_blocks(edges):
+    rows = edges[15:25].reshape(NNZ * 128, 128)
+    return [rows[128 * j : 128 * j + 128] for j in range(NNZ)]
+
+
+def last_sweep_kernel(index, every, y0, own, theirs, inner, outer, out):
     p, q = own_place()
     take = lambda t: every[column_place(t)]
     pw, pe = jnp.maximum(p - 1, 0), jnp.minimum(p + 1, GX - 1)
@@ -435,30 +536,46 @@
     def put(i, a, b, rows):
         out[i] = y0[a * GY + b] - sweep(index, a, b, rows, take)
 
-    put(0, p, q, b0.at[0])
-    put(3, p, ql, blow)
-    put(4, p, qr, bhigh)
+    put(0, p, q, own)
+
+    @pl.when(q % 2 == 0)
+    def _():
+        put(3, p, ql, edge_blocks(outer))
+        put(4, p, qr, edge_blocks(inner))
+
+    @pl.when(q % 2 == 1)
+    def _():
+        put(3, p, ql, edge_blocks(inner))
+        put(4, p, qr, edge_blocks(outer))
 
     @pl.when(p % 2 == 0)
     def _():
-        put(1, pw, q, b1.at[1])
-        put(2, pe, q, b0.at[1])
+        put(1, pw, q, packed_blocks(theirs, 1))
+        put(2, pe, q, packed_blocks(theirs, 0))
 
     @pl.when(p % 2 == 1)
     def _():
-        put(1, pw, q, b0.at[1])
-        put(2, pe, q, b3.at[1])
-
-
-def last_sweep(index, every, y0, pairs, blow, bhigh):
-    return pl.pallas_call(
-        last_sweep_kernel,
-        in_specs=[smem()] + [whole()] * 7,
+        put(1, pw, q, packed_blocks(theirs, 0))
+        put(2, pe, q, packed_blocks(theirs, 3))
+
+
+def first_last_kernel(index, every, y0, own, by_core, inner, outer, out):
+    last_sweep_kernel(index, every, y0, own, by_core.at[27:59], inner, outer, out)
+
+
+def later_last_kernel(index, every, y0, own, theirs, inner, outer, out):
+    last_sweep_kernel(index, every, y0, own.at[0], theirs, inner, outer, out)
+
+
+def last_sweep(kernel, index, every, y0, own, theirs, inner, outer):
+    return pl.pallas_call(
+        kernel,
+        in_specs=[smem()] + [whole()] * 6,
         out_specs=whole(),
         out_shape=shape(5, 8, 128),
         compiler_params=params(),
         name="last_sweep",
-    )(index, every, y0, pairs[0], pairs[1], pairs[3], blow, bhigh)
+    )(index, every, y0, own, theirs, inner, outer)
 
 
 def alphas(total):
@@ -474,7 +591,11 @@
     return are, aim
 
 
-def restart_kernel(index, every, before, b0, b1, b2, b3, out, y0, alpha):
+def restart_kernel(index, every, before, b0, b1, b2, b3, by_core, out, y0, alpha, own, theirs, sems):
+    copies = [pltpu.make_async_copy(rows, own.at[k], sems.at[k]) for k, rows in enumerate((b0, b1, b2, b3))]
+    copies.append(pltpu.make_async_copy(by_core.at[27:59], theirs, sems.at[4]))
+    for copy in copies:
+        copy.start()
     are, aim = alphas(jnp.sum(every[...], axis=0)[6:7])
     alpha[:8] = are
     alpha[8:] = aim
@@ -487,18 +608,27 @@
         y0[t] = before[t] - (are * part + aim * pltpu.roll(part, 64, 1))
 
     lax.fori_loop(0, TILES, coarse, None, unroll=8)
-    column_sweep(index, y0, lambda t: y0[t].astype(BF16), (b0, b1, b2, b3), out)
-
-
-def restart(index, every, before, pairs):
+    for copy in copies:
+        copy.wait()
+    column_sweep(index, y0, lambda t: y0[t].astype(BF16), column_rows(own, theirs), out)
+
+
+def restart(index, every, before, rows, by_core):
     return pl.pallas_call(
         restart_kernel,
-        in_specs=[smem()] + [whole()] * 6,
-        out_specs=[whole()] * 3,
-        out_shape=[shape(GY, GX, 8, 128, dtype=BF16), shape(TILES, 8, 128), shape(16, 128)],
+        in_specs=[smem()] + [whole()] * 2 + [anywhere()] * 5,
+        out_specs=[whole()] * 5,
+        out_shape=[
+            shape(GY, GX, 8, 128, dtype=BF16),
+            shape(TILES, 8, 128),
+            shape(16, 128),
+            shape(4, NNZ, 128, 128, dtype=BF16),
+            shape(32, SLAB, 128, dtype=BF16),
+        ],
+        scratch_shapes=[pltpu.SemaphoreType.DMA((5,))],
         compiler_params=params(),
         name="restart",
-    )(index, every, before, *pairs)
+    )(index, every, before, *[far(row) for row in rows], far(by_core))
 
 
 def image_kernel(last, ys, pe, elow, ehigh, eleft, eright, depth, masks, absorb, res, local, part,
@@ -506,8 +636,16 @@
     if last:
         direction, image, pay, mats, rows, edge, sides, acc = refs
     else:
-        direction, image, pay, ylo, yhi, mats, rows, edge, sides, acc = refs
+        direction, image, pay_far, in_far, out_far, mats, rows, edge, sides, acc, pay, inner, outer, sems = refs
     f = pl.program_id(0)
+
+    def sent(i):
+        two = pl.ds(2 * i, 2)
+        return (
+            pltpu.make_async_copy(inner.at[two], in_far.at[two], sems.at[i]),
+            pltpu.make_async_copy(outer.at[two], out_far.at[two], sems.at[FIELDS + i]),
+        )
+
     sub8 = iota((8, NZ), 0)
 
     @pl.when(f == 0)
@@ -523,8 +661,9 @@
         mats[2] = jnp.concatenate([lo, nlo], axis=0)
         rows[...] = jnp.concatenate([hi, lo], axis=0)
         acc[...] = jnp.zeros_like(acc)
-        for i, slab in enumerate((eleft, eright)):
-            sides[i] = slab[0, 0, :TY].astype(F32) + slab[0, 0, TY : 2 * TY].astype(F32)
+        by_core, by_chip = [s[0, :TY].astype(F32) + s[0, TY : 2 * TY].astype(F32) for s in (eleft, eright)]
+        sides[0] = jnp.where(own_core() == 0, by_chip, by_core)
+        sides[1] = jnp.where(own_core() == 0, by_core, by_chip)
         for x in range(TX):
             low = jnp.broadcast_to(ehigh[0, 0, x : x + 1, :], (8, 128))
             high = jnp.broadcast_to(elow[0, 0, x : x + 1, :], (8, 128))
@@ -572,8 +711,9 @@
     if not last:
         acc[row, :] = restrict_rows(ire, iim, pe[...], rows[...])
         for c, value in ((0, ire), (1, iim)):
-            ylo[c] = pack_low(value)
-            yhi[c] = pack_high(value)
+            inner[2 * f + c], outer[2 * f + c] = by_pairs(pack_low(value), pack_high(value))
+        for copy in sent(f):
+            copy.start()
 
     @pl.when(f == FIELDS - 1)
     def _():
@@ -581,18 +721,27 @@
             pay[...] = jnp.broadcast_to(acc[6:7, :], pay.shape)
         else:
             pay[...] = jnp.broadcast_to(acc[...][None], pay.shape)
+            copy = pltpu.make_async_copy(pay, pay_far, sems.at[2 * FIELDS])
+            copy.start()
+            for i in range(FIELDS):
+                for other in sent(i):
+                    other.wait()
+            copy.wait()
 
 
 def image_call(last, ys, pe, dlow, dhigh, dleft, dright, depth, masks, absorb, res, local, part):
     edge_y = channel(lambda f: 16, 4, 8, NZ)
-    edge_x = channel(lambda f: 8, 3, SLAB, NZ)
+    edge_x = slab_of(lambda f: 8)
     cells = fields(TX, TY, NZ)
     pay = (TILES, 128) if last else (TILES, 8, 128)
-    out_specs = [cells, cells, fixed(*pay)]
-    out_shape = [(shape if last else far_shape)(12, TX, TY, NZ), shape(12, TX, TY, NZ), shape(*pay)]
+    out_specs = [cells, cells, fixed(*pay) if last else anywhere()]
+    scratch = []
+    out_shape = [(shape if last else far_shape)(12, TX, TY, NZ), shape(12, TX, TY, NZ), (shape if last else far_shape)(*pay)]
     if not last:
-        out_specs += [fields(4, 8, NZ)] * 2
-        out_shape += [shape(12, 4, 8, NZ)] * 2
+        out_specs += [anywhere()] * 2
+        out_shape += [far_shape(12, 4, 8, NZ)] * 2
+        scratch = [pltpu.VMEM(pay, F32)] + [pltpu.VMEM((12, 4, 8, NZ), F32)] * 2
+        scratch.append(pltpu.SemaphoreType.DMA((2 * FIELDS + 1,)))
     return pl.pallas_call(
         functools.partial(image_kernel, last),
         grid=(FIELDS,),
@@ -607,7 +756,7 @@
             pltpu.VMEM((2, TX, 8, 128), F32),
             pltpu.VMEM((2, TY, 128), F32),
             pltpu.VMEM((8, 128), F32),
-        ],
+        ] + scratch,
         compiler_params=params(),
         name="image",
     )(ys, pe, dlow, dhigh, dleft, dright, depth, masks, absorb, res, local, part)
@@ -647,14 +796,13 @@
     )(every, alpha, dir1, dir2, res, img)
 
 
-def down(value, axis):
-    count = lax.axis_size(axis)
-    return lax.ppermute(value, axis, [(i + 1, i) for i in range(count - 1)])
-
-
-def up(value, axis):
-    count = lax.axis_size(axis)
-    return lax.ppermute(value, axis, [(i, i + 1) for i in range(count - 1)])
+def swap_pairs(value):
+    return lax.ppermute(value, "gy", [(i, i ^ 1) for i in range(GY)])
+
+
+def swap_between(value):
+    ends = [(i, i + 1) for i in range(1, GY - 1, 2)]
+    return lax.ppermute(value, "gy", ends + [(j, i) for i, j in ends])
 
 
 def gather(copies, axes=BOTH):
@@ -663,6 +811,11 @@
 
 def swap_cores(value):
     return lax.ppermute(value, "gx", [(i, i ^ 1) for i in range(GX)])
+
+
+def swap_chips(value):
+    ends = [(i, i + 1) for i in range(1, GX - 1, 2)]
+    return lax.ppermute(value, "gx", ends + [(j, i) for i, j in ends])
 
 
 def round_x(value, k):
@@ -678,40 +831,36 @@
     blocks = coupling_blocks.reshape(NNZ, 128, 128)
     index = coupling_index.reshape(-1)
 
-    y0b, pe, ylo, yhi = first(src, masks, absorption, plane_basis, depth_basis)
+    y0b, pe, inner, outer = first(src, masks, absorption, plane_basis, depth_basis, blocks)
     all0 = gather(y0b)
-    low0, high0 = down(ylo, "gy"), up(yhi, "gy")
-    other = swap_cores(blocks)
-    own_pair = jnp.stack([blocks, other])
-    blow, bhigh = up(blocks, "gy"), down(blocks, "gy")
-    y1b = tile_sweep(index, after(all0, other), blocks)
+    inner0, outer0 = swap_pairs(inner), swap_between(outer)
+    rows = [blocks] + [round_x(blocks, k) for k in (1, 2, 3)]
+    y1b = tile_sweep(index, all0, blocks)
     all1 = gather(y1b)
-    to_left, to_right = slabs(src, masks, absorption, after(pe, y1b), low0, high0)
-    left0, right0 = up(to_right, "gx"), down(to_left, "gx")
-    mine = after(own_pair, y1b)
-    pairs = [own_pair] + [round_x(mine, k) for k in (1, 2, 3)]
-    y2b = column_call(False, index, after(all1, left0, right0, blow, bhigh), all0, pairs)
+    for_core, for_chip, low0, high0 = slabs(src, masks, absorption, after(pe, y1b), inner0, outer0, rows)
+    core0, chip0 = swap_cores(for_core), swap_chips(for_chip)
+    y2b = first_column(index, after(all1, core0, chip0), all0, rows, core0)
     all2 = gather(y2b, "gy").reshape(TILES, 8, 128)
     local, part = local_solve(
-        src, low0, high0, after(left0, all2), right0, masks, absorption, low0, high0, left0, right0
+        src, low0, high0, after(core0, all2), chip0, masks, absorption, low0, high0, core0, chip0
     )
-    ys = last_sweep(index, after(all2, part), all0, pairs, blow, bhigh)
-    dir1, img1, pay, ylo, yhi = image_call(
-        False, ys, pe, low0, high0, left0, right0, depth_basis, masks, absorption, src, local, part
+    ys = last_sweep(first_last_kernel, index, after(all2, part), all0, blocks, core0, inner0, outer0)
+    dir1, img1, pay, inner, outer = image_call(
+        False, ys, pe, low0, high0, core0, chip0, depth_basis, masks, absorption, src, local, part
     )
 
     all3 = gather(pay)
-    low1, high1 = down(ylo, "gy"), up(yhi, "gy")
-    y1b, y0, alpha = restart(index, all3, all0, pairs)
+    inner1, outer1 = swap_pairs(inner), swap_between(outer)
+    y1b, y0, alpha, own, theirs = restart(index, all3, all0, rows, core0)
     all1 = gather(y1b, "gy").reshape(TILES, 8, 128)
-    res, low, high, to_left, to_right = update(src, img1, alpha, low0, high0, low1, high1)
-    left, right = up(to_right, "gx"), down(to_left, "gx")
-    y2b = column_call(True, index, after(all1, left, right), y0, pairs)
+    res, low, high, for_core, for_chip = update(src, img1, alpha, low0, high0, inner1, outer1)
+    by_core, by_chip = swap_cores(for_core), swap_chips(for_chip)
+    y2b = column_call(index, after(all1, by_core, by_chip), y0, own, theirs)
     all2 = gather(y2b, "gy").reshape(TILES, 8, 128)
-    local, part = local_solve(res, low, high, after(left, all2), right, masks, absorption, low0, high0, left0, right0)
-    ys = last_sweep(index, after(all2, part), y0, pairs, blow, bhigh)
+    local, part = local_solve(res, low, high, after(by_core, all2), by_chip, masks, absorption, low0, high0, core0, chip0)
+    ys = last_sweep(later_last_kernel, index, after(all2, part), y0, own, theirs, inner0, outer0)
     dir2, img2, pay = image_call(
-        True, ys, pe, low0, high0, left0, right0, depth_basis, masks, absorption, res, local, part
+        True, ys, pe, low0, high0, core0, chip0, depth_basis, masks, absorption, res, local, part
     )
     all3 = gather(pay)
     solution, residual = finish(all3, alpha, dir1, dir2, res, img2)

time: 187 us -> 167 us (0.89)
  starting transfers between devices: 46.9 us -> 31.8 us
  local copies, waits for them, and re-layouts: 11.4 us -> 3.73 us
  blocking collectives: 75.7 us -> 68.8 us
  waiting for transfers between devices: 14.1 us -> 20.3 us
  Pallas kernels: 36.1 us -> 40.5 us
    ppermute x10 -> x6, starting transfers between devices: 25.9 us -> 10.6 us  [the longest x2 4.89 us: swap_chips(): return lax.ppermute(value, 'gx', ends + [(j, i) for i, j in ends])]
    all_to_all x5, blocking collectives: 75.7 us -> 68.8 us  [gather(): return lax.all_to_all(copies, axes, 0, 0, tiled=True)]
    unnamed x69 -> x57, local copies, waits for them, and re-layouts: 10.4 us -> 3.53 us
    all_to_all x2, waiting for transfers between devices: 13.1 us -> 18.6 us  [gather(): return lax.all_to_all(copies, axes, 0, 0, tiled=True)]
    pallas_call x7, Pallas kernels: 13.2 us -> 16.3 us  [the longest x1 4.52 us: first(): pl.pallas_call(first_kernel, in_specs=[anywhere()] * 6, out_specs=[anywhe...]
  transfers between devices with their start and end apart: 16 -> 13, of which waited for: 4 -> 3; matrix products, arithmetic and copies ran while one was open for 1% -> 0% of each run, Pallas kernels for 2% -> 2%
where the time goes in v3:
time: 167 us; the launch traced here: 166 us
  blocking collectives  68.8 us (41%)
  Pallas kernels  40.5 us (24%)
  starting transfers between devices  31.8 us (19%)
  waiting for transfers between devices  20.3 us (12%)
  local copies, waits for them, and re-layouts  3.73 us (2%)
    all_to_all x5, blocking collectives, gather(): return lax.all_to_all(copies, axes, 0, 0, tiled=True)  68.8 us
    all_to_all x2, waiting for transfers between devices, gather(): return lax.all_to_all(copies, axes, 0, 0, tiled=True)  18.6 us
    all_to_all x2, starting transfers between devices, gather(): return lax.all_to_all(copies, axes, 0, 0, tiled=True)  16.3 us
    pallas_call x2, Pallas kernels, local_solve(): pl.pallas_call(local_kernel, grid=(FIELDS,), in_specs=[fields(TX, TY, NZ)...  10.4 us
    pallas_call x2, Pallas kernels, image_call(): pl.pallas_call(functools.partial(image_kernel, last), grid=(FIELDS,), in_...  8.74 us
    ppermute x2, starting transfers between devices, swap_chips(): return lax.ppermute(value, 'gx', ends + [(j, i) for i, j in ends])  4.89 us
    pallas_call x1, Pallas kernels, first(): pl.pallas_call(first_kernel, in_specs=[anywhere()] * 6, out_specs=[anywhe...  4.52 us
    ppermute x3, starting transfers between devices, round_x(): return lax.ppermute(value, 'gx', [(i, (i + 2 * k) % GX) for i in range(GX)])  3.55 us
  transfers between devices with their start and end apart: 13, of which 3 were waited for; matrix products, arithmetic and copies ran while one was open for 0% of the time, Pallas kernels for 2%

profile of v3, /device:TPU:1, one launch (start us, length us, event | category | flops | bytes accessed | tf_op | source)
XLA Modules:
  0.0 166.1 jit_solution(15285823897134494267)
XLA Ops:
  0.6 0.0 copy-start.13
  0.7 4.5 %first.1 = (f32[128,8,128]{2,1,0:T(8,128)}, f32[256,128]{1,0:T(8,128)S(1)}, bf16[25,4,16,128]{3,2,1,0:T(8,128)(2,1)}, bf16[25,4,16,128]{3,2,1,0:T(8,128)(2,1)}) custom-call(f32[12,8,32,128]{3,2,1,0:T(8,128)} %bitcast.11, s32[3,8,32,128]{3,2,1,0:T(8,128)} %masks.5, f32[8,32,128]{2,1,0:T(8,128)} %absorb.9, f32[8,8,32]{2,1,0:T(8,128)} %plane_far.1, ...), custom_call_target="tpu_custom_call" | custom-call | tf_op jit(solution)/shard_map/first/pallas_call | solution.py:192
  5.2 0.0 copy-start.2
  5.2 0.0 copy-start.7
  5.2 0.0 copy-start.14
  5.2 11.5 %all-to-all-start = ((f32[128,8,128]{2,1,0:T(8,128)}), f32[128,8,128]{2,1,0:T(8,128)S(1)}, u32[]{:S(2)}, u32[]{:S(2)}) async-start(f32[128,8,128]{2,1,0:T(8,128)} %get-tuple-element.41), calls=%async_computation | async-start | bytes 1048576 | tf_op jit(solution)/shard_map/all_to_all | solution.py:809
  16.7 1.5 collective-permute-start
  18.2 1.4 collective-permute-start.1
  19.6 2.4 %collective-permute-start.4 = (bf16[5,128,128]{2,1,0:T(8,128)(2,1)S(1)}, bf16[5,128,128]{2,1,0:T(8,128)(2,1)}, u32[]{:S(2)}, u32[]{:S(2)}) collective-permute-start(bf16[5,128,128]{2,1,0:T(8,128)(2,1)S(1)} %bitcast.18), channel_id=1, source_target_pairs={{0,96},{16,112},{32,0},{48,16},{64,32},{80,48},{96,64},{112,80},{1... | collective-permute-start | bytes 491528 | tf_op jit(solution)/shard_map/ppermute | solution.py:822
  22.0 0.6 collective-permute-start.3
  22.6 0.6 collective-permute-start.2
  23.2 0.1 copy.10
  23.3 0.2 reshape.30.index
  23.5 7.3 %all-to-all-done.every.y0.before = f32[128,8,128]{2,1,0:T(8,128)S(1)} async-done(((f32[128,8,128]{2,1,0:T(8,128)}), f32[128,8,128]{2,1,0:T(8,128)S(1)}, u32[]{:S(2)}, u32[]{:S(2)}) %all-to-all-start) | async-done | bytes 524320 | tf_op jit(solution)/shard_map/all_to_all | solution.py:809
  30.8 0.8 tile_sweep.1
  31.6 1.7 collective-permute-done.2.b1
  33.3 1.6 slabs.1
  35.0 0.5 collective-permute-start.5
  35.5 2.7 %collective-permute-start.6 = (bf16[27,80,128]{2,1,0:T(8,128)(2,1)S(1)}, bf16[27,80,128]{2,1,0:T(8,128)(2,1)S(1)}, u32[]{:S(2)}, u32[]{:S(2)}) collective-permute-start(bf16[27,80,128]{2,1,0:T(8,128)(2,1)S(1)} %get-tuple-element.47), channel_id=1, source_target_pairs={{16,32},{48,64},{80,96},{32,16},{64,48},{96,80},{17,33},{49,65},{8... | collective-permute-start | bytes 1658888 | tf_op jit(solution)/shard_map/ppermute | solution.py:818
  38.2 0.0 copy-start.15
  38.3 20.6 %all_to_all.41.every = bf16[128,8,128]{2,1,0:T(8,128)(2,1)S(1)} all-to-all(bf16[128,8,128]{2,1,0:T(8,128)(2,1)S(1)} %tile_sweep.1), channel_id=1, replica_groups=mesh['gx'=8,'gy'=16] {'gx','gy'}, dimensions={0} | all-to-all | bytes 524288 | tf_op jit(solution)/shard_map/all_to_all | solution.py:809
  58.9 1.1 copy-done.11
  60.0 2.3 %column_sweep.2 = bf16[16,8,8,128]{3,2,1,0:T(8,128)(2,1)S(1)} custom-call(s32[640]{0:T(1024)S(1)} %reshape.30.index, bf16[128,8,128]{2,1,0:T(8,128)(2,1)S(1)} %all_to_all.41.every, f32[128,8,128]{2,1,0:T(8,128)S(1)} %copy-done.11, bf16[5,128,128]{2,1,0:T(8,128)(2,1)S(1)} %bitcast.23, bf16[5,128,128]{2,1,0:T(8,128)(2,1)} %collective-permute-done.2.b1, ...), custom_call_target="tpu_custom_call" | custom-call | tf_op jit(solution)/shard_map/column_sweep/pallas_call | solution.py:496
  62.3 10.8 %all_to_all.42 = bf16[16,8,8,128]{3,2,1,0:T(8,128)(2,1)S(1)} all-to-all(bf16[16,8,8,128]{3,2,1,0:T(8,128)(2,1)S(1)} %column_sweep.2), channel_id=1, replica_groups=mesh['gx'=8,'gy'=16] {'gy'}, dimensions={0} | all-to-all | bytes 524288 | tf_op jit(solution)/shard_map/all_to_all | solution.py:809
  73.1 5.2 %local.2 = (f32[12,8,32,128]{3,2,1,0:T(8,128)S(1)}, f32[12,8,32,128]{3,2,1,0:T(8,128)S(1)}) custom-call(f32[12,8,32,128]{3,2,1,0:T(8,128)S(1)} %bitcast.13, f32[17,4,8,128]{3,2,1,0:T(8,128)S(1)} %get-tuple-element.49.low.mlow.alow.elow.low0, f32[17,4,8,128]{3,2,1,0:T(8,128)S(1)} %get-tuple-element.50.high.mhigh.ahigh.ehigh.high0, ...), custom_call_target="tpu_custom_call" | custom-call | tf_op jit(solution)/shard_map/local/pallas_call | solution.py:419
  78.3 0.0 copy-start.26
  78.3 1.8 %last_sweep.2.ys = f32[5,8,128]{2,1,0:T(8,128)S(1)} custom-call(s32[640]{0:T(1024)S(1)} %reshape.30.index, bf16[128,8,128]{2,1,0:T(8,128)(2,1)S(1)} %bitcast.27, f32[128,8,128]{2,1,0:T(8,128)S(1)} %copy-done.11, bf16[5,128,128]{2,1,0:T(8,128)(2,1)S(1)} %bitcast.24, bf16[59,80,128]{2,1,0:T(8,128)(2,1)S(1)} %collective-permute-done.5.by_core.left.mleft.aleft.eleft, ...), custom_call_target="tpu_custom_call" | custom-call | tf_op jit(solution)/shard_map/last_sweep/pallas_call | solution.py:571
  80.1 0.0 copy-done
  80.1 5.7 %image.2 = (f32[12,8,32,128]{3,2,1,0:T(8,128)}, f32[12,8,32,128]{3,2,1,0:T(8,128)S(1)}, f32[128,8,128]{2,1,0:T(8,128)}, f32[12,4,8,128]{3,2,1,0:T(8,128)}, f32[12,4,8,128]{3,2,1,0:T(8,128)}) custom-call(f32[5,8,128]{2,1,0:T(8,128)S(1)} %last_sweep.2.ys, f32[256,128]{1,0:T(8,128)S(1)} %copy-done.24, ...), custom_call_target="tpu_custom_call" | custom-call | tf_op jit(solution)/shard_map/image/pallas_call | solution.py:745
  85.9 0.0 copy-start.21
  85.9 1.1 copy-done.21
  87.0 4.8 %all-to-all-start.3 = ((f32[128,8,128]{2,1,0:T(8,128)}), f32[128,8,128]{2,1,0:T(8,128)S(1)}, u32[]{:S(2)}, u32[]{:S(2)}) async-start(f32[128,8,128]{2,1,0:T(8,128)} %get-tuple-element.55), calls=%async_computation.3 | async-start | bytes 1048576 | tf_op jit(solution)/shard_map/all_to_all | solution.py:809
  91.9 1.5 collective-permute-start.7
  93.4 1.3 collective-permute-start.8
  94.8 11.3 %all-to-all-done.3.every = f32[128,8,128]{2,1,0:T(8,128)S(1)} async-done(((f32[128,8,128]{2,1,0:T(8,128)}), f32[128,8,128]{2,1,0:T(8,128)S(1)}, u32[]{:S(2)}, u32[]{:S(2)}) %all-to-all-start.3) | async-done | bytes 524320 | tf_op jit(solution)/shard_map/all_to_all | solution.py:809
  106.1 1.0 copy-done.12
  107.1 2.9 %restart.1 = (bf16[16,8,8,128]{3,2,1,0:T(8,128)(2,1)S(1)}, f32[128,8,128]{2,1,0:T(8,128)S(1)}, f32[16,128]{1,0:T(8,128)S(1)}, bf16[4,5,128,128]{3,2,1,0:T(8,128)(2,1)S(1)}, bf16[32,80,128]{2,1,0:T(8,128)(2,1)S(1)}) custom-call(s32[640]{0:T(1024)S(1)} %reshape.30.index, f32[128,8,128]{2,1,0:T(8,128)S(1)} %all-to-all-done.3.every, ...), custom_call_target="tpu_custom_call" | custom-call | tf_op jit(solution)/shard_map/restart/pallas_call | solution.py:617
  110.1 1.4 update.1
  111.5 0.7 collective-permute-start.9
  112.2 2.1 %collective-permute-start.10 = (bf16[18,80,128]{2,1,0:T(8,128)(2,1)S(1)}, bf16[18,80,128]{2,1,0:T(8,128)(2,1)S(1)}, u32[]{:S(2)}, u32[]{:S(2)}) collective-permute-start(bf16[18,80,128]{2,1,0:T(8,128)(2,1)S(1)} %get-tuple-element.62), channel_id=1, source_target_pairs={{16,32},{48,64},{80,96},{32,16},{64,48},{96,80},{17,33},{49,65},{8... | collective-permute-start | bytes 1105928 | tf_op jit(solution)/shard_map/ppermute | solution.py:818
  114.4 10.8 %all_to_all.43 = bf16[16,8,8,128]{3,2,1,0:T(8,128)(2,1)S(1)} all-to-all(bf16[16,8,8,128]{3,2,1,0:T(8,128)(2,1)S(1)} %get-tuple-element.56), channel_id=1, replica_groups=mesh['gx'=8,'gy'=16] {'gy'}, dimensions={0} | all-to-all | bytes 524288 | tf_op jit(solution)/shard_map/all_to_all | solution.py:809
  125.2 1.4 column_sweep.3
  126.6 11.1 %all_to_all.44 = bf16[16,8,8,128]{3,2,1,0:T(8,128)(2,1)S(1)} all-to-all(bf16[16,8,8,128]{3,2,1,0:T(8,128)(2,1)S(1)} %column_sweep.3), channel_id=1, replica_groups=mesh['gx'=8,'gy'=16] {'gy'}, dimensions={0} | all-to-all | bytes 524288 | tf_op jit(solution)/shard_map/all_to_all | solution.py:809
  137.7 5.2 %local.3 = (f32[12,8,32,128]{3,2,1,0:T(8,128)S(1)}, f32[12,8,32,128]{3,2,1,0:T(8,128)S(1)}) custom-call(f32[12,8,32,128]{3,2,1,0:T(8,128)S(1)} %get-tuple-element.67.src.res, f32[12,4,8,128]{3,2,1,0:T(8,128)S(1)} %get-tuple-element.68.low, f32[12,4,8,128]{3,2,1,0:T(8,128)S(1)} %get-tuple-element.69.high, ...), custom_call_target="tpu_custom_call" | custom-call | tf_op jit(solution)/shard_map/local/pallas_call | solution.py:419
  142.9 1.8 %last_sweep.3.ys = f32[5,8,128]{2,1,0:T(8,128)S(1)} custom-call(s32[640]{0:T(1024)S(1)} %reshape.30.index, bf16[128,8,128]{2,1,0:T(8,128)(2,1)S(1)} %bitcast.25, f32[128,8,128]{2,1,0:T(8,128)S(1)} %get-tuple-element.64.y0, bf16[4,5,128,128]{3,2,1,0:T(8,128)(2,1)S(1)} %get-tuple-element.65.own, bf16[32,80,128]{2,1,0:T(8,128)(2,1)S(1)} %get-tuple-element.66.theirs, ...), custom_call_target="tpu_custom_call" | custom-call | tf_op jit(solution)/shard_map/last_sweep/pallas_call | solution.py:571
  144.7 3.0 %image.3 = (f32[12,8,32,128]{3,2,1,0:T(8,128)S(1)}, f32[12,8,32,128]{3,2,1,0:T(8,128)S(1)}, f32[128,128]{1,0:T(8,128)S(1)}) custom-call(f32[5,8,128]{2,1,0:T(8,128)S(1)} %last_sweep.3.ys, f32[256,128]{1,0:T(8,128)S(1)} %copy-done.25, f32[17,4,8,128]{3,2,1,0:T(8,128)S(1)} %copy-done.4, f32[17,4,8,128]{3,2,1,0:T(8,128)S(1)} %copy-done.6, ...), custom_call_target="tpu_custom_call" | custom-call | tf_op jit(solution)/shard_map/image/pallas_call | solution.py:745
  147.7 15.5 %all_to_all.45 = f32[128,1,128]{2,1,0:T(1,128)S(1)} all-to-all(f32[128,1,128]{2,1,0:T(1,128)S(1)} %bitcast.29), channel_id=1, replica_groups=mesh['gx'=8,'gy'=16] {'gx','gy'}, dimensions={0} | all-to-all | bytes 131072 | tf_op jit(solution)/shard_map/all_to_all | solution.py:809
  163.3 2.9 %finish.1 = (f32[12,8,32,128]{3,2,1,0:T(8,128)}, f32[12,8,32,128]{3,2,1,0:T(8,128)}) custom-call(f32[128,128]{1,0:T(8,128)S(1)} %bitcast.28, f32[16,128]{1,0:T(8,128)S(1)} %get-tuple-element.58.alpha, f32[12,8,32,128]{3,2,1,0:T(8,128)S(1)} %copy-done.20, f32[12,8,32,128]{3,2,1,0:T(8,128)S(1)} %get-tuple-element.76.dir2, ...), custom_call_target="tpu_custom_call" | custom-call | tf_op jit(solution)/shard_map/finish/pallas_call | solution.py:787
  (55 shorter events, 0.1 us)
Async XLA Ops:
  0.6 19.0 %copy-start.13 = (bf16[1,1,5,128,128]{4,3,2,1,0:T(8,128)(2,1)S(1)}, bf16[1,1,5,128,128]{4,3,2,1,0:T(8,128)(2,1)}, u32[]{:S(2)}) copy-start(bf16[1,1,5,128,128]{4,3,2,1,0:T(8,128)(2,1)} %param.12) | copy-start | bytes 491524
  0.6 22.5 %copy-start.27 = (s32[8,16,5]{1,0,2:T(8,128)S(1)}, s32[8,16,5]{1,0,2:T(8,128)}, u32[]{:S(2)}) copy-start(s32[8,16,5]{1,0,2:T(8,128)} %param.13) | copy-start | bytes 7684
  5.2 29.7 %copy-start.23 = (f32[256,128]{1,0:T(8,128)}, f32[256,128]{1,0:T(8,128)S(1)}, u32[]{:S(2)}) copy-start(f32[256,128]{1,0:T(8,128)S(1)} %get-tuple-element.43.pe) | copy-start | bytes 393220
  5.2 28.1 %copy-start.2 = (f32[3,2,2,8,32,128]{5,4,3,2,1,0:T(8,128)S(1)}, f32[3,2,2,8,32,128]{5,4,3,2,1,0:T(8,128)}, u32[]{:S(2)}) copy-start(f32[3,2,2,8,32,128]{5,4,3,2,1,0:T(8,128)} %param.7) | copy-start | bytes 4718596
  5.2 28.1 %copy-start.7 = (s32[3,8,32,128]{3,2,1,0:T(8,128)S(1)}, s32[3,8,32,128]{3,2,1,0:T(8,128)}, u32[]{:S(2)}) copy-start(s32[3,8,32,128]{3,2,1,0:T(8,128)} %masks.5) | copy-start | bytes 1179652
  5.2 28.1 %copy-start.14 = (f32[8,32,128]{2,1,0:T(8,128)S(1)}, f32[8,32,128]{2,1,0:T(8,128)}, u32[]{:S(2)}) copy-start(f32[8,32,128]{2,1,0:T(8,128)} %absorb.9) | copy-start | bytes 393220
  5.2 25.6 %all-to-all-start = ((f32[128,8,128]{2,1,0:T(8,128)}), f32[128,8,128]{2,1,0:T(8,128)S(1)}, u32[]{:S(2)}, u32[]{:S(2)}) async-start(f32[128,8,128]{2,1,0:T(8,128)} %get-tuple-element.41), calls=%async_computation | async-start | bytes 1048576 | tf_op jit(solution)/shard_map/all_to_all | solution.py:809
  16.7 16.6 %collective-permute-start = (bf16[25,4,16,128]{3,2,1,0:T(8,128)(2,1)}, bf16[25,4,16,128]{3,2,1,0:T(8,128)(2,1)S(1)}, u32[]{:S(2)}, u32[]{:S(2)}) collective-permute-start(bf16[25,4,16,128]{3,2,1,0:T(8,128)(2,1)} %get-tuple-element.44), channel_id=1, source_target_pairs={{0,1},{1,0},{2,3},{3,2},{4,5},{5,4},{6,7},{7,6},{8,9},{9,8},{10,11... | collective-permute-start | bytes 1228808 | tf_op jit(solution)/shard_map/ppermute | solution.py:800
  18.2 15.1 %collective-permute-start.1 = (bf16[25,4,16,128]{3,2,1,0:T(8,128)(2,1)}, bf16[25,4,16,128]{3,2,1,0:T(8,128)(2,1)}, u32[]{:S(2)}, u32[]{:S(2)}) collective-permute-start(bf16[25,4,16,128]{3,2,1,0:T(8,128)(2,1)} %get-tuple-element.45), channel_id=1, source_target_pairs={{1,2},{3,4},{5,6},{7,8},{9,10},{11,12},{13,14},{2,1},{4,3},{6,5},{... | collective-permute-start | bytes 1228808 | tf_op jit(solution)/shard_map/ppermute | solution.py:805
  19.6 12.0 %collective-permute-start.4 = (bf16[5,128,128]{2,1,0:T(8,128)(2,1)S(1)}, bf16[5,128,128]{2,1,0:T(8,128)(2,1)}, u32[]{:S(2)}, u32[]{:S(2)}) collective-permute-start(bf16[5,128,128]{2,1,0:T(8,128)(2,1)S(1)} %bitcast.18), channel_id=1, source_target_pairs={{0,96},{16,112},{32,0},{48,16},{64,32},{80,48},{96,64},{112,80},{1... | collective-permute-start | bytes 491528 | tf_op jit(solution)/shard_map/ppermute | solution.py:822
  22.0 9.6 %collective-permute-start.3 = (bf16[5,128,128]{2,1,0:T(8,128)(2,1)S(1)}, bf16[5,128,128]{2,1,0:T(8,128)(2,1)}, u32[]{:S(2)}, u32[]{:S(2)}) collective-permute-start(bf16[5,128,128]{2,1,0:T(8,128)(2,1)S(1)} %bitcast.19), channel_id=1, source_target_pairs={{0,64},{16,80},{32,96},{48,112},{64,0},{80,16},{96,32},{112,48},{1... | collective-permute-start | bytes 491528 | tf_op jit(solution)/shard_map/ppermute | solution.py:822
  22.6 10.7 %collective-permute-start.2 = (bf16[5,128,128]{2,1,0:T(8,128)(2,1)S(1)}, bf16[5,128,128]{2,1,0:T(8,128)(2,1)}, u32[]{:S(2)}, u32[]{:S(2)}) collective-permute-start(bf16[5,128,128]{2,1,0:T(8,128)(2,1)S(1)} %bitcast.20), channel_id=1, source_target_pairs={{0,32},{16,48},{32,64},{48,80},{64,96},{80,112},{96,0},{112,16},{1... | collective-permute-start | bytes 491528 | tf_op jit(solution)/shard_map/ppermute | solution.py:822
  30.8 4.1 %copy-start.10 = (f32[128,8,128]{2,1,0:T(8,128)}, f32[128,8,128]{2,1,0:T(8,128)S(1)}, u32[]{:S(2)}) copy-start(f32[128,8,128]{2,1,0:T(8,128)S(1)} %all-to-all-done.every.y0.before) | copy-start | bytes 1572868
  33.3 1.6 copy-start.17
  34.9 45.1 %copy-start.3 = (f32[17,4,8,128]{3,2,1,0:T(8,128)}, f32[17,4,8,128]{3,2,1,0:T(8,128)S(1)}, u32[]{:S(2)}) copy-start(f32[17,4,8,128]{3,2,1,0:T(8,128)S(1)} %get-tuple-element.49.low.mlow.alow.elow.low0) | copy-start | bytes 835588
  34.9 45.1 %copy-start.5 = (f32[17,4,8,128]{3,2,1,0:T(8,128)}, f32[17,4,8,128]{3,2,1,0:T(8,128)S(1)}, u32[]{:S(2)}) copy-start(f32[17,4,8,128]{3,2,1,0:T(8,128)S(1)} %get-tuple-element.50.high.mhigh.ahigh.ehigh.high0) | copy-start | bytes 835588
  35.0 23.9 %collective-permute-start.5 = (bf16[59,80,128]{2,1,0:T(8,128)(2,1)S(1)}, bf16[59,80,128]{2,1,0:T(8,128)(2,1)S(1)}, u32[]{:S(2)}, u32[]{:S(2)}) collective-permute-start(bf16[59,80,128]{2,1,0:T(8,128)(2,1)S(1)} %get-tuple-element.46), channel_id=1, source_target_pairs={{0,16},{16,0},{32,48},{48,32},{64,80},{80,64},{96,112},{112,96},{1... | collective-permute-start | bytes 3624968 | tf_op jit(solution)/shard_map/ppermute | solution.py:813
  35.5 23.4 %collective-permute-start.6 = (bf16[27,80,128]{2,1,0:T(8,128)(2,1)S(1)}, bf16[27,80,128]{2,1,0:T(8,128)(2,1)S(1)}, u32[]{:S(2)}, u32[]{:S(2)}) collective-permute-start(bf16[27,80,128]{2,1,0:T(8,128)(2,1)S(1)} %get-tuple-element.47), channel_id=1, source_target_pairs={{16,32},{48,64},{80,96},{32,16},{64,48},{96,80},{17,33},{49,65},{8... | collective-permute-start | bytes 1658888 | tf_op jit(solution)/shard_map/ppermute | solution.py:818
  38.2 34.8 %copy-start.15 = (f32[8,32,128]{2,1,0:T(8,128)S(1)}, f32[8,32,128]{2,1,0:T(8,128)}, u32[]{:S(2)}) copy-start(f32[8,32,128]{2,1,0:T(8,128)} %absorb.9) | copy-start | bytes 393220
  58.8 14.2 %copy-start.8 = (s32[3,8,32,128]{3,2,1,0:T(8,128)S(1)}, s32[3,8,32,128]{3,2,1,0:T(8,128)}, u32[]{:S(2)}) copy-start(s32[3,8,32,128]{3,2,1,0:T(8,128)} %masks.5) | copy-start | bytes 1179652
  58.9 1.1 copy-start.11
  60.0 20.2 %copy-start = (bf16[59,80,128]{2,1,0:T(8,128)(2,1)}, bf16[59,80,128]{2,1,0:T(8,128)(2,1)S(1)}, u32[]{:S(2)}) copy-start(bf16[59,80,128]{2,1,0:T(8,128)(2,1)S(1)} %collective-permute-done.5.by_core.left.mleft.aleft.eleft) | copy-start | bytes 3624964
  73.1 5.2 %copy-start.18 = (bf16[25,4,16,128]{3,2,1,0:T(8,128)(2,1)S(1)}, bf16[25,4,16,128]{3,2,1,0:T(8,128)(2,1)}, u32[]{:S(2)}) copy-start(bf16[25,4,16,128]{3,2,1,0:T(8,128)(2,1)} %copy-done.17) | copy-start | bytes 1228804
  78.3 1.9 %copy-start.24 = (f32[256,128]{1,0:T(8,128)S(1)}, f32[256,128]{1,0:T(8,128)}, u32[]{:S(2)}) copy-start(f32[256,128]{1,0:T(8,128)} %copy-done.23) | copy-start | bytes 393220
  78.3 1.9 %copy-start.26 = (f32[8,128]{1,0:T(8,128)S(1)}, f32[8,128]{1,0:T(8,128)}, u32[]{:S(2)}) copy-start(f32[8,128]{1,0:T(8,128)} %depth.3) | copy-start | bytes 12292
  85.9 1.1 copy-start.21
  87.0 19.1 %all-to-all-start.3 = ((f32[128,8,128]{2,1,0:T(8,128)}), f32[128,8,128]{2,1,0:T(8,128)S(1)}, u32[]{:S(2)}, u32[]{:S(2)}) async-start(f32[128,8,128]{2,1,0:T(8,128)} %get-tuple-element.55), calls=%async_computation.3 | async-start | bytes 1048576 | tf_op jit(solution)/shard_map/all_to_all | solution.py:809
  91.9 18.2 %copy-start.4 = (f32[17,4,8,128]{3,2,1,0:T(8,128)S(1)}, f32[17,4,8,128]{3,2,1,0:T(8,128)}, u32[]{:S(2)}) copy-start(f32[17,4,8,128]{3,2,1,0:T(8,128)} %copy-done.3) | copy-start | bytes 835588
  91.9 18.2 %copy-start.6 = (f32[17,4,8,128]{3,2,1,0:T(8,128)S(1)}, f32[17,4,8,128]{3,2,1,0:T(8,128)}, u32[]{:S(2)}) copy-start(f32[17,4,8,128]{3,2,1,0:T(8,128)} %copy-done.5) | copy-start | bytes 835588
  91.9 18.2 %collective-permute-start.7 = (f32[12,4,8,128]{3,2,1,0:T(8,128)}, f32[12,4,8,128]{3,2,1,0:T(8,128)}, u32[]{:S(2)}, u32[]{:S(2)}) collective-permute-start(f32[12,4,8,128]{3,2,1,0:T(8,128)} %get-tuple-element.59), channel_id=1, source_target_pairs={{0,1},{1,0},{2,3},{3,2},{4,5},{5,4},{6,7},{7,6},{8,9},{9,8},{10,11... | collective-permute-start | bytes 589832 | tf_op jit(solution)/shard_map/ppermute | solution.py:800
  93.4 16.7 %collective-permute-start.8 = (f32[12,4,8,128]{3,2,1,0:T(8,128)}, f32[12,4,8,128]{3,2,1,0:T(8,128)}, u32[]{:S(2)}, u32[]{:S(2)}) collective-permute-start(f32[12,4,8,128]{3,2,1,0:T(8,128)} %get-tuple-element.60), channel_id=1, source_target_pairs={{1,2},{3,4},{5,6},{7,8},{9,10},{11,12},{13,14},{2,1},{4,3},{6,5},{... | collective-permute-start | bytes 589832 | tf_op jit(solution)/shard_map/ppermute | solution.py:805
  106.1 1.0 copy-start.12
  107.1 3.0 %copy-start.22 = (f32[12,8,32,128]{3,2,1,0:T(8,128)S(1)}, f32[12,8,32,128]{3,2,1,0:T(8,128)}, u32[]{:S(2)}) copy-start(f32[12,8,32,128]{3,2,1,0:T(8,128)} %copy-done.21) | copy-start | bytes 4718596
  111.5 13.6 %collective-permute-start.9 = (bf16[18,80,128]{2,1,0:T(8,128)(2,1)S(1)}, bf16[18,80,128]{2,1,0:T(8,128)(2,1)S(1)}, u32[]{:S(2)}, u32[]{:S(2)}) collective-permute-start(bf16[18,80,128]{2,1,0:T(8,128)(2,1)S(1)} %get-tuple-element.61), channel_id=1, source_target_pairs={{0,16},{16,0},{32,48},{48,32},{64,80},{80,64},{96,112},{112,96},{1... | collective-permute-start | bytes 1105928 | tf_op jit(solution)/shard_map/ppermute | solution.py:813
  112.2 12.9 %collective-permute-start.10 = (bf16[18,80,128]{2,1,0:T(8,128)(2,1)S(1)}, bf16[18,80,128]{2,1,0:T(8,128)(2,1)S(1)}, u32[]{:S(2)}, u32[]{:S(2)}) collective-permute-start(bf16[18,80,128]{2,1,0:T(8,128)(2,1)S(1)} %get-tuple-element.62), channel_id=1, source_target_pairs={{16,32},{48,64},{80,96},{32,16},{64,48},{96,80},{17,33},{49,65},{8... | collective-permute-start | bytes 1105928 | tf_op jit(solution)/shard_map/ppermute | solution.py:818
  125.1 12.6 %copy-start.1 = (bf16[59,80,128]{2,1,0:T(8,128)(2,1)S(1)}, bf16[59,80,128]{2,1,0:T(8,128)(2,1)}, u32[]{:S(2)}) copy-start(bf16[59,80,128]{2,1,0:T(8,128)(2,1)} %copy-done) | copy-start | bytes 3624964
  125.1 12.6 %copy-start.9 = (s32[3,8,32,128]{3,2,1,0:T(8,128)S(1)}, s32[3,8,32,128]{3,2,1,0:T(8,128)}, u32[]{:S(2)}) copy-start(s32[3,8,32,128]{3,2,1,0:T(8,128)} %masks.5) | copy-start | bytes 1179652
  125.1 12.6 %copy-start.16 = (f32[8,32,128]{2,1,0:T(8,128)S(1)}, f32[8,32,128]{2,1,0:T(8,128)}, u32[]{:S(2)}) copy-start(f32[8,32,128]{2,1,0:T(8,128)} %absorb.9) | copy-start | bytes 393220
  137.7 5.2 %copy-start.19 = (bf16[25,4,16,128]{3,2,1,0:T(8,128)(2,1)S(1)}, bf16[25,4,16,128]{3,2,1,0:T(8,128)(2,1)}, u32[]{:S(2)}) copy-start(bf16[25,4,16,128]{3,2,1,0:T(8,128)(2,1)} %copy-done.17) | copy-start | bytes 1228804
  142.9 1.8 %copy-start.25 = (f32[256,128]{1,0:T(8,128)S(1)}, f32[256,128]{1,0:T(8,128)}, u32[]{:S(2)}) copy-start(f32[256,128]{1,0:T(8,128)} %copy-done.23) | copy-start | bytes 393220
  144.7 18.6 %copy-start.20 = (f32[12,8,32,128]{3,2,1,0:T(8,128)S(1)}, f32[12,8,32,128]{3,2,1,0:T(8,128)}, u32[]{:S(2)}) copy-start(f32[12,8,32,128]{3,2,1,0:T(8,128)} %get-tuple-element.75.dir1) | copy-start | bytes 4718596

commit v4 on v3

--- a/solution.py
+++ b/solution.py
@@ -88,7 +88,7 @@
 
 
 def first_kernel(
-    src_far, masks_far, absorb_far, plane_far, depth_far, blocks_far, y0b_far, pe, in_far, out_far,
+    src_far, masks_far, absorb_far, plane_far, depth_far, blocks_far, y0b_far, pe, in_far, out_far, y0_far,
     src, masks, absorb, plane, depth, blocks, y0b, inner, outer, rows, y0, sems,
 ):
     copies = []
@@ -137,9 +137,13 @@
         re, im = src[2 * f], src[2 * f + 1]
         y0[f : f + 1, :] = restrict_rows(re, im, pe[...], rows[...])
         put(refs, (f, FIELDS + f), edges(re, im))
-    y0b[...] = jnp.broadcast_to(y0[...][None], y0b.shape)
-    results = [pltpu.make_async_copy(y0b, y0b_far, sems.at[FIELDS + 5])]
+    y0b[...] = jnp.broadcast_to(y0[...].astype(BF16)[None], y0b.shape)
+    results = [
+        pltpu.make_async_copy(y0b, y0b_far, sems.at[FIELDS + 5]),
+        pltpu.make_async_copy(y0, y0_far, sems.at[FIELDS + 8]),
+    ]
     results[0].start()
+    results[1].start()
     copies[FIELDS].wait()
     copies[FIELDS + 1].wait()
     put(refs, (12,), edges(masks[0].astype(F32), masks[1].astype(F32)))
@@ -154,8 +158,8 @@
             ref[15 + 2 * j : 17 + 2 * j] = blocks[j].reshape(2, 4, 16, 128)
     results.append(pltpu.make_async_copy(inner, in_far, sems.at[FIELDS + 6]))
     results.append(pltpu.make_async_copy(outer, out_far, sems.at[FIELDS + 7]))
-    results[1].start()
     results[2].start()
+    results[3].start()
     for copy in results:
         copy.wait()
 
@@ -192,8 +196,10 @@
     return pl.pallas_call(
         first_kernel,
         in_specs=[anywhere()] * 6,
-        out_specs=[anywhere(), whole(), anywhere(), anywhere()],
-        out_shape=[far_shape(TILES, 8, 128), shape(CELLS, 128), far_shape(*EDGES, dtype=BF16), far_shape(*EDGES, dtype=BF16)],
+        out_specs=[anywhere(), whole()] + [anywhere()] * 3,
+        out_shape=[far_shape(TILES, 8, 128, dtype=BF16), shape(CELLS, 128)]
+        + [far_shape(*EDGES, dtype=BF16)] * 2
+        + [far_shape(8, 128)],
         scratch_shapes=[
             pltpu.VMEM((12, TX, TY, NZ), F32),
             pltpu.VMEM((3, TX, TY, NZ), jnp.int32),
@@ -201,12 +207,12 @@
             pltpu.VMEM((8, TX, TY), F32),
             pltpu.VMEM((8, NZ), F32),
             pltpu.VMEM((NNZ, 128, 128), BF16),
-            pltpu.VMEM((TILES, 8, 128), F32),
+            pltpu.VMEM((TILES, 8, 128), BF16),
             pltpu.VMEM(EDGES, BF16),
             pltpu.VMEM(EDGES, BF16),
             pltpu.VMEM((256, 256), BF16),
             pltpu.VMEM((8, 128), F32),
-            pltpu.SemaphoreType.DMA((FIELDS + 8,)),
+            pltpu.SemaphoreType.DMA((FIELDS + 9,)),
         ],
         compiler_params=params(),
         name="first",
@@ -450,32 +456,32 @@
     return pl.BlockSpec(memory_space=pltpu.SMEM)
 
 
-def tile_sweep_kernel(index, every, blocks, out):
+def tile_sweep_kernel(index, every, y0, blocks, out):
     p, q = own_place()
-    y = every[p * GY + q] - sweep(index, p, q, blocks, lambda t: every[t].astype(BF16))
+    y = y0[...] - sweep(index, p, q, blocks, lambda t: every[t])
     out[...] = jnp.broadcast_to(y.astype(BF16)[None], out.shape)
 
 
-def tile_sweep(index, every, blocks):
+def tile_sweep(index, every, y0, blocks):
     return pl.pallas_call(
         tile_sweep_kernel,
-        in_specs=[smem()] + [whole()] * 2,
+        in_specs=[smem()] + [whole()] * 3,
         out_specs=whole(),
         out_shape=shape(TILES, 8, 128, dtype=BF16),
         compiler_params=params(),
         name="tile_sweep",
-    )(index, every, blocks)
+    )(index, every, y0, blocks)
 
 
 def column_place(t):
     return (t % GY) * GX + t // GY
 
 
-def column_sweep(index, y0, chosen, rows, out):
+def column_sweep(index, own, y0, chosen, rows, out):
     p, q = own_place()
     for i in range(GX):
         a = ((p // 2 + GX // 2 - i // 2) % (GX // 2)) * 2 + (p % 2 + i % 2) % 2
-        y = y0[a * GY + q] - sweep(index, a, q, rows(i), chosen)
+        y = (own if i == 0 else y0[a * GY + q].astype(F32)) - sweep(index, a, q, rows(i), chosen)
         out[:, a] = jnp.broadcast_to(y.astype(BF16)[None], (GY, 8, 128))
 
 
@@ -484,23 +490,23 @@
     return [rows[128 * j : 128 * j + 128] for j in range(NNZ)]
 
 
-def first_column_kernel(index, every, y0, b0, b1, b2, b3, by_core, out):
+def first_column_kernel(index, every, y0, y0_own, b0, b1, b2, b3, by_core, out):
     own = (b0, b1, b2, b3)
     theirs = by_core.at[27:59]
     column_sweep(
-        index, y0, lambda t: every[t], lambda i: packed_blocks(theirs, i // 2) if i % 2 else own[i // 2], out
+        index, y0_own[...], y0, lambda t: every[t], lambda i: packed_blocks(theirs, i // 2) if i % 2 else own[i // 2], out
     )
 
 
-def first_column(index, every, y0, rows, by_core):
+def first_column(index, every, y0, y0_own, rows, by_core):
     return pl.pallas_call(
         first_column_kernel,
-        in_specs=[smem()] + [whole()] * 7,
+        in_specs=[smem()] + [whole()] * 8,
         out_specs=whole(),
         out_shape=shape(GY, GX, 8, 128, dtype=BF16),
         compiler_params=params(),
         name="column_sweep",
-    )(index, every, y0, *rows, by_core)
+    )(index, every, y0, y0_own, *rows, by_core)
 
 
 def column_rows(own, theirs):
@@ -508,7 +514,8 @@
 
 
 def column_sweep_kernel(index, every, y0, own, theirs, out):
-    column_sweep(index, y0, lambda t: every[column_place(t)], column_rows(own, theirs), out)
+    p, q = own_place()
+    column_sweep(index, y0[p * GY + q], y0, lambda t: every[column_place(t)], column_rows(own, theirs), out)
 
 
 def column_call(index, every, y0, own, theirs):
@@ -527,16 +534,16 @@
     return [rows[128 * j : 128 * j + 128] for j in range(NNZ)]
 
 
-def last_sweep_kernel(index, every, y0, own, theirs, inner, outer, out):
+def last_sweep_kernel(index, every, y0, y0_own, own, theirs, inner, outer, out):
     p, q = own_place()
     take = lambda t: every[column_place(t)]
     pw, pe = jnp.maximum(p - 1, 0), jnp.minimum(p + 1, GX - 1)
     ql, qr = jnp.maximum(q - 1, 0), jnp.minimum(q + 1, GY - 1)
 
     def put(i, a, b, rows):
-        out[i] = y0[a * GY + b] - sweep(index, a, b, rows, take)
-
-    put(0, p, q, own)
+        out[i] = y0[a * GY + b].astype(F32) - sweep(index, a, b, rows, take)
+
+    out[0] = y0_own - sweep(index, p, q, own, take)
 
     @pl.when(q % 2 == 0)
     def _():
@@ -559,23 +566,24 @@
         put(2, pe, q, packed_blocks(theirs, 3))
 
 
-def first_last_kernel(index, every, y0, own, by_core, inner, outer, out):
-    last_sweep_kernel(index, every, y0, own, by_core.at[27:59], inner, outer, out)
+def first_last_kernel(index, every, y0, own, by_core, inner, outer, y0_own, out):
+    last_sweep_kernel(index, every, y0, y0_own[...], own, by_core.at[27:59], inner, outer, out)
 
 
 def later_last_kernel(index, every, y0, own, theirs, inner, outer, out):
-    last_sweep_kernel(index, every, y0, own.at[0], theirs, inner, outer, out)
-
-
-def last_sweep(kernel, index, every, y0, own, theirs, inner, outer):
+    p, q = own_place()
+    last_sweep_kernel(index, every, y0, y0[p * GY + q], own.at[0], theirs, inner, outer, out)
+
+
+def last_sweep(kernel, index, every, y0, own, theirs, inner, outer, *more):
     return pl.pallas_call(
         kernel,
-        in_specs=[smem()] + [whole()] * 6,
+        in_specs=[smem()] + [whole()] * (6 + len(more)),
         out_specs=whole(),
         out_shape=shape(5, 8, 128),
         compiler_params=params(),
         name="last_sweep",
-    )(index, every, y0, own, theirs, inner, outer)
+    )(index, every, y0, own, theirs, inner, outer, *more)
 
 
 def alphas(total):
@@ -591,10 +599,13 @@
     return are, aim
 
 
-def restart_kernel(index, every, before, b0, b1, b2, b3, by_core, out, y0, alpha, own, theirs, sems):
+def restart_kernel(
+    index, every, before, y0_far, b0, b1, b2, b3, by_core, out, y0, alpha, own, theirs, mine, sems
+):
     copies = [pltpu.make_async_copy(rows, own.at[k], sems.at[k]) for k, rows in enumerate((b0, b1, b2, b3))]
     copies.append(pltpu.make_async_copy(by_core.at[27:59], theirs, sems.at[4]))
-    for copy in copies:
+    copies.append(pltpu.make_async_copy(y0_far, mine, sems.at[5]))
+    for copy in copies[::-1]:
         copy.start()
     are, aim = alphas(jnp.sum(every[...], axis=0)[6:7])
     alpha[:8] = are
@@ -603,20 +614,26 @@
     are = jnp.where(sub < FIELDS, are, 0.0)
     aim = jnp.where(sub < FIELDS, jnp.where(lane < 64, -aim, aim), 0.0)
 
+    def next_coarse(y, part):
+        change = y - part
+        return y - (are * change + aim * pltpu.roll(change, 64, 1))
+
     def coarse(t, _):
-        part = every[t]
-        y0[t] = before[t] - (are * part + aim * pltpu.roll(part, 64, 1))
+        y0[t] = next_coarse(before[t].astype(F32), every[t])
 
     lax.fori_loop(0, TILES, coarse, None, unroll=8)
     for copy in copies:
         copy.wait()
-    column_sweep(index, y0, lambda t: y0[t].astype(BF16), column_rows(own, theirs), out)
-
-
-def restart(index, every, before, rows, by_core):
+    p, q = own_place()
+    exact = next_coarse(mine[...], every[p * GY + q])
+    y0[p * GY + q] = exact
+    column_sweep(index, exact, y0, lambda t: y0[t].astype(BF16), column_rows(own, theirs), out)
+
+
+def restart(index, every, before, y0_own, rows, by_core):
     return pl.pallas_call(
         restart_kernel,
-        in_specs=[smem()] + [whole()] * 2 + [anywhere()] * 5,
+        in_specs=[smem()] + [whole()] * 2 + [anywhere()] * 6,
         out_specs=[whole()] * 5,
         out_shape=[
             shape(GY, GX, 8, 128, dtype=BF16),
@@ -625,141 +642,128 @@
             shape(4, NNZ, 128, 128, dtype=BF16),
             shape(32, SLAB, 128, dtype=BF16),
         ],
-        scratch_shapes=[pltpu.SemaphoreType.DMA((5,))],
+        scratch_shapes=[pltpu.VMEM((8, 128), F32), pltpu.SemaphoreType.DMA((6,))],
         compiler_params=params(),
         name="restart",
-    )(index, every, before, *[far(row) for row in rows], far(by_core))
-
-
-def image_kernel(last, ys, pe, elow, ehigh, eleft, eright, depth, masks, absorb, res, local, part,
-                 *refs):
+    )(index, every, before, far(y0_own), *[far(row) for row in rows], far(by_core))
+
+
+def image_kernel(last, ys, pe, elow, ehigh, by_core, by_chip, depth, masks, absorb, res, local, part, *refs):
     if last:
-        direction, image, pay, mats, rows, edge, sides, acc = refs
+        direction, image, pay, mats, rows, edge, acc = refs
     else:
-        direction, image, pay_far, in_far, out_far, mats, rows, edge, sides, acc, pay, inner, outer, sems = refs
-    f = pl.program_id(0)
-
-    def sent(i):
-        two = pl.ds(2 * i, 2)
-        return (
-            pltpu.make_async_copy(inner.at[two], in_far.at[two], sems.at[i]),
-            pltpu.make_async_copy(outer.at[two], out_far.at[two], sems.at[FIELDS + i]),
-        )
+        (dir_far, img_far, pay_far, in_far, out_far, mats, rows, edge, acc,
+         direction, image, pay, inner, outer, sems) = refs
+
+    def sent(f):
+        two = pl.ds(2 * f, 2)
+        pairs = ((inner, in_far), (outer, out_far), (direction, dir_far), (image, img_far))
+        return [pltpu.make_async_copy(a.at[two], b.at[two], sems.at[4 * f + i]) for i, (a, b) in enumerate(pairs)]
 
     sub8 = iota((8, NZ), 0)
-
-    @pl.when(f == 0)
-    def _():
-        d = depth[...]
-        lane = iota((8, NZ), 1)
-        beside = jnp.where(lane == 0, 0.0, pltpu.roll(d, 1, 1))
-        beside = beside + jnp.where(lane == NZ - 1, 0.0, pltpu.roll(d, NZ - 1, 1))
-        hi, lo = split(depth_matrix(d))
-        nhi, nlo = split(depth_matrix(beside))
-        mats[0] = jnp.concatenate([hi, hi], axis=0)
-        mats[1] = jnp.concatenate([nhi, nhi], axis=0)
-        mats[2] = jnp.concatenate([lo, nlo], axis=0)
-        rows[...] = jnp.concatenate([hi, lo], axis=0)
-        acc[...] = jnp.zeros_like(acc)
-        by_core, by_chip = [s[0, :TY].astype(F32) + s[0, TY : 2 * TY].astype(F32) for s in (eleft, eright)]
-        sides[0] = jnp.where(own_core() == 0, by_chip, by_core)
-        sides[1] = jnp.where(own_core() == 0, by_core, by_chip)
-        for x in range(TX):
-            low = jnp.broadcast_to(ehigh[0, 0, x : x + 1, :], (8, 128))
-            high = jnp.broadcast_to(elow[0, 0, x : x + 1, :], (8, 128))
-            edge[0, x] = jnp.where(sub8 == 0, low, 0.0)
-            edge[1, x] = jnp.where(sub8 == 7, high, 0.0)
-
-    row = pl.ds(f, 1)
-    one = pe[...] * ys[0, row, :]
-    three = one.reshape(TX, TY, 128)
-    west = (sides[0] * ys[1, row, :])[None]
-    east = (sides[1] * ys[2, row, :])[None]
-    sub = iota((TX, TY, 128), 1)
-    near = jnp.concatenate([west, three[:-1]], axis=0) + jnp.concatenate([three[1:], east], axis=0)
-    near = near + jnp.where(sub == 0, 0.0, pltpu.roll(three, 1, 1))
-    near = near + jnp.where(sub == TY - 1, 0.0, pltpu.roll(three, TY - 1, 1))
-    first_rows = near[:, :8] + edge[0] * ys[3, row, :]
-    last_rows = near[:, TY - 8 :] + edge[1] * ys[4, row, :]
-    near = jnp.concatenate([first_rows, near[:, 8 : TY - 8], last_rows], axis=1).reshape(CELLS, 128)
-    ohi, olo = split(one)
-    nhi, nlo = split(near)
-    o = jnp.concatenate([ohi, olo], axis=1)
-    n = jnp.concatenate([nhi, nlo], axis=1)
-    fine = mm(o, mats[0]) + mm(ohi, mats[2, :128])
-    beside = mm(n, mats[0]) + mm(o, mats[1]) + mm(jnp.concatenate([nhi, ohi], axis=1), mats[2])
-    cre, cim = fine[:, :NZ].reshape(TX, TY, NZ), fine[:, NZ:].reshape(TX, TY, NZ)
-    bre, bim = beside[:, :NZ].reshape(TX, TY, NZ), beside[:, NZ:].reshape(TX, TY, NZ)
-    direction[0] = local[0] + cre
-    direction[1] = local[1] + cim
-    dre = 5.5 - masks[0].astype(F32)
-    dim = absorb[...]
-    ire = part[0] + (dre * cre - dim * cim - bre)
-    iim = part[1] + (dre * cim + dim * cre - bim)
-    image[0] = ire
-    image[1] = iim
-    rre, rim = res[0], res[1]
+    d = depth[...]
+    lane = iota((8, NZ), 1)
+    beside = jnp.where(lane == 0, 0.0, pltpu.roll(d, 1, 1))
+    beside = beside + jnp.where(lane == NZ - 1, 0.0, pltpu.roll(d, NZ - 1, 1))
+    hi, lo = split(depth_matrix(d))
+    nhi, nlo = split(depth_matrix(beside))
+    mats[0] = jnp.concatenate([hi, hi], axis=0)
+    mats[1] = jnp.concatenate([nhi, nhi], axis=0)
+    mats[2] = jnp.concatenate([lo, nlo], axis=0)
+    rows[...] = jnp.concatenate([hi, lo], axis=0)
+    core_side, chip_side = [s[24, :TY].astype(F32) + s[24, TY : 2 * TY].astype(F32) for s in (by_core, by_chip)]
+    west_edge = jnp.where(own_core() == 0, chip_side, core_side)
+    east_edge = jnp.where(own_core() == 0, core_side, chip_side)
+    for x in range(TX):
+        low = jnp.broadcast_to(ehigh[16, 0, x : x + 1, :], (8, 128))
+        high = jnp.broadcast_to(elow[16, 0, x : x + 1, :], (8, 128))
+        edge[0, x] = jnp.where(sub8 == 0, low, 0.0)
+        edge[1, x] = jnp.where(sub8 == 7, high, 0.0)
 
     def total(v):
         return jnp.sum(jnp.sum(v, axis=(0, 1)).reshape(1, NZ), axis=1, keepdims=True)
 
     lane1 = iota((1, 128), 1)
-    dots = jnp.where(lane1 == f, total(ire * rre + iim * rim), 0.0)
-    dots = dots + jnp.where(lane1 == f + 8, total(ire * rim - iim * rre), 0.0)
-    dots = dots + jnp.where(lane1 == f + 16, total(ire * ire + iim * iim), 0.0)
-    acc[6:7, :] = acc[6:7, :] + dots
-    if not last:
-        acc[row, :] = restrict_rows(ire, iim, pe[...], rows[...])
-        for c, value in ((0, ire), (1, iim)):
-            inner[2 * f + c], outer[2 * f + c] = by_pairs(pack_low(value), pack_high(value))
-        for copy in sent(f):
-            copy.start()
-
-    @pl.when(f == FIELDS - 1)
-    def _():
-        if last:
-            pay[...] = jnp.broadcast_to(acc[6:7, :], pay.shape)
-        else:
-            pay[...] = jnp.broadcast_to(acc[...][None], pay.shape)
-            copy = pltpu.make_async_copy(pay, pay_far, sems.at[2 * FIELDS])
-            copy.start()
-            for i in range(FIELDS):
-                for other in sent(i):
-                    other.wait()
-            copy.wait()
-
-
-def image_call(last, ys, pe, dlow, dhigh, dleft, dright, depth, masks, absorb, res, local, part):
-    edge_y = channel(lambda f: 16, 4, 8, NZ)
-    edge_x = slab_of(lambda f: 8)
-    cells = fields(TX, TY, NZ)
-    pay = (TILES, 128) if last else (TILES, 8, 128)
-    out_specs = [cells, cells, fixed(*pay) if last else anywhere()]
-    scratch = []
-    out_shape = [(shape if last else far_shape)(12, TX, TY, NZ), shape(12, TX, TY, NZ), (shape if last else far_shape)(*pay)]
-    if not last:
-        out_specs += [anywhere()] * 2
+    dots = jnp.zeros((1, 128), F32)
+    for f in range(FIELDS):
+        a, b, row = 2 * f, 2 * f + 1, slice(f, f + 1)
+        one = pe[...] * ys[0, row, :]
+        three = one.reshape(TX, TY, 128)
+        west = (west_edge * ys[1, row, :])[None]
+        east = (east_edge * ys[2, row, :])[None]
+        sub = iota((TX, TY, 128), 1)
+        near = jnp.concatenate([west, three[:-1]], axis=0) + jnp.concatenate([three[1:], east], axis=0)
+        near = near + jnp.where(sub == 0, 0.0, pltpu.roll(three, 1, 1))
+        near = near + jnp.where(sub == TY - 1, 0.0, pltpu.roll(three, TY - 1, 1))
+        first_rows = near[:, :8] + edge[0] * ys[3, row, :]
+        last_rows = near[:, TY - 8 :] + edge[1] * ys[4, row, :]
+        near = jnp.concatenate([first_rows, near[:, 8 : TY - 8], last_rows], axis=1).reshape(CELLS, 128)
+        ohi, olo = split(one)
+        nhi, nlo = split(near)
+        o = jnp.concatenate([ohi, olo], axis=1)
+        n = jnp.concatenate([nhi, nlo], axis=1)
+        fine = mm(o, mats[0]) + mm(ohi, mats[2, :128])
+        beside = mm(n, mats[0]) + mm(o, mats[1]) + mm(jnp.concatenate([nhi, ohi], axis=1), mats[2])
+        cre, cim = fine[:, :NZ].reshape(TX, TY, NZ), fine[:, NZ:].reshape(TX, TY, NZ)
+        bre, bim = beside[:, :NZ].reshape(TX, TY, NZ), beside[:, NZ:].reshape(TX, TY, NZ)
+        direction[a] = local[a] + cre
+        direction[b] = local[b] + cim
+        dre = 5.5 - masks[f // 2].astype(F32)
+        dim = absorb[...]
+        ire = part[a] + (dre * cre - dim * cim - bre)
+        iim = part[b] + (dre * cim + dim * cre - bim)
+        image[a] = ire
+        image[b] = iim
+        rre, rim = res[a], res[b]
+        dots = dots + jnp.where(lane1 == f, total(ire * rre + iim * rim), 0.0)
+        dots = dots + jnp.where(lane1 == f + 8, total(ire * rim - iim * rre), 0.0)
+        dots = dots + jnp.where(lane1 == f + 16, total(ire * ire + iim * iim), 0.0)
+        if not last:
+            acc[row, :] = restrict_rows(rre - ire, rim - iim, pe[...], rows[...])
+            for ch, value in ((a, ire), (b, iim)):
+                inner[ch], outer[ch] = by_pairs(pack_low(value), pack_high(value))
+            for copy in sent(f):
+                copy.start()
+    if last:
+        pay[...] = jnp.broadcast_to(dots, pay.shape)
+    else:
+        acc[6:7, :] = dots
+        acc[7:8, :] = jnp.zeros((1, 128), F32)
+        pay[...] = jnp.broadcast_to(acc[...][None], pay.shape)
+        copy = pltpu.make_async_copy(pay, pay_far, sems.at[4 * FIELDS])
+        copy.start()
+        for f in range(FIELDS):
+            for other in sent(f):
+                other.wait()
+        copy.wait()
+
+
+def image_call(last, ys, pe, dlow, dhigh, by_core, by_chip, depth, masks, absorb, res, local, part):
+    cells = (12, TX, TY, NZ)
+    scratch = [
+        pltpu.VMEM((3, 256, 256), BF16),
+        pltpu.VMEM((256, 256), BF16),
+        pltpu.VMEM((2, TX, 8, 128), F32),
+        pltpu.VMEM((8, 128), F32),
+    ]
+    if last:
+        out_specs = [whole()] * 3
+        out_shape = [shape(*cells), shape(*cells), shape(TILES, 128)]
+    else:
+        out_specs = [anywhere()] * 5
+        out_shape = [far_shape(*cells), far_shape(*cells), far_shape(TILES, 8, 128)]
         out_shape += [far_shape(12, 4, 8, NZ)] * 2
-        scratch = [pltpu.VMEM(pay, F32)] + [pltpu.VMEM((12, 4, 8, NZ), F32)] * 2
-        scratch.append(pltpu.SemaphoreType.DMA((2 * FIELDS + 1,)))
+        scratch += [pltpu.VMEM(cells, F32)] * 2 + [pltpu.VMEM((TILES, 8, 128), F32)]
+        scratch += [pltpu.VMEM((12, 4, 8, NZ), F32)] * 2 + [pltpu.SemaphoreType.DMA((4 * FIELDS + 1,))]
     return pl.pallas_call(
         functools.partial(image_kernel, last),
-        grid=(FIELDS,),
-        in_specs=[fixed(5, 8, 128)]
-        + [fixed(CELLS, 128), edge_y, edge_y, edge_x, edge_x, fixed(8, NZ)]
-        + [channel(lambda f: f // 2, TX, TY, NZ), fixed(TX, TY, NZ), cells, cells, cells],
+        in_specs=[whole()] * 12,
         out_specs=out_specs,
         out_shape=out_shape,
-        scratch_shapes=[
-            pltpu.VMEM((3, 256, 256), BF16),
-            pltpu.VMEM((256, 256), BF16),
-            pltpu.VMEM((2, TX, 8, 128), F32),
-            pltpu.VMEM((2, TY, 128), F32),
-            pltpu.VMEM((8, 128), F32),
-        ] + scratch,
+        scratch_shapes=scratch,
         compiler_params=params(),
         name="image",
-    )(ys, pe, dlow, dhigh, dleft, dright, depth, masks, absorb, res, local, part)
+    )(ys, pe, dlow, dhigh, by_core, by_chip, depth, masks, absorb, res, local, part)
 
 
 def finish_kernel(every, alpha, dir1, dir2, res, img, solution, residual, two):
@@ -831,27 +835,27 @@
     blocks = coupling_blocks.reshape(NNZ, 128, 128)
     index = coupling_index.reshape(-1)
 
-    y0b, pe, inner, outer = first(src, masks, absorption, plane_basis, depth_basis, blocks)
+    y0b, pe, inner, outer, y0_own = first(src, masks, absorption, plane_basis, depth_basis, blocks)
     all0 = gather(y0b)
     inner0, outer0 = swap_pairs(inner), swap_between(outer)
     rows = [blocks] + [round_x(blocks, k) for k in (1, 2, 3)]
-    y1b = tile_sweep(index, all0, blocks)
-    all1 = gather(y1b)
-    for_core, for_chip, low0, high0 = slabs(src, masks, absorption, after(pe, y1b), inner0, outer0, rows)
+    y1b = tile_sweep(index, all0, y0_own, blocks)
+    all1 = gather(after(y1b, *rows))
+    for_core, for_chip, low0, high0 = slabs(src, masks, absorption, after(pe, all1), inner0, outer0, rows)
     core0, chip0 = swap_cores(for_core), swap_chips(for_chip)
-    y2b = first_column(index, after(all1, core0, chip0), all0, rows, core0)
+    y2b = first_column(index, all1, all0, y0_own, rows, core0)
     all2 = gather(y2b, "gy").reshape(TILES, 8, 128)
     local, part = local_solve(
         src, low0, high0, after(core0, all2), chip0, masks, absorption, low0, high0, core0, chip0
     )
-    ys = last_sweep(first_last_kernel, index, after(all2, part), all0, blocks, core0, inner0, outer0)
+    ys = last_sweep(first_last_kernel, index, after(all2, part), all0, blocks, core0, inner0, outer0, y0_own)
     dir1, img1, pay, inner, outer = image_call(
         False, ys, pe, low0, high0, core0, chip0, depth_basis, masks, absorption, src, local, part
     )
 
     all3 = gather(pay)
     inner1, outer1 = swap_pairs(inner), swap_between(outer)
-    y1b, y0, alpha, own, theirs = restart(index, all3, all0, rows, core0)
+    y1b, y0, alpha, own, theirs = restart(index, all3, all0, y0_own, rows, core0)
     all1 = gather(y1b, "gy").reshape(TILES, 8, 128)
     res, low, high, for_core, for_chip = update(src, img1, alpha, low0, high0, inner1, outer1)
     by_core, by_chip = swap_cores(for_core), swap_chips(for_chip)

time: 167 us -> 157 us (0.940)
  Pallas kernels: 40.5 us -> 36.6 us
  waiting for transfers between devices: 20.3 us -> 16.5 us
  blocking collectives: 68.8 us -> 67.1 us
    pallas_call x6, Pallas kernels: 15.4 us -> 11.5 us  [the longest x2 5.73 us: image_call(): pl.pallas_call(functools.partial(image_kernel, last), in_specs=[whole()]...]
    all_to_all x2, waiting for transfers between devices: 18.6 us -> 15.2 us  [gather(): return lax.all_to_all(copies, axes, 0, 0, tiled=True)]
    unnamed x57 -> x65, local copies, waits for them, and re-layouts: 3.53 us -> 3.46 us
  transfers between devices with their start and end apart: 13 -> 13, of which waited for: 3 -> 4; matrix products, arithmetic and copies ran while one was open for 0% -> 1% of each run, Pallas kernels for 2% -> 4%
where the time goes in v4:
time: 157 us
  blocking collectives  67.1 us (43%)
  Pallas kernels  36.6 us (23%)
  starting transfers between devices  30.8 us (20%)
  waiting for transfers between devices  16.5 us (11%)
  local copies, waits for them, and re-layouts  4.5 us (3%)
    all_to_all x5, blocking collectives, gather(): return lax.all_to_all(copies, axes, 0, 0, tiled=True)  67.1 us
    all_to_all x2, starting transfers between devices, gather(): return lax.all_to_all(copies, axes, 0, 0, tiled=True)  16.7 us
    all_to_all x2, waiting for transfers between devices, gather(): return lax.all_to_all(copies, axes, 0, 0, tiled=True)  15.2 us
    pallas_call x2, Pallas kernels, local_solve(): pl.pallas_call(local_kernel, grid=(FIELDS,), in_specs=[fields(TX, TY, NZ)...  10.3 us
    pallas_call x2, Pallas kernels, image_call(): pl.pallas_call(functools.partial(image_kernel, last), in_specs=[whole()]...  5.73 us
    pallas_call x1, Pallas kernels, first(): pl.pallas_call(first_kernel, in_specs=[anywhere()] * 6, out_specs=[anywhe...  4.53 us
    ppermute x2, starting transfers between devices, swap_chips(): return lax.ppermute(value, 'gx', ends + [(j, i) for i, j in ends])  4.42 us
    ppermute x3, starting transfers between devices, round_x(): return lax.ppermute(value, 'gx', [(i, (i + 2 * k) % GX) for i in range(GX)])  3.82 us
  transfers between devices with their start and end apart: 13, of which 4 were waited for; matrix products, arithmetic and copies ran while one was open for 1% of the time, Pallas kernels for 4%

profile of v4, /device:TPU:1, one launch (start us, length us, event | category | flops | bytes accessed | tf_op | source)
XLA Modules:
  0.0 156.7 jit_solution(13705443471727574056)
XLA Ops:
  0.6 0.0 copy-start.13
  0.7 0.0 copy-start.7
  0.7 0.0 copy-start.14
  0.7 4.5 %first.1 = (bf16[128,8,128]{2,1,0:T(8,128)(2,1)}, f32[256,128]{1,0:T(8,128)S(1)}, bf16[25,4,16,128]{3,2,1,0:T(8,128)(2,1)}, bf16[25,4,16,128]{3,2,1,0:T(8,128)(2,1)}, f32[8,128]{1,0:T(8,128)}) custom-call(f32[12,8,32,128]{3,2,1,0:T(8,128)} %bitcast.11, s32[3,8,32,128]{3,2,1,0:T(8,128)} %masks.5, f32[8,32,128]{2,1,0:T(8,128)} %absorb.9, ...), custom_call_target="tpu_custom_call" | custom-call | tf_op jit(solution)/shard_map/first/pallas_call | solution.py:196
  5.2 11.5 %all-to-all-start = ((bf16[128,8,128]{2,1,0:T(8,128)(2,1)}), bf16[128,8,128]{2,1,0:T(8,128)(2,1)S(1)}, u32[]{:S(2)}, u32[]{:S(2)}) async-start(bf16[128,8,128]{2,1,0:T(8,128)(2,1)} %get-tuple-element.42), calls=%async_computation | async-start | bytes 524288 | tf_op jit(solution)/shard_map/all_to_all | solution.py:813
  16.8 2.7 %collective-permute-start.2 = (bf16[5,128,128]{2,1,0:T(8,128)(2,1)S(1)}, bf16[5,128,128]{2,1,0:T(8,128)(2,1)}, u32[]{:S(2)}, u32[]{:S(2)}) collective-permute-start(bf16[5,128,128]{2,1,0:T(8,128)(2,1)S(1)} %bitcast.18), channel_id=1, source_target_pairs={{0,96},{16,112},{32,0},{48,16},{64,32},{80,48},{96,64},{112,80},{1... | collective-permute-start | bytes 491528 | tf_op jit(solution)/shard_map/ppermute | solution.py:826
  19.4 0.6 collective-permute-start.1
  20.0 0.6 collective-permute-start
  20.6 1.2 collective-permute-start.3
  21.8 0.7 collective-permute-start.4
  22.5 0.7 copy.10
  23.2 1.0 reshape.30.index
  24.2 3.9 %all-to-all-done.every.y0.before = bf16[128,8,128]{2,1,0:T(8,128)(2,1)S(1)} async-done(((bf16[128,8,128]{2,1,0:T(8,128)(2,1)}), bf16[128,8,128]{2,1,0:T(8,128)(2,1)S(1)}, u32[]{:S(2)}, u32[]{:S(2)}) %all-to-all-start) | async-done | bytes 262176 | tf_op jit(solution)/shard_map/all_to_all | solution.py:813
  28.2 0.7 copy-done.28
  28.9 0.8 tile_sweep.1
  29.7 0.0 collective-permute-done.1.b2
  29.7 1.0 collective-permute-done.b1
  30.7 18.8 %all_to_all.41.every = bf16[128,8,128]{2,1,0:T(8,128)(2,1)S(1)} all-to-all(bf16[128,8,128]{2,1,0:T(8,128)(2,1)S(1)} %tile_sweep.1), channel_id=1, replica_groups=mesh['gx'=8,'gy'=16] {'gx','gy'}, dimensions={0} | all-to-all | bytes 524288 | tf_op jit(solution)/shard_map/all_to_all | solution.py:813
  49.5 0.0 collective-permute-done.3.inner
  49.5 1.6 %slabs.1 = (bf16[59,80,128]{2,1,0:T(8,128)(2,1)S(1)}, bf16[27,80,128]{2,1,0:T(8,128)(2,1)S(1)}, f32[17,4,8,128]{3,2,1,0:T(8,128)S(1)}, f32[17,4,8,128]{3,2,1,0:T(8,128)S(1)}) custom-call(f32[12,8,32,128]{3,2,1,0:T(8,128)S(1)} %bitcast.12, s32[3,8,32,128]{3,2,1,0:T(8,128)S(1)} %copy-done.7, f32[8,32,128]{2,1,0:T(8,128)S(1)} %copy-done.14, ...), custom_call_target="tpu_custom_call" | custom-call | tf_op jit(solution)/shard_map/slabs/pallas_call | solution.py:296
  51.2 0.6 collective-permute-start.5
  51.8 2.3 %collective-permute-start.6 = (bf16[27,80,128]{2,1,0:T(8,128)(2,1)S(1)}, bf16[27,80,128]{2,1,0:T(8,128)(2,1)S(1)}, u32[]{:S(2)}, u32[]{:S(2)}) collective-permute-start(bf16[27,80,128]{2,1,0:T(8,128)(2,1)S(1)} %get-tuple-element.53), channel_id=1, source_target_pairs={{16,32},{48,64},{80,96},{32,16},{64,48},{96,80},{17,33},{49,65},{8... | collective-permute-start | bytes 1658888 | tf_op jit(solution)/shard_map/ppermute | solution.py:822
  54.1 0.2 collective-permute-done.5.by_core.left.mleft.aleft
  54.3 0.9 copy-done.11
  55.3 2.3 %column_sweep.2 = bf16[16,8,8,128]{3,2,1,0:T(8,128)(2,1)S(1)} custom-call(s32[640]{0:T(1024)S(1)} %reshape.30.index, bf16[128,8,128]{2,1,0:T(8,128)(2,1)S(1)} %all_to_all.41.every, bf16[128,8,128]{2,1,0:T(8,128)(2,1)S(1)} %copy-done.11, f32[8,128]{1,0:T(8,128)S(1)} %copy-done.29, bf16[5,128,128]{2,1,0:T(8,128)(2,1)S(1)} %bitcast.23, ...), custom_call_target="tpu_custom_call" | custom-call | tf_op jit(solution)/shard_map/column_sweep/pallas_call | solution.py:502
  57.6 10.9 %all_to_all.42 = bf16[16,8,8,128]{3,2,1,0:T(8,128)(2,1)S(1)} all-to-all(bf16[16,8,8,128]{3,2,1,0:T(8,128)(2,1)S(1)} %column_sweep.2), channel_id=1, replica_groups=mesh['gx'=8,'gy'=16] {'gy'}, dimensions={0} | all-to-all | bytes 524288 | tf_op jit(solution)/shard_map/all_to_all | solution.py:813
  68.6 5.2 %local.2 = (f32[12,8,32,128]{3,2,1,0:T(8,128)S(1)}, f32[12,8,32,128]{3,2,1,0:T(8,128)S(1)}) custom-call(f32[12,8,32,128]{3,2,1,0:T(8,128)S(1)} %bitcast.13, f32[17,4,8,128]{3,2,1,0:T(8,128)S(1)} %get-tuple-element.50.low.mlow.alow.elow.low0, f32[17,4,8,128]{3,2,1,0:T(8,128)S(1)} %get-tuple-element.51.high.mhigh.ahigh.ehigh.high0, ...), custom_call_target="tpu_custom_call" | custom-call | tf_op jit(solution)/shard_map/local/pallas_call | solution.py:425
  73.8 0.0 copy-start.30
  73.8 1.3 last_sweep.2.ys
  75.1 0.0 copy-done
  75.2 3.9 %image.2 = (f32[12,8,32,128]{3,2,1,0:T(8,128)}, f32[12,8,32,128]{3,2,1,0:T(8,128)}, f32[128,8,128]{2,1,0:T(8,128)}, f32[12,4,8,128]{3,2,1,0:T(8,128)}, f32[12,4,8,128]{3,2,1,0:T(8,128)}) custom-call(f32[5,8,128]{2,1,0:T(8,128)S(1)} %last_sweep.2.ys, f32[256,128]{1,0:T(8,128)S(1)} %copy-done.26, ...), custom_call_target="tpu_custom_call" | custom-call | tf_op jit(solution)/shard_map/image/pallas_call | solution.py:758
  79.1 5.2 %all-to-all-start.3 = ((f32[128,8,128]{2,1,0:T(8,128)}), f32[128,8,128]{2,1,0:T(8,128)S(1)}, u32[]{:S(2)}, u32[]{:S(2)}) async-start(f32[128,8,128]{2,1,0:T(8,128)} %get-tuple-element.57), calls=%async_computation.3 | async-start | bytes 1048576 | tf_op jit(solution)/shard_map/all_to_all | solution.py:813
  84.3 1.5 collective-permute-start.7
  85.8 1.3 collective-permute-start.8
  87.1 11.3 %all-to-all-done.3.every = f32[128,8,128]{2,1,0:T(8,128)S(1)} async-done(((f32[128,8,128]{2,1,0:T(8,128)}), f32[128,8,128]{2,1,0:T(8,128)S(1)}, u32[]{:S(2)}, u32[]{:S(2)}) %all-to-all-start.3) | async-done | bytes 524320 | tf_op jit(solution)/shard_map/all_to_all | solution.py:813
  98.4 0.9 copy-done.12
  99.3 3.0 %restart.1 = (bf16[16,8,8,128]{3,2,1,0:T(8,128)(2,1)S(1)}, f32[128,8,128]{2,1,0:T(8,128)S(1)}, f32[16,128]{1,0:T(8,128)S(1)}, bf16[4,5,128,128]{3,2,1,0:T(8,128)(2,1)S(1)}, bf16[32,80,128]{2,1,0:T(8,128)(2,1)S(1)}) custom-call(s32[640]{0:T(1024)S(1)} %reshape.30.index, f32[128,8,128]{2,1,0:T(8,128)S(1)} %all-to-all-done.3.every, ...), custom_call_target="tpu_custom_call" | custom-call | tf_op jit(solution)/shard_map/restart/pallas_call | solution.py:634
  102.4 1.5 update.1
  103.8 0.7 collective-permute-start.9
  104.5 2.1 %collective-permute-start.10 = (bf16[18,80,128]{2,1,0:T(8,128)(2,1)S(1)}, bf16[18,80,128]{2,1,0:T(8,128)(2,1)S(1)}, u32[]{:S(2)}, u32[]{:S(2)}) collective-permute-start(bf16[18,80,128]{2,1,0:T(8,128)(2,1)S(1)} %get-tuple-element.64), channel_id=1, source_target_pairs={{16,32},{48,64},{80,96},{32,16},{64,48},{96,80},{17,33},{49,65},{8... | collective-permute-start | bytes 1105928 | tf_op jit(solution)/shard_map/ppermute | solution.py:822
  106.7 10.8 %all_to_all.43 = bf16[16,8,8,128]{3,2,1,0:T(8,128)(2,1)S(1)} all-to-all(bf16[16,8,8,128]{3,2,1,0:T(8,128)(2,1)S(1)} %get-tuple-element.58), channel_id=1, replica_groups=mesh['gx'=8,'gy'=16] {'gy'}, dimensions={0} | all-to-all | bytes 524288 | tf_op jit(solution)/shard_map/all_to_all | solution.py:813
  117.5 1.4 column_sweep.3
  118.9 11.1 %all_to_all.44 = bf16[16,8,8,128]{3,2,1,0:T(8,128)(2,1)S(1)} all-to-all(bf16[16,8,8,128]{3,2,1,0:T(8,128)(2,1)S(1)} %column_sweep.3), channel_id=1, replica_groups=mesh['gx'=8,'gy'=16] {'gy'}, dimensions={0} | all-to-all | bytes 524288 | tf_op jit(solution)/shard_map/all_to_all | solution.py:813
  130.0 5.1 %local.3 = (f32[12,8,32,128]{3,2,1,0:T(8,128)S(1)}, f32[12,8,32,128]{3,2,1,0:T(8,128)S(1)}) custom-call(f32[12,8,32,128]{3,2,1,0:T(8,128)S(1)} %get-tuple-element.69.src.res, f32[12,4,8,128]{3,2,1,0:T(8,128)S(1)} %get-tuple-element.70.low, f32[12,4,8,128]{3,2,1,0:T(8,128)S(1)} %get-tuple-element.71.high, ...), custom_call_target="tpu_custom_call" | custom-call | tf_op jit(solution)/shard_map/local/pallas_call | solution.py:425
  135.2 1.3 last_sweep.3.ys
  136.5 1.8 %image.3 = (f32[12,8,32,128]{3,2,1,0:T(8,128)S(1)}, f32[12,8,32,128]{3,2,1,0:T(8,128)S(1)}, f32[128,128]{1,0:T(8,128)S(1)}) custom-call(f32[5,8,128]{2,1,0:T(8,128)S(1)} %last_sweep.3.ys, f32[256,128]{1,0:T(8,128)S(1)} %copy-done.27, f32[17,4,8,128]{3,2,1,0:T(8,128)S(1)} %copy-done.4, f32[17,4,8,128]{3,2,1,0:T(8,128)S(1)} %copy-done.6, ...), custom_call_target="tpu_custom_call" | custom-call | tf_op jit(solution)/shard_map/image/pallas_call | solution.py:758
  138.3 15.6 %all_to_all.45 = f32[128,1,128]{2,1,0:T(1,128)S(1)} all-to-all(f32[128,1,128]{2,1,0:T(1,128)S(1)} %bitcast.29), channel_id=1, replica_groups=mesh['gx'=8,'gy'=16] {'gx','gy'}, dimensions={0} | all-to-all | bytes 131072 | tf_op jit(solution)/shard_map/all_to_all | solution.py:813
  153.8 2.9 %finish.1 = (f32[12,8,32,128]{3,2,1,0:T(8,128)}, f32[12,8,32,128]{3,2,1,0:T(8,128)}) custom-call(f32[128,128]{1,0:T(8,128)S(1)} %bitcast.28, f32[16,128]{1,0:T(8,128)S(1)} %get-tuple-element.60.alpha, f32[12,8,32,128]{3,2,1,0:T(8,128)S(1)} %copy-done.23, f32[12,8,32,128]{3,2,1,0:T(8,128)S(1)} %get-tuple-element.78.dir2, ...), custom_call_target="tpu_custom_call" | custom-call | tf_op jit(solution)/shard_map/finish/pallas_call | solution.py:791
  (63 shorter events, 0.1 us)
Async XLA Ops:
  0.6 16.1 %copy-start.13 = (bf16[1,1,5,128,128]{4,3,2,1,0:T(8,128)(2,1)S(1)}, bf16[1,1,5,128,128]{4,3,2,1,0:T(8,128)(2,1)}, u32[]{:S(2)}) copy-start(bf16[1,1,5,128,128]{4,3,2,1,0:T(8,128)(2,1)} %param.12) | copy-start | bytes 491524
  0.6 21.8 %copy-start.31 = (s32[8,16,5]{1,0,2:T(8,128)S(1)}, s32[8,16,5]{1,0,2:T(8,128)}, u32[]{:S(2)}) copy-start(s32[8,16,5]{1,0,2:T(8,128)} %param.13) | copy-start | bytes 7684
  0.7 48.8 %copy-start.2 = (f32[3,2,2,8,32,128]{5,4,3,2,1,0:T(8,128)S(1)}, f32[3,2,2,8,32,128]{5,4,3,2,1,0:T(8,128)}, u32[]{:S(2)}) copy-start(f32[3,2,2,8,32,128]{5,4,3,2,1,0:T(8,128)} %param.7) | copy-start | bytes 4718596
  0.7 48.8 %copy-start.7 = (s32[3,8,32,128]{3,2,1,0:T(8,128)S(1)}, s32[3,8,32,128]{3,2,1,0:T(8,128)}, u32[]{:S(2)}) copy-start(s32[3,8,32,128]{3,2,1,0:T(8,128)} %masks.5) | copy-start | bytes 1179652
  0.7 48.8 %copy-start.14 = (f32[8,32,128]{2,1,0:T(8,128)S(1)}, f32[8,32,128]{2,1,0:T(8,128)}, u32[]{:S(2)}) copy-start(f32[8,32,128]{2,1,0:T(8,128)} %absorb.9) | copy-start | bytes 393220
  5.2 45.9 %copy-start.25 = (f32[256,128]{1,0:T(8,128)}, f32[256,128]{1,0:T(8,128)S(1)}, u32[]{:S(2)}) copy-start(f32[256,128]{1,0:T(8,128)S(1)} %get-tuple-element.46.pe) | copy-start | bytes 393220
  5.2 23.0 %all-to-all-start = ((bf16[128,8,128]{2,1,0:T(8,128)(2,1)}), bf16[128,8,128]{2,1,0:T(8,128)(2,1)S(1)}, u32[]{:S(2)}, u32[]{:S(2)}) async-start(bf16[128,8,128]{2,1,0:T(8,128)(2,1)} %get-tuple-element.42), calls=%async_computation | async-start | bytes 524288 | tf_op jit(solution)/shard_map/all_to_all | solution.py:813
  16.8 12.9 %collective-permute-start.2 = (bf16[5,128,128]{2,1,0:T(8,128)(2,1)S(1)}, bf16[5,128,128]{2,1,0:T(8,128)(2,1)}, u32[]{:S(2)}, u32[]{:S(2)}) collective-permute-start(bf16[5,128,128]{2,1,0:T(8,128)(2,1)S(1)} %bitcast.18), channel_id=1, source_target_pairs={{0,96},{16,112},{32,0},{48,16},{64,32},{80,48},{96,64},{112,80},{1... | collective-permute-start | bytes 491528 | tf_op jit(solution)/shard_map/ppermute | solution.py:826
  19.4 10.3 %collective-permute-start.1 = (bf16[5,128,128]{2,1,0:T(8,128)(2,1)S(1)}, bf16[5,128,128]{2,1,0:T(8,128)(2,1)}, u32[]{:S(2)}, u32[]{:S(2)}) collective-permute-start(bf16[5,128,128]{2,1,0:T(8,128)(2,1)S(1)} %bitcast.19), channel_id=1, source_target_pairs={{0,64},{16,80},{32,96},{48,112},{64,0},{80,16},{96,32},{112,48},{1... | collective-permute-start | bytes 491528 | tf_op jit(solution)/shard_map/ppermute | solution.py:826
  20.0 10.7 %collective-permute-start = (bf16[5,128,128]{2,1,0:T(8,128)(2,1)S(1)}, bf16[5,128,128]{2,1,0:T(8,128)(2,1)}, u32[]{:S(2)}, u32[]{:S(2)}) collective-permute-start(bf16[5,128,128]{2,1,0:T(8,128)(2,1)S(1)} %bitcast.20), channel_id=1, source_target_pairs={{0,32},{16,48},{32,64},{48,80},{64,96},{80,112},{96,0},{112,16},{1... | collective-permute-start | bytes 491528 | tf_op jit(solution)/shard_map/ppermute | solution.py:826
  20.6 28.9 %collective-permute-start.3 = (bf16[25,4,16,128]{3,2,1,0:T(8,128)(2,1)}, bf16[25,4,16,128]{3,2,1,0:T(8,128)(2,1)S(1)}, u32[]{:S(2)}, u32[]{:S(2)}) collective-permute-start(bf16[25,4,16,128]{3,2,1,0:T(8,128)(2,1)} %get-tuple-element.47), channel_id=1, source_target_pairs={{0,1},{1,0},{2,3},{3,2},{4,5},{5,4},{6,7},{7,6},{8,9},{9,8},{10,11... | collective-permute-start | bytes 1228808 | tf_op jit(solution)/shard_map/ppermute | solution.py:804
  21.8 27.7 %collective-permute-start.4 = (bf16[25,4,16,128]{3,2,1,0:T(8,128)(2,1)}, bf16[25,4,16,128]{3,2,1,0:T(8,128)(2,1)S(1)}, u32[]{:S(2)}, u32[]{:S(2)}) collective-permute-start(bf16[25,4,16,128]{3,2,1,0:T(8,128)(2,1)} %get-tuple-element.48), channel_id=1, source_target_pairs={{1,2},{3,4},{5,6},{7,8},{9,10},{11,12},{13,14},{2,1},{4,3},{6,5},{... | collective-permute-start | bytes 1228808 | tf_op jit(solution)/shard_map/ppermute | solution.py:809
  28.2 23.0 %copy-start.10 = (bf16[128,8,128]{2,1,0:T(8,128)(2,1)}, bf16[128,8,128]{2,1,0:T(8,128)(2,1)S(1)}, u32[]{:S(2)}) copy-start(bf16[128,8,128]{2,1,0:T(8,128)(2,1)S(1)} %all-to-all-done.every.y0.before) | copy-start | bytes 786436
  28.2 0.7 copy-start.28
  49.5 4.8 %copy-start.29 = (f32[8,128]{1,0:T(8,128)S(1)}, f32[8,128]{1,0:T(8,128)}, u32[]{:S(2)}) copy-start(f32[8,128]{1,0:T(8,128)} %get-tuple-element.43.y0.y0_own.y0_far) | copy-start | bytes 12292
  49.5 1.7 %copy-start.17 = (bf16[25,4,16,128]{3,2,1,0:T(8,128)(2,1)}, bf16[25,4,16,128]{3,2,1,0:T(8,128)(2,1)S(1)}, u32[]{:S(2)}) copy-start(bf16[25,4,16,128]{3,2,1,0:T(8,128)(2,1)S(1)} %collective-permute-done.3.inner) | copy-start | bytes 1228804
  49.5 1.6 %copy-start.20 = (bf16[25,4,16,128]{3,2,1,0:T(8,128)(2,1)}, bf16[25,4,16,128]{3,2,1,0:T(8,128)(2,1)S(1)}, u32[]{:S(2)}) copy-start(bf16[25,4,16,128]{3,2,1,0:T(8,128)(2,1)S(1)} %collective-permute-done.4.outer) | copy-start | bytes 1228804
  51.2 24.0 %copy-start.3 = (f32[17,4,8,128]{3,2,1,0:T(8,128)}, f32[17,4,8,128]{3,2,1,0:T(8,128)S(1)}, u32[]{:S(2)}) copy-start(f32[17,4,8,128]{3,2,1,0:T(8,128)S(1)} %get-tuple-element.50.low.mlow.alow.elow.low0) | copy-start | bytes 835588
  51.2 23.9 %copy-start.5 = (f32[17,4,8,128]{3,2,1,0:T(8,128)}, f32[17,4,8,128]{3,2,1,0:T(8,128)S(1)}, u32[]{:S(2)}) copy-start(f32[17,4,8,128]{3,2,1,0:T(8,128)S(1)} %get-tuple-element.51.high.mhigh.ahigh.ehigh.high0) | copy-start | bytes 835588
  51.2 3.1 %collective-permute-start.5 = (bf16[59,80,128]{2,1,0:T(8,128)(2,1)S(1)}, bf16[59,80,128]{2,1,0:T(8,128)(2,1)S(1)}, u32[]{:S(2)}, u32[]{:S(2)}) collective-permute-start(bf16[59,80,128]{2,1,0:T(8,128)(2,1)S(1)} %get-tuple-element.49), channel_id=1, source_target_pairs={{0,16},{16,0},{32,48},{48,32},{64,80},{80,64},{96,112},{112,96},{1... | collective-permute-start | bytes 3624968 | tf_op jit(solution)/shard_map/ppermute | solution.py:817
  51.8 16.8 %copy-start.8 = (s32[3,8,32,128]{3,2,1,0:T(8,128)S(1)}, s32[3,8,32,128]{3,2,1,0:T(8,128)}, u32[]{:S(2)}) copy-start(s32[3,8,32,128]{3,2,1,0:T(8,128)} %masks.5) | copy-start | bytes 1179652
  51.8 16.8 %collective-permute-start.6 = (bf16[27,80,128]{2,1,0:T(8,128)(2,1)S(1)}, bf16[27,80,128]{2,1,0:T(8,128)(2,1)S(1)}, u32[]{:S(2)}, u32[]{:S(2)}) collective-permute-start(bf16[27,80,128]{2,1,0:T(8,128)(2,1)S(1)} %get-tuple-element.53), channel_id=1, source_target_pairs={{16,32},{48,64},{80,96},{32,16},{64,48},{96,80},{17,33},{49,65},{8... | collective-permute-start | bytes 1658888 | tf_op jit(solution)/shard_map/ppermute | solution.py:822
  54.3 1.0 copy-start.11
  55.3 19.9 %copy-start = (bf16[59,80,128]{2,1,0:T(8,128)(2,1)}, bf16[59,80,128]{2,1,0:T(8,128)(2,1)S(1)}, u32[]{:S(2)}) copy-start(bf16[59,80,128]{2,1,0:T(8,128)(2,1)S(1)} %collective-permute-done.5.by_core.left.mleft.aleft) | copy-start | bytes 3624964
  55.3 13.3 %copy-start.15 = (f32[8,32,128]{2,1,0:T(8,128)S(1)}, f32[8,32,128]{2,1,0:T(8,128)}, u32[]{:S(2)}) copy-start(f32[8,32,128]{2,1,0:T(8,128)} %absorb.9) | copy-start | bytes 393220
  68.6 5.2 %copy-start.18 = (bf16[25,4,16,128]{3,2,1,0:T(8,128)(2,1)S(1)}, bf16[25,4,16,128]{3,2,1,0:T(8,128)(2,1)}, u32[]{:S(2)}) copy-start(bf16[25,4,16,128]{3,2,1,0:T(8,128)(2,1)} %copy-done.17) | copy-start | bytes 1228804
  68.6 5.2 %copy-start.21 = (bf16[25,4,16,128]{3,2,1,0:T(8,128)(2,1)S(1)}, bf16[25,4,16,128]{3,2,1,0:T(8,128)(2,1)}, u32[]{:S(2)}) copy-start(bf16[25,4,16,128]{3,2,1,0:T(8,128)(2,1)} %copy-done.20) | copy-start | bytes 1228804
  73.8 1.4 copy-start.26
  73.8 1.4 copy-start.30
  79.1 19.2 %all-to-all-start.3 = ((f32[128,8,128]{2,1,0:T(8,128)}), f32[128,8,128]{2,1,0:T(8,128)S(1)}, u32[]{:S(2)}, u32[]{:S(2)}) async-start(f32[128,8,128]{2,1,0:T(8,128)} %get-tuple-element.57), calls=%async_computation.3 | async-start | bytes 1048576 | tf_op jit(solution)/shard_map/all_to_all | solution.py:813
  84.3 18.1 %copy-start.4 = (f32[17,4,8,128]{3,2,1,0:T(8,128)S(1)}, f32[17,4,8,128]{3,2,1,0:T(8,128)}, u32[]{:S(2)}) copy-start(f32[17,4,8,128]{3,2,1,0:T(8,128)} %copy-done.3) | copy-start | bytes 835588
  84.3 18.1 %copy-start.6 = (f32[17,4,8,128]{3,2,1,0:T(8,128)S(1)}, f32[17,4,8,128]{3,2,1,0:T(8,128)}, u32[]{:S(2)}) copy-start(f32[17,4,8,128]{3,2,1,0:T(8,128)} %copy-done.5) | copy-start | bytes 835588
  84.3 18.0 %collective-permute-start.7 = (f32[12,4,8,128]{3,2,1,0:T(8,128)}, f32[12,4,8,128]{3,2,1,0:T(8,128)}, u32[]{:S(2)}, u32[]{:S(2)}) collective-permute-start(f32[12,4,8,128]{3,2,1,0:T(8,128)} %get-tuple-element.61), channel_id=1, source_target_pairs={{0,1},{1,0},{2,3},{3,2},{4,5},{5,4},{6,7},{7,6},{8,9},{9,8},{10,11... | collective-permute-start | bytes 589832 | tf_op jit(solution)/shard_map/ppermute | solution.py:804
  85.8 16.6 %collective-permute-start.8 = (f32[12,4,8,128]{3,2,1,0:T(8,128)}, f32[12,4,8,128]{3,2,1,0:T(8,128)}, u32[]{:S(2)}, u32[]{:S(2)}) collective-permute-start(f32[12,4,8,128]{3,2,1,0:T(8,128)} %get-tuple-element.62), channel_id=1, source_target_pairs={{1,2},{3,4},{5,6},{7,8},{9,10},{11,12},{13,14},{2,1},{4,3},{6,5},{... | collective-permute-start | bytes 589832 | tf_op jit(solution)/shard_map/ppermute | solution.py:809
  98.4 1.0 copy-start.12
  99.3 3.1 %copy-start.24 = (f32[12,8,32,128]{3,2,1,0:T(8,128)S(1)}, f32[12,8,32,128]{3,2,1,0:T(8,128)}, u32[]{:S(2)}) copy-start(f32[12,8,32,128]{3,2,1,0:T(8,128)} %get-tuple-element.59.img) | copy-start | bytes 4718596
  103.8 13.6 %collective-permute-start.9 = (bf16[18,80,128]{2,1,0:T(8,128)(2,1)S(1)}, bf16[18,80,128]{2,1,0:T(8,128)(2,1)S(1)}, u32[]{:S(2)}, u32[]{:S(2)}) collective-permute-start(bf16[18,80,128]{2,1,0:T(8,128)(2,1)S(1)} %get-tuple-element.63), channel_id=1, source_target_pairs={{0,16},{16,0},{32,48},{48,32},{64,80},{80,64},{96,112},{112,96},{1... | collective-permute-start | bytes 1105928 | tf_op jit(solution)/shard_map/ppermute | solution.py:817
  104.5 12.9 %collective-permute-start.10 = (bf16[18,80,128]{2,1,0:T(8,128)(2,1)S(1)}, bf16[18,80,128]{2,1,0:T(8,128)(2,1)S(1)}, u32[]{:S(2)}, u32[]{:S(2)}) collective-permute-start(bf16[18,80,128]{2,1,0:T(8,128)(2,1)S(1)} %get-tuple-element.64), channel_id=1, source_target_pairs={{16,32},{48,64},{80,96},{32,16},{64,48},{96,80},{17,33},{49,65},{8... | collective-permute-start | bytes 1105928 | tf_op jit(solution)/shard_map/ppermute | solution.py:822
  117.4 12.6 %copy-start.1 = (bf16[59,80,128]{2,1,0:T(8,128)(2,1)S(1)}, bf16[59,80,128]{2,1,0:T(8,128)(2,1)}, u32[]{:S(2)}) copy-start(bf16[59,80,128]{2,1,0:T(8,128)(2,1)} %copy-done) | copy-start | bytes 3624964
  117.4 12.6 %copy-start.9 = (s32[3,8,32,128]{3,2,1,0:T(8,128)S(1)}, s32[3,8,32,128]{3,2,1,0:T(8,128)}, u32[]{:S(2)}) copy-start(s32[3,8,32,128]{3,2,1,0:T(8,128)} %masks.5) | copy-start | bytes 1179652
  117.5 12.6 %copy-start.16 = (f32[8,32,128]{2,1,0:T(8,128)S(1)}, f32[8,32,128]{2,1,0:T(8,128)}, u32[]{:S(2)}) copy-start(f32[8,32,128]{2,1,0:T(8,128)} %absorb.9) | copy-start | bytes 393220
  130.0 5.1 %copy-start.19 = (bf16[25,4,16,128]{3,2,1,0:T(8,128)(2,1)S(1)}, bf16[25,4,16,128]{3,2,1,0:T(8,128)(2,1)}, u32[]{:S(2)}) copy-start(bf16[25,4,16,128]{3,2,1,0:T(8,128)(2,1)} %copy-done.17) | copy-start | bytes 1228804
  130.0 5.1 %copy-start.22 = (bf16[25,4,16,128]{3,2,1,0:T(8,128)(2,1)S(1)}, bf16[25,4,16,128]{3,2,1,0:T(8,128)(2,1)}, u32[]{:S(2)}) copy-start(bf16[25,4,16,128]{3,2,1,0:T(8,128)(2,1)} %copy-done.20) | copy-start | bytes 1228804
  135.1 1.3 copy-start.27
  136.5 17.4 %copy-start.23 = (f32[12,8,32,128]{3,2,1,0:T(8,128)S(1)}, f32[12,8,32,128]{3,2,1,0:T(8,128)}, u32[]{:S(2)}) copy-start(f32[12,8,32,128]{3,2,1,0:T(8,128)} %get-tuple-element.77.dir1) | copy-start | bytes 4718596

commit v5 on v4

--- a/solution.py
+++ b/solution.py
@@ -607,7 +607,11 @@
     copies.append(pltpu.make_async_copy(y0_far, mine, sems.at[5]))
     for copy in copies[::-1]:
         copy.start()
-    are, aim = alphas(jnp.sum(every[...], axis=0)[6:7])
+    parts = every[...].reshape(8, 16, 8, 128)
+    parts = [parts[i] for i in range(8)]
+    while len(parts) > 1:
+        parts = [x + y for x, y in zip(parts[::2], parts[1::2])]
+    are, aim = alphas(jnp.sum(parts[0], axis=0)[6:7])
     alpha[:8] = are
     alpha[8:] = aim
     sub, lane = iota((8, 128), 0), iota((8, 128), 1)
@@ -618,10 +622,8 @@
         change = y - part
         return y - (are * change + aim * pltpu.roll(change, 64, 1))
 
-    def coarse(t, _):
+    for t in range(TILES):
         y0[t] = next_coarse(before[t].astype(F32), every[t])
-
-    lax.fori_loop(0, TILES, coarse, None, unroll=8)
     for copy in copies:
         copy.wait()
     p, q = own_place()
@@ -766,35 +768,35 @@
     )(ys, pe, dlow, dhigh, by_core, by_chip, depth, masks, absorb, res, local, part)
 
 
-def finish_kernel(every, alpha, dir1, dir2, res, img, solution, residual, two):
-    f = pl.program_id(0)
-
-    @pl.when(f == 0)
-    def _():
-        are, aim = alphas(jnp.sum(every[...], axis=0, keepdims=True))
-        two[:8] = are
-        two[8:] = aim
-
-    are, aim = alpha[pl.ds(f, 1), :], alpha[pl.ds(f + 8, 1), :]
-    bre, bim = two[pl.ds(f, 1), :], two[pl.ds(f + 8, 1), :]
-    sre, sim = complex_times(are, aim, dir1[0], dir1[1])
-    tre, tim = complex_times(bre, bim, dir2[0], dir2[1])
-    solution[0] = sre + tre
-    solution[1] = sim + tim
-    pre, pim = complex_times(bre, bim, img[0], img[1])
-    residual[0] = res[0] - pre
-    residual[1] = res[1] - pim
+def finish_kernel(every, alpha, dir1, dir2, res, img, sol_far, res_far, sol, left, sems):
+    are, aim = alpha[:8], alpha[8:]
+    bre, bim = alphas(jnp.sum(every[...], axis=0, keepdims=True))
+    copies = []
+    for f in range(FIELDS):
+        a, b, row = 2 * f, 2 * f + 1, slice(f, f + 1)
+        sre, sim = complex_times(are[row], aim[row], dir1[a], dir1[b])
+        tre, tim = complex_times(bre[row], bim[row], dir2[a], dir2[b])
+        sol[a] = sre + tre
+        sol[b] = sim + tim
+        pre, pim = complex_times(bre[row], bim[row], img[a], img[b])
+        left[a] = res[a] - pre
+        left[b] = res[b] - pim
+        two = pl.ds(a, 2)
+        for i, (here, there) in enumerate(((sol, sol_far), (left, res_far))):
+            copies.append(pltpu.make_async_copy(here.at[two], there.at[two], sems.at[2 * f + i]))
+            copies[-1].start()
+    for copy in copies:
+        copy.wait()
 
 
 def finish(every, alpha, dir1, dir2, res, img):
-    cells = fields(TX, TY, NZ)
+    cells = (12, TX, TY, NZ)
     return pl.pallas_call(
         finish_kernel,
-        grid=(FIELDS,),
-        in_specs=[fixed(TILES, 128), fixed(16, 128), cells, cells, cells, cells],
-        out_specs=[cells, cells],
-        out_shape=[shape(12, TX, TY, NZ)] * 2,
-        scratch_shapes=[pltpu.VMEM((16, 128), F32)],
+        in_specs=[whole()] * 6,
+        out_specs=[anywhere()] * 2,
+        out_shape=[far_shape(*cells)] * 2,
+        scratch_shapes=[pltpu.VMEM(cells, F32)] * 2 + [pltpu.SemaphoreType.DMA((2 * FIELDS,))],
         compiler_params=params(),
         name="finish",
     )(every, alpha, dir1, dir2, res, img)

time: 157 us -> 157 us (level)
  no operation moved by 1% of the time
where the time goes in v5:
time: 157 us; the launch traced here: 156 us
  blocking collectives  67.2 us (43%)
  Pallas kernels  35.8 us (23%)
  starting transfers between devices  30.8 us (20%)
  waiting for transfers between devices  16.5 us (11%)
  local copies, waits for them, and re-layouts  4.5 us (3%)
    all_to_all x5, blocking collectives, gather(): return lax.all_to_all(copies, axes, 0, 0, tiled=True)  67.2 us
    all_to_all x2, starting transfers between devices, gather(): return lax.all_to_all(copies, axes, 0, 0, tiled=True)  16.7 us
    all_to_all x2, waiting for transfers between devices, gather(): return lax.all_to_all(copies, axes, 0, 0, tiled=True)  15.2 us
    pallas_call x2, Pallas kernels, local_solve(): pl.pallas_call(local_kernel, grid=(FIELDS,), in_specs=[fields(TX, TY, NZ)...  10.3 us
    pallas_call x2, Pallas kernels, image_call(): pl.pallas_call(functools.partial(image_kernel, last), in_specs=[whole()]...  5.73 us
    pallas_call x1, Pallas kernels, first(): pl.pallas_call(first_kernel, in_specs=[anywhere()] * 6, out_specs=[anywhe...  4.53 us
    ppermute x2, starting transfers between devices, swap_chips(): return lax.ppermute(value, 'gx', ends + [(j, i) for i, j in ends])  4.42 us
    ppermute x3, starting transfers between devices, round_x(): return lax.ppermute(value, 'gx', [(i, (i + 2 * k) % GX) for i in range(GX)])  3.82 us
  transfers between devices with their start and end apart: 13, of which 4 were waited for; matrix products, arithmetic and copies ran while one was open for 1% of the time, Pallas kernels for 4%

profile of v5, /device:TPU:1, one launch (start us, length us, event | category | flops | bytes accessed | tf_op | source)
XLA Modules:
  0.0 156.0 jit_solution(3667251078646740657)
XLA Ops:
  0.6 0.0 copy-start.13
  0.7 0.0 copy-start.7
  0.7 0.0 copy-start.14
  0.7 4.5 %first.1 = (bf16[128,8,128]{2,1,0:T(8,128)(2,1)}, f32[256,128]{1,0:T(8,128)S(1)}, bf16[25,4,16,128]{3,2,1,0:T(8,128)(2,1)}, bf16[25,4,16,128]{3,2,1,0:T(8,128)(2,1)}, f32[8,128]{1,0:T(8,128)}) custom-call(f32[12,8,32,128]{3,2,1,0:T(8,128)} %bitcast.11, s32[3,8,32,128]{3,2,1,0:T(8,128)} %masks.5, f32[8,32,128]{2,1,0:T(8,128)} %absorb.9, ...), custom_call_target="tpu_custom_call" | custom-call | tf_op jit(solution)/shard_map/first/pallas_call | solution.py:196
  5.2 11.5 %all-to-all-start = ((bf16[128,8,128]{2,1,0:T(8,128)(2,1)}), bf16[128,8,128]{2,1,0:T(8,128)(2,1)S(1)}, u32[]{:S(2)}, u32[]{:S(2)}) async-start(bf16[128,8,128]{2,1,0:T(8,128)(2,1)} %get-tuple-element.42), calls=%async_computation | async-start | bytes 524288 | tf_op jit(solution)/shard_map/all_to_all | solution.py:815
  16.8 2.7 %collective-permute-start.2 = (bf16[5,128,128]{2,1,0:T(8,128)(2,1)S(1)}, bf16[5,128,128]{2,1,0:T(8,128)(2,1)}, u32[]{:S(2)}, u32[]{:S(2)}) collective-permute-start(bf16[5,128,128]{2,1,0:T(8,128)(2,1)S(1)} %bitcast.18), channel_id=1, source_target_pairs={{0,96},{16,112},{32,0},{48,16},{64,32},{80,48},{96,64},{112,80},{1... | collective-permute-start | bytes 491528 | tf_op jit(solution)/shard_map/ppermute | solution.py:828
  19.4 0.6 collective-permute-start.1
  20.0 0.6 collective-permute-start
  20.6 1.2 collective-permute-start.3
  21.8 0.7 collective-permute-start.4
  22.5 0.7 copy.10
  23.2 1.0 reshape.30.index
  24.2 3.9 %all-to-all-done.every.y0.before = bf16[128,8,128]{2,1,0:T(8,128)(2,1)S(1)} async-done(((bf16[128,8,128]{2,1,0:T(8,128)(2,1)}), bf16[128,8,128]{2,1,0:T(8,128)(2,1)S(1)}, u32[]{:S(2)}, u32[]{:S(2)}) %all-to-all-start) | async-done | bytes 262176 | tf_op jit(solution)/shard_map/all_to_all | solution.py:815
  28.2 0.7 copy-done.28
  28.9 0.8 tile_sweep.1
  29.7 0.0 collective-permute-done.2.b3
  29.7 1.0 collective-permute-done.b1
  30.7 18.8 %all_to_all.41.every = bf16[128,8,128]{2,1,0:T(8,128)(2,1)S(1)} all-to-all(bf16[128,8,128]{2,1,0:T(8,128)(2,1)S(1)} %tile_sweep.1), channel_id=1, replica_groups=mesh['gx'=8,'gy'=16] {'gx','gy'}, dimensions={0} | all-to-all | bytes 524288 | tf_op jit(solution)/shard_map/all_to_all | solution.py:815
  49.5 1.6 %slabs.1 = (bf16[59,80,128]{2,1,0:T(8,128)(2,1)S(1)}, bf16[27,80,128]{2,1,0:T(8,128)(2,1)S(1)}, f32[17,4,8,128]{3,2,1,0:T(8,128)S(1)}, f32[17,4,8,128]{3,2,1,0:T(8,128)S(1)}) custom-call(f32[12,8,32,128]{3,2,1,0:T(8,128)S(1)} %bitcast.12, s32[3,8,32,128]{3,2,1,0:T(8,128)S(1)} %copy-done.7, f32[8,32,128]{2,1,0:T(8,128)S(1)} %copy-done.14, ...), custom_call_target="tpu_custom_call" | custom-call | tf_op jit(solution)/shard_map/slabs/pallas_call | solution.py:296
  51.2 0.6 collective-permute-start.5
  51.8 2.3 %collective-permute-start.6 = (bf16[27,80,128]{2,1,0:T(8,128)(2,1)S(1)}, bf16[27,80,128]{2,1,0:T(8,128)(2,1)S(1)}, u32[]{:S(2)}, u32[]{:S(2)}) collective-permute-start(bf16[27,80,128]{2,1,0:T(8,128)(2,1)S(1)} %get-tuple-element.53), channel_id=1, source_target_pairs={{16,32},{48,64},{80,96},{32,16},{64,48},{96,80},{17,33},{49,65},{8... | collective-permute-start | bytes 1658888 | tf_op jit(solution)/shard_map/ppermute | solution.py:824
  54.1 0.2 collective-permute-done.5.by_core.left.mleft.aleft
  54.3 0.9 copy-done.11
  55.3 2.3 %column_sweep.2 = bf16[16,8,8,128]{3,2,1,0:T(8,128)(2,1)S(1)} custom-call(s32[640]{0:T(1024)S(1)} %reshape.30.index, bf16[128,8,128]{2,1,0:T(8,128)(2,1)S(1)} %all_to_all.41.every, bf16[128,8,128]{2,1,0:T(8,128)(2,1)S(1)} %copy-done.11, f32[8,128]{1,0:T(8,128)S(1)} %copy-done.29, bf16[5,128,128]{2,1,0:T(8,128)(2,1)S(1)} %bitcast.23, ...), custom_call_target="tpu_custom_call" | custom-call | tf_op jit(solution)/shard_map/column_sweep/pallas_call | solution.py:502
  57.6 10.9 %all_to_all.42 = bf16[16,8,8,128]{3,2,1,0:T(8,128)(2,1)S(1)} all-to-all(bf16[16,8,8,128]{3,2,1,0:T(8,128)(2,1)S(1)} %column_sweep.2), channel_id=1, replica_groups=mesh['gx'=8,'gy'=16] {'gy'}, dimensions={0} | all-to-all | bytes 524288 | tf_op jit(solution)/shard_map/all_to_all | solution.py:815
  68.5 0.0 collective-permute-done.6.right.mright.aright.by_chip
  68.6 5.2 %local.2 = (f32[12,8,32,128]{3,2,1,0:T(8,128)S(1)}, f32[12,8,32,128]{3,2,1,0:T(8,128)S(1)}) custom-call(f32[12,8,32,128]{3,2,1,0:T(8,128)S(1)} %bitcast.13, f32[17,4,8,128]{3,2,1,0:T(8,128)S(1)} %get-tuple-element.50.low.mlow.alow.elow.low0, f32[17,4,8,128]{3,2,1,0:T(8,128)S(1)} %get-tuple-element.51.high.mhigh.ahigh.ehigh.high0, ...), custom_call_target="tpu_custom_call" | custom-call | tf_op jit(solution)/shard_map/local/pallas_call | solution.py:425
  73.8 0.0 copy-start.30
  73.8 1.3 last_sweep.2.ys
  75.1 0.0 copy-done
  75.2 3.9 %image.2 = (f32[12,8,32,128]{3,2,1,0:T(8,128)}, f32[12,8,32,128]{3,2,1,0:T(8,128)}, f32[128,8,128]{2,1,0:T(8,128)}, f32[12,4,8,128]{3,2,1,0:T(8,128)}, f32[12,4,8,128]{3,2,1,0:T(8,128)}) custom-call(f32[5,8,128]{2,1,0:T(8,128)S(1)} %last_sweep.2.ys, f32[256,128]{1,0:T(8,128)S(1)} %copy-done.26, ...), custom_call_target="tpu_custom_call" | custom-call | tf_op jit(solution)/shard_map/image/pallas_call | solution.py:760
  79.1 5.2 %all-to-all-start.3 = ((f32[128,8,128]{2,1,0:T(8,128)}), f32[128,8,128]{2,1,0:T(8,128)S(1)}, u32[]{:S(2)}, u32[]{:S(2)}) async-start(f32[128,8,128]{2,1,0:T(8,128)} %get-tuple-element.57), calls=%async_computation.3 | async-start | bytes 1048576 | tf_op jit(solution)/shard_map/all_to_all | solution.py:815
  84.3 1.5 collective-permute-start.7
  85.8 1.3 collective-permute-start.8
  87.1 11.3 %all-to-all-done.3.every = f32[128,8,128]{2,1,0:T(8,128)S(1)} async-done(((f32[128,8,128]{2,1,0:T(8,128)}), f32[128,8,128]{2,1,0:T(8,128)S(1)}, u32[]{:S(2)}, u32[]{:S(2)}) %all-to-all-start.3) | async-done | bytes 524320 | tf_op jit(solution)/shard_map/all_to_all | solution.py:815
  98.4 0.9 copy-done.12
  99.3 2.8 %restart.1 = (bf16[16,8,8,128]{3,2,1,0:T(8,128)(2,1)S(1)}, f32[128,8,128]{2,1,0:T(8,128)S(1)}, f32[16,128]{1,0:T(8,128)S(1)}, bf16[4,5,128,128]{3,2,1,0:T(8,128)(2,1)S(1)}, bf16[32,80,128]{2,1,0:T(8,128)(2,1)S(1)}) custom-call(s32[640]{0:T(1024)S(1)} %reshape.30.index, f32[128,8,128]{2,1,0:T(8,128)S(1)} %all-to-all-done.3.every, ...), custom_call_target="tpu_custom_call" | custom-call | tf_op jit(solution)/shard_map/restart/pallas_call | solution.py:636
  102.2 1.5 update.1
  103.6 0.7 collective-permute-start.9
  104.3 2.2 %collective-permute-start.10 = (bf16[18,80,128]{2,1,0:T(8,128)(2,1)S(1)}, bf16[18,80,128]{2,1,0:T(8,128)(2,1)S(1)}, u32[]{:S(2)}, u32[]{:S(2)}) collective-permute-start(bf16[18,80,128]{2,1,0:T(8,128)(2,1)S(1)} %get-tuple-element.64), channel_id=1, source_target_pairs={{16,32},{48,64},{80,96},{32,16},{64,48},{96,80},{17,33},{49,65},{8... | collective-permute-start | bytes 1105928 | tf_op jit(solution)/shard_map/ppermute | solution.py:824
  106.5 10.8 %all_to_all.43 = bf16[16,8,8,128]{3,2,1,0:T(8,128)(2,1)S(1)} all-to-all(bf16[16,8,8,128]{3,2,1,0:T(8,128)(2,1)S(1)} %get-tuple-element.58), channel_id=1, replica_groups=mesh['gx'=8,'gy'=16] {'gy'}, dimensions={0} | all-to-all | bytes 524288 | tf_op jit(solution)/shard_map/all_to_all | solution.py:815
  117.2 1.4 column_sweep.3
  118.6 11.1 %all_to_all.44 = bf16[16,8,8,128]{3,2,1,0:T(8,128)(2,1)S(1)} all-to-all(bf16[16,8,8,128]{3,2,1,0:T(8,128)(2,1)S(1)} %column_sweep.3), channel_id=1, replica_groups=mesh['gx'=8,'gy'=16] {'gy'}, dimensions={0} | all-to-all | bytes 524288 | tf_op jit(solution)/shard_map/all_to_all | solution.py:815
  129.8 5.1 %local.3 = (f32[12,8,32,128]{3,2,1,0:T(8,128)S(1)}, f32[12,8,32,128]{3,2,1,0:T(8,128)S(1)}) custom-call(f32[12,8,32,128]{3,2,1,0:T(8,128)S(1)} %get-tuple-element.69.src.res, f32[12,4,8,128]{3,2,1,0:T(8,128)S(1)} %get-tuple-element.70.low, f32[12,4,8,128]{3,2,1,0:T(8,128)S(1)} %get-tuple-element.71.high, ...), custom_call_target="tpu_custom_call" | custom-call | tf_op jit(solution)/shard_map/local/pallas_call | solution.py:425
  134.9 1.3 last_sweep.3.ys
  136.3 1.8 %image.3 = (f32[12,8,32,128]{3,2,1,0:T(8,128)S(1)}, f32[12,8,32,128]{3,2,1,0:T(8,128)S(1)}, f32[128,128]{1,0:T(8,128)S(1)}) custom-call(f32[5,8,128]{2,1,0:T(8,128)S(1)} %last_sweep.3.ys, f32[256,128]{1,0:T(8,128)S(1)} %copy-done.27, f32[17,4,8,128]{3,2,1,0:T(8,128)S(1)} %copy-done.4, f32[17,4,8,128]{3,2,1,0:T(8,128)S(1)} %copy-done.6, ...), custom_call_target="tpu_custom_call" | custom-call | tf_op jit(solution)/shard_map/image/pallas_call | solution.py:760
  138.1 15.6 %all_to_all.45 = f32[128,1,128]{2,1,0:T(1,128)S(1)} all-to-all(f32[128,1,128]{2,1,0:T(1,128)S(1)} %bitcast.29), channel_id=1, replica_groups=mesh['gx'=8,'gy'=16] {'gx','gy'}, dimensions={0} | all-to-all | bytes 131072 | tf_op jit(solution)/shard_map/all_to_all | solution.py:815
  153.6 2.2 %finish.1 = (f32[12,8,32,128]{3,2,1,0:T(8,128)}, f32[12,8,32,128]{3,2,1,0:T(8,128)}) custom-call(f32[128,128]{1,0:T(8,128)S(1)} %bitcast.28, f32[16,128]{1,0:T(8,128)S(1)} %get-tuple-element.60.alpha, f32[12,8,32,128]{3,2,1,0:T(8,128)S(1)} %copy-done.23, f32[12,8,32,128]{3,2,1,0:T(8,128)S(1)} %get-tuple-element.78.dir2, ...), custom_call_target="tpu_custom_call" | custom-call | tf_op jit(solution)/shard_map/finish/pallas_call | solution.py:794
  (63 shorter events, 0.1 us)
Async XLA Ops:
  0.6 16.1 %copy-start.13 = (bf16[1,1,5,128,128]{4,3,2,1,0:T(8,128)(2,1)S(1)}, bf16[1,1,5,128,128]{4,3,2,1,0:T(8,128)(2,1)}, u32[]{:S(2)}) copy-start(bf16[1,1,5,128,128]{4,3,2,1,0:T(8,128)(2,1)} %param.12) | copy-start | bytes 491524
  0.6 21.8 %copy-start.31 = (s32[8,16,5]{1,0,2:T(8,128)S(1)}, s32[8,16,5]{1,0,2:T(8,128)}, u32[]{:S(2)}) copy-start(s32[8,16,5]{1,0,2:T(8,128)} %param.13) | copy-start | bytes 7684
  0.7 48.8 %copy-start.2 = (f32[3,2,2,8,32,128]{5,4,3,2,1,0:T(8,128)S(1)}, f32[3,2,2,8,32,128]{5,4,3,2,1,0:T(8,128)}, u32[]{:S(2)}) copy-start(f32[3,2,2,8,32,128]{5,4,3,2,1,0:T(8,128)} %param.7) | copy-start | bytes 4718596
  0.7 48.8 %copy-start.7 = (s32[3,8,32,128]{3,2,1,0:T(8,128)S(1)}, s32[3,8,32,128]{3,2,1,0:T(8,128)}, u32[]{:S(2)}) copy-start(s32[3,8,32,128]{3,2,1,0:T(8,128)} %masks.5) | copy-start | bytes 1179652
  0.7 48.8 %copy-start.14 = (f32[8,32,128]{2,1,0:T(8,128)S(1)}, f32[8,32,128]{2,1,0:T(8,128)}, u32[]{:S(2)}) copy-start(f32[8,32,128]{2,1,0:T(8,128)} %absorb.9) | copy-start | bytes 393220
  5.2 45.9 %copy-start.25 = (f32[256,128]{1,0:T(8,128)}, f32[256,128]{1,0:T(8,128)S(1)}, u32[]{:S(2)}) copy-start(f32[256,128]{1,0:T(8,128)S(1)} %get-tuple-element.46.pe) | copy-start | bytes 393220
  5.2 23.0 %all-to-all-start = ((bf16[128,8,128]{2,1,0:T(8,128)(2,1)}), bf16[128,8,128]{2,1,0:T(8,128)(2,1)S(1)}, u32[]{:S(2)}, u32[]{:S(2)}) async-start(bf16[128,8,128]{2,1,0:T(8,128)(2,1)} %get-tuple-element.42), calls=%async_computation | async-start | bytes 524288 | tf_op jit(solution)/shard_map/all_to_all | solution.py:815
  16.8 12.9 %collective-permute-start.2 = (bf16[5,128,128]{2,1,0:T(8,128)(2,1)S(1)}, bf16[5,128,128]{2,1,0:T(8,128)(2,1)}, u32[]{:S(2)}, u32[]{:S(2)}) collective-permute-start(bf16[5,128,128]{2,1,0:T(8,128)(2,1)S(1)} %bitcast.18), channel_id=1, source_target_pairs={{0,96},{16,112},{32,0},{48,16},{64,32},{80,48},{96,64},{112,80},{1... | collective-permute-start | bytes 491528 | tf_op jit(solution)/shard_map/ppermute | solution.py:828
  19.4 10.3 %collective-permute-start.1 = (bf16[5,128,128]{2,1,0:T(8,128)(2,1)S(1)}, bf16[5,128,128]{2,1,0:T(8,128)(2,1)}, u32[]{:S(2)}, u32[]{:S(2)}) collective-permute-start(bf16[5,128,128]{2,1,0:T(8,128)(2,1)S(1)} %bitcast.19), channel_id=1, source_target_pairs={{0,64},{16,80},{32,96},{48,112},{64,0},{80,16},{96,32},{112,48},{1... | collective-permute-start | bytes 491528 | tf_op jit(solution)/shard_map/ppermute | solution.py:828
  20.0 10.7 %collective-permute-start = (bf16[5,128,128]{2,1,0:T(8,128)(2,1)S(1)}, bf16[5,128,128]{2,1,0:T(8,128)(2,1)}, u32[]{:S(2)}, u32[]{:S(2)}) collective-permute-start(bf16[5,128,128]{2,1,0:T(8,128)(2,1)S(1)} %bitcast.20), channel_id=1, source_target_pairs={{0,32},{16,48},{32,64},{48,80},{64,96},{80,112},{96,0},{112,16},{1... | collective-permute-start | bytes 491528 | tf_op jit(solution)/shard_map/ppermute | solution.py:828
  20.6 28.9 %collective-permute-start.3 = (bf16[25,4,16,128]{3,2,1,0:T(8,128)(2,1)}, bf16[25,4,16,128]{3,2,1,0:T(8,128)(2,1)S(1)}, u32[]{:S(2)}, u32[]{:S(2)}) collective-permute-start(bf16[25,4,16,128]{3,2,1,0:T(8,128)(2,1)} %get-tuple-element.47), channel_id=1, source_target_pairs={{0,1},{1,0},{2,3},{3,2},{4,5},{5,4},{6,7},{7,6},{8,9},{9,8},{10,11... | collective-permute-start | bytes 1228808 | tf_op jit(solution)/shard_map/ppermute | solution.py:806
  21.8 27.7 %collective-permute-start.4 = (bf16[25,4,16,128]{3,2,1,0:T(8,128)(2,1)}, bf16[25,4,16,128]{3,2,1,0:T(8,128)(2,1)S(1)}, u32[]{:S(2)}, u32[]{:S(2)}) collective-permute-start(bf16[25,4,16,128]{3,2,1,0:T(8,128)(2,1)} %get-tuple-element.48), channel_id=1, source_target_pairs={{1,2},{3,4},{5,6},{7,8},{9,10},{11,12},{13,14},{2,1},{4,3},{6,5},{... | collective-permute-start | bytes 1228808 | tf_op jit(solution)/shard_map/ppermute | solution.py:811
  28.2 23.0 %copy-start.10 = (bf16[128,8,128]{2,1,0:T(8,128)(2,1)}, bf16[128,8,128]{2,1,0:T(8,128)(2,1)S(1)}, u32[]{:S(2)}) copy-start(bf16[128,8,128]{2,1,0:T(8,128)(2,1)S(1)} %all-to-all-done.every.y0.before) | copy-start | bytes 786436
  28.2 0.7 copy-start.28
  49.5 4.8 %copy-start.29 = (f32[8,128]{1,0:T(8,128)S(1)}, f32[8,128]{1,0:T(8,128)}, u32[]{:S(2)}) copy-start(f32[8,128]{1,0:T(8,128)} %get-tuple-element.43.y0.y0_own.y0_far) | copy-start | bytes 12292
  49.5 1.7 %copy-start.17 = (bf16[25,4,16,128]{3,2,1,0:T(8,128)(2,1)}, bf16[25,4,16,128]{3,2,1,0:T(8,128)(2,1)S(1)}, u32[]{:S(2)}) copy-start(bf16[25,4,16,128]{3,2,1,0:T(8,128)(2,1)S(1)} %collective-permute-done.3.inner) | copy-start | bytes 1228804
  49.5 1.6 %copy-start.20 = (bf16[25,4,16,128]{3,2,1,0:T(8,128)(2,1)}, bf16[25,4,16,128]{3,2,1,0:T(8,128)(2,1)S(1)}, u32[]{:S(2)}) copy-start(bf16[25,4,16,128]{3,2,1,0:T(8,128)(2,1)S(1)} %collective-permute-done.4.outer) | copy-start | bytes 1228804
  51.2 24.0 %copy-start.3 = (f32[17,4,8,128]{3,2,1,0:T(8,128)}, f32[17,4,8,128]{3,2,1,0:T(8,128)S(1)}, u32[]{:S(2)}) copy-start(f32[17,4,8,128]{3,2,1,0:T(8,128)S(1)} %get-tuple-element.50.low.mlow.alow.elow.low0) | copy-start | bytes 835588
  51.2 23.9 %copy-start.5 = (f32[17,4,8,128]{3,2,1,0:T(8,128)}, f32[17,4,8,128]{3,2,1,0:T(8,128)S(1)}, u32[]{:S(2)}) copy-start(f32[17,4,8,128]{3,2,1,0:T(8,128)S(1)} %get-tuple-element.51.high.mhigh.ahigh.ehigh.high0) | copy-start | bytes 835588
  51.2 3.1 %collective-permute-start.5 = (bf16[59,80,128]{2,1,0:T(8,128)(2,1)S(1)}, bf16[59,80,128]{2,1,0:T(8,128)(2,1)S(1)}, u32[]{:S(2)}, u32[]{:S(2)}) collective-permute-start(bf16[59,80,128]{2,1,0:T(8,128)(2,1)S(1)} %get-tuple-element.49), channel_id=1, source_target_pairs={{0,16},{16,0},{32,48},{48,32},{64,80},{80,64},{96,112},{112,96},{1... | collective-permute-start | bytes 3624968 | tf_op jit(solution)/shard_map/ppermute | solution.py:819
  51.8 16.8 %copy-start.8 = (s32[3,8,32,128]{3,2,1,0:T(8,128)S(1)}, s32[3,8,32,128]{3,2,1,0:T(8,128)}, u32[]{:S(2)}) copy-start(s32[3,8,32,128]{3,2,1,0:T(8,128)} %masks.5) | copy-start | bytes 1179652
  51.8 16.8 %collective-permute-start.6 = (bf16[27,80,128]{2,1,0:T(8,128)(2,1)S(1)}, bf16[27,80,128]{2,1,0:T(8,128)(2,1)S(1)}, u32[]{:S(2)}, u32[]{:S(2)}) collective-permute-start(bf16[27,80,128]{2,1,0:T(8,128)(2,1)S(1)} %get-tuple-element.53), channel_id=1, source_target_pairs={{16,32},{48,64},{80,96},{32,16},{64,48},{96,80},{17,33},{49,65},{8... | collective-permute-start | bytes 1658888 | tf_op jit(solution)/shard_map/ppermute | solution.py:824
  54.3 1.0 copy-start.11
  55.3 19.9 %copy-start = (bf16[59,80,128]{2,1,0:T(8,128)(2,1)}, bf16[59,80,128]{2,1,0:T(8,128)(2,1)S(1)}, u32[]{:S(2)}) copy-start(bf16[59,80,128]{2,1,0:T(8,128)(2,1)S(1)} %collective-permute-done.5.by_core.left.mleft.aleft) | copy-start | bytes 3624964
  55.3 13.3 %copy-start.15 = (f32[8,32,128]{2,1,0:T(8,128)S(1)}, f32[8,32,128]{2,1,0:T(8,128)}, u32[]{:S(2)}) copy-start(f32[8,32,128]{2,1,0:T(8,128)} %absorb.9) | copy-start | bytes 393220
  68.6 5.2 %copy-start.18 = (bf16[25,4,16,128]{3,2,1,0:T(8,128)(2,1)S(1)}, bf16[25,4,16,128]{3,2,1,0:T(8,128)(2,1)}, u32[]{:S(2)}) copy-start(bf16[25,4,16,128]{3,2,1,0:T(8,128)(2,1)} %copy-done.17) | copy-start | bytes 1228804
  68.6 5.2 %copy-start.21 = (bf16[25,4,16,128]{3,2,1,0:T(8,128)(2,1)S(1)}, bf16[25,4,16,128]{3,2,1,0:T(8,128)(2,1)}, u32[]{:S(2)}) copy-start(bf16[25,4,16,128]{3,2,1,0:T(8,128)(2,1)} %copy-done.20) | copy-start | bytes 1228804
  73.8 1.4 copy-start.26
  73.8 1.4 copy-start.30
  79.1 19.2 %all-to-all-start.3 = ((f32[128,8,128]{2,1,0:T(8,128)}), f32[128,8,128]{2,1,0:T(8,128)S(1)}, u32[]{:S(2)}, u32[]{:S(2)}) async-start(f32[128,8,128]{2,1,0:T(8,128)} %get-tuple-element.57), calls=%async_computation.3 | async-start | bytes 1048576 | tf_op jit(solution)/shard_map/all_to_all | solution.py:815
  84.3 17.9 %copy-start.4 = (f32[17,4,8,128]{3,2,1,0:T(8,128)S(1)}, f32[17,4,8,128]{3,2,1,0:T(8,128)}, u32[]{:S(2)}) copy-start(f32[17,4,8,128]{3,2,1,0:T(8,128)} %copy-done.3) | copy-start | bytes 835588
  84.3 17.9 %copy-start.6 = (f32[17,4,8,128]{3,2,1,0:T(8,128)S(1)}, f32[17,4,8,128]{3,2,1,0:T(8,128)}, u32[]{:S(2)}) copy-start(f32[17,4,8,128]{3,2,1,0:T(8,128)} %copy-done.5) | copy-start | bytes 835588
  84.3 17.8 %collective-permute-start.7 = (f32[12,4,8,128]{3,2,1,0:T(8,128)}, f32[12,4,8,128]{3,2,1,0:T(8,128)}, u32[]{:S(2)}, u32[]{:S(2)}) collective-permute-start(f32[12,4,8,128]{3,2,1,0:T(8,128)} %get-tuple-element.61), channel_id=1, source_target_pairs={{0,1},{1,0},{2,3},{3,2},{4,5},{5,4},{6,7},{7,6},{8,9},{9,8},{10,11... | collective-permute-start | bytes 589832 | tf_op jit(solution)/shard_map/ppermute | solution.py:806
  85.8 16.4 %collective-permute-start.8 = (f32[12,4,8,128]{3,2,1,0:T(8,128)}, f32[12,4,8,128]{3,2,1,0:T(8,128)}, u32[]{:S(2)}, u32[]{:S(2)}) collective-permute-start(f32[12,4,8,128]{3,2,1,0:T(8,128)} %get-tuple-element.62), channel_id=1, source_target_pairs={{1,2},{3,4},{5,6},{7,8},{9,10},{11,12},{13,14},{2,1},{4,3},{6,5},{... | collective-permute-start | bytes 589832 | tf_op jit(solution)/shard_map/ppermute | solution.py:811
  98.4 1.0 copy-start.12
  99.3 2.8 %copy-start.24 = (f32[12,8,32,128]{3,2,1,0:T(8,128)S(1)}, f32[12,8,32,128]{3,2,1,0:T(8,128)}, u32[]{:S(2)}) copy-start(f32[12,8,32,128]{3,2,1,0:T(8,128)} %get-tuple-element.59.img) | copy-start | bytes 4718596
  103.6 13.6 %collective-permute-start.9 = (bf16[18,80,128]{2,1,0:T(8,128)(2,1)S(1)}, bf16[18,80,128]{2,1,0:T(8,128)(2,1)S(1)}, u32[]{:S(2)}, u32[]{:S(2)}) collective-permute-start(bf16[18,80,128]{2,1,0:T(8,128)(2,1)S(1)} %get-tuple-element.63), channel_id=1, source_target_pairs={{0,16},{16,0},{32,48},{48,32},{64,80},{80,64},{96,112},{112,96},{1... | collective-permute-start | bytes 1105928 | tf_op jit(solution)/shard_map/ppermute | solution.py:819
  104.3 12.9 %collective-permute-start.10 = (bf16[18,80,128]{2,1,0:T(8,128)(2,1)S(1)}, bf16[18,80,128]{2,1,0:T(8,128)(2,1)S(1)}, u32[]{:S(2)}, u32[]{:S(2)}) collective-permute-start(bf16[18,80,128]{2,1,0:T(8,128)(2,1)S(1)} %get-tuple-element.64), channel_id=1, source_target_pairs={{16,32},{48,64},{80,96},{32,16},{64,48},{96,80},{17,33},{49,65},{8... | collective-permute-start | bytes 1105928 | tf_op jit(solution)/shard_map/ppermute | solution.py:824
  117.2 12.6 %copy-start.1 = (bf16[59,80,128]{2,1,0:T(8,128)(2,1)S(1)}, bf16[59,80,128]{2,1,0:T(8,128)(2,1)}, u32[]{:S(2)}) copy-start(bf16[59,80,128]{2,1,0:T(8,128)(2,1)} %copy-done) | copy-start | bytes 3624964
  117.2 12.6 %copy-start.9 = (s32[3,8,32,128]{3,2,1,0:T(8,128)S(1)}, s32[3,8,32,128]{3,2,1,0:T(8,128)}, u32[]{:S(2)}) copy-start(s32[3,8,32,128]{3,2,1,0:T(8,128)} %masks.5) | copy-start | bytes 1179652
  117.2 12.6 %copy-start.16 = (f32[8,32,128]{2,1,0:T(8,128)S(1)}, f32[8,32,128]{2,1,0:T(8,128)}, u32[]{:S(2)}) copy-start(f32[8,32,128]{2,1,0:T(8,128)} %absorb.9) | copy-start | bytes 393220
  129.8 5.1 %copy-start.19 = (bf16[25,4,16,128]{3,2,1,0:T(8,128)(2,1)S(1)}, bf16[25,4,16,128]{3,2,1,0:T(8,128)(2,1)}, u32[]{:S(2)}) copy-start(bf16[25,4,16,128]{3,2,1,0:T(8,128)(2,1)} %copy-done.17) | copy-start | bytes 1228804
  129.8 5.1 %copy-start.22 = (bf16[25,4,16,128]{3,2,1,0:T(8,128)(2,1)S(1)}, bf16[25,4,16,128]{3,2,1,0:T(8,128)(2,1)}, u32[]{:S(2)}) copy-start(bf16[25,4,16,128]{3,2,1,0:T(8,128)(2,1)} %copy-done.20) | copy-start | bytes 1228804
  134.9 1.3 copy-start.27
  136.3 17.4 %copy-start.23 = (f32[12,8,32,128]{3,2,1,0:T(8,128)S(1)}, f32[12,8,32,128]{3,2,1,0:T(8,128)}, u32[]{:S(2)}) copy-start(f32[12,8,32,128]{3,2,1,0:T(8,128)} %get-tuple-element.77.dir1) | copy-start | bytes 4718596

commit v6 on v5

--- a/solution.py
+++ b/solution.py
@@ -363,7 +363,7 @@
         i, by_chip_on = (p + 3, 0) if p < 0 else (p - TX, 1)
         return jnp.where(core == by_chip_on, slab_part(by_chip, i, c), slab_part(by_core, i, c))
 
-    which = (pl.program_id(0) // 2) % 2
+    which = pl.program_id(0) % 2
     for p in range(-3, TX + 3):
         i = p + 3
         if 0 <= p < TX:
@@ -374,15 +374,8 @@
         dre = 5.5 - m
         inside = dim > 1.0
         scale = 1.0 / jnp.where(inside, dre * dre + dim * dim, 1.0)
-        ire = jnp.where(inside, dre * scale, 0.0)
-        iim = jnp.where(inside, -dim * scale, 0.0)
-        inv[0, i] = ire
-        inv[1, i] = iim
-        re = plane(src[0], low[0], high[0], left, right, 0, p)
-        im = plane(src[1], low[1], high[1], left, right, 1, p)
-        r[0, i] = re
-        r[1, i] = im
-        z1[0, i], z1[1, i] = complex_times(ire, iim, re, im)
+        inv[0, i] = jnp.where(inside, dre * scale, 0.0)
+        inv[1, i] = jnp.where(inside, -dim * scale, 0.0)
 
     def near(z, c, i):
         mid = z[c, i]
@@ -391,21 +384,31 @@
         total = total + jnp.where(lane == 0, 0.0, pltpu.roll(mid, 1, 1))
         return total + jnp.where(lane == NZ - 1, 0.0, pltpu.roll(mid, NZ - 1, 1))
 
-    for i in range(1, TX + 5):
-        re = r[0, i] + near(z1, 0, i)
-        im = r[1, i] + near(z1, 1, i)
-        z2[0, i], z2[1, i] = complex_times(inv[0, i], inv[1, i], re, im)
-    for i in range(2, TX + 4):
-        re = r[0, i] + near(z2, 0, i)
-        im = r[1, i] + near(z2, 1, i)
-        zre, zim = complex_times(inv[0, i], inv[1, i], re, im)
-        z3[0, i], z3[1, i] = zre, zim
-        if 3 <= i < TX + 3:
-            local[0, i - 3], local[1, i - 3] = zre[:TY], zim[:TY]
-            image[0, i - 3], image[1, i - 3] = re[:TY], im[:TY]
-    for i in range(3, TX + 3):
-        for c in range(2):
-            image[c, i - 3] = image[c, i - 3] - near(z3, c, i)[:TY]
+    for s in range(2):
+        u, w = 2 * s, 2 * s + 1
+        sides = left.at[3 * s : 3 * s + 3], right.at[3 * s : 3 * s + 3]
+        for p in range(-3, TX + 3):
+            i = p + 3
+            re = plane(src[u], low[u], high[u], *sides, 0, p)
+            im = plane(src[w], low[w], high[w], *sides, 1, p)
+            r[0, i] = re
+            r[1, i] = im
+            z1[0, i], z1[1, i] = complex_times(inv[0, i], inv[1, i], re, im)
+        for i in range(1, TX + 5):
+            re = r[0, i] + near(z1, 0, i)
+            im = r[1, i] + near(z1, 1, i)
+            z2[0, i], z2[1, i] = complex_times(inv[0, i], inv[1, i], re, im)
+        for i in range(2, TX + 4):
+            re = r[0, i] + near(z2, 0, i)
+            im = r[1, i] + near(z2, 1, i)
+            zre, zim = complex_times(inv[0, i], inv[1, i], re, im)
+            z3[0, i], z3[1, i] = zre, zim
+            if 3 <= i < TX + 3:
+                local[u, i - 3], local[w, i - 3] = zre[:TY], zim[:TY]
+                image[u, i - 3], image[w, i - 3] = re[:TY], im[:TY]
+        for i in range(3, TX + 3):
+            for c in range(2):
+                image[u + c, i - 3] = image[u + c, i - 3] - near(z3, c, i)[:TY]
 
 
 def channel(offset, *dims):
@@ -416,23 +419,28 @@
     return pl.BlockSpec((3, SLAB, NZ), lambda f: (which(f), 0, 0))
 
 
+def four(*shape):
+    return pl.BlockSpec((4,) + shape, lambda f: (f,) + (0,) * len(shape))
+
+
 def local_solve(res, low, high, left, right, masks, absorb, dlow, dhigh, dleft, dright):
-    of_mask = lambda f: 12 + f // 2
+    of_mask = lambda f: 12 + f
     of_absorb = lambda f: 15
     y = (4, 8, NZ)
-    pair, mask_pair, absorb_pair = slab_of(lambda f: f), slab_of(lambda f: 6 + f // 4), slab_of(lambda f: 7)
+    pair = pl.BlockSpec((6, SLAB, NZ), lambda f: (f, 0, 0))
+    mask_pair, absorb_pair = slab_of(lambda f: 6 + f // 2), slab_of(lambda f: 7)
     planes = pltpu.VMEM((2, TX + 6, TY + 8, NZ), F32)
     return pl.pallas_call(
         local_kernel,
-        grid=(FIELDS,),
+        grid=(3,),
         in_specs=[
-            fields(TX, TY, NZ), fields(*y), fields(*y), pair, pair,
-            channel(lambda f: f // 2, TX, TY, NZ),
+            four(TX, TY, NZ), four(*y), four(*y), pair, pair,
+            channel(lambda f: f, TX, TY, NZ),
             channel(of_mask, *y), channel(of_mask, *y), mask_pair, mask_pair,
             fixed(TX, TY, NZ),
             channel(of_absorb, *y), channel(of_absorb, *y), absorb_pair, absorb_pair,
         ],
-        out_specs=[fields(TX, TY, NZ)] * 2,
+        out_specs=[four(TX, TY, NZ)] * 2,
         out_shape=[shape(12, TX, TY, NZ)] * 2,
         scratch_shapes=[planes] * 5,
         compiler_params=params(),

time: 157 us -> 156 us (level)
  no operation moved by 1% of the time
where the time goes in v6:
time: 156 us; the launch traced here: 155 us
  blocking collectives  67.1 us (43%)
  Pallas kernels  34.7 us (22%)
  starting transfers between devices  30.8 us (20%)
  waiting for transfers between devices  16.5 us (11%)
  local copies, waits for them, and re-layouts  4.5 us (3%)
    all_to_all x5, blocking collectives, gather(): return lax.all_to_all(copies, axes, 0, 0, tiled=True)  67.1 us
    all_to_all x2, starting transfers between devices, gather(): return lax.all_to_all(copies, axes, 0, 0, tiled=True)  16.6 us
    all_to_all x2, waiting for transfers between devices, gather(): return lax.all_to_all(copies, axes, 0, 0, tiled=True)  15.2 us
    pallas_call x2, Pallas kernels, local_solve(): pl.pallas_call(local_kernel, grid=(3,), in_specs=[four(TX, TY, NZ), four(...  9.23 us
    pallas_call x2, Pallas kernels, image_call(): pl.pallas_call(functools.partial(image_kernel, last), in_specs=[whole()]...  5.73 us
    pallas_call x1, Pallas kernels, first(): pl.pallas_call(first_kernel, in_specs=[anywhere()] * 6, out_specs=[anywhe...  4.53 us
    ppermute x2, starting transfers between devices, swap_chips(): return lax.ppermute(value, 'gx', ends + [(j, i) for i, j in ends])  4.42 us
    ppermute x3, starting transfers between devices, round_x(): return lax.ppermute(value, 'gx', [(i, (i + 2 * k) % GX) for i in range(GX)])  3.82 us
  transfers between devices with their start and end apart: 13, of which 4 were waited for; matrix products, arithmetic and copies ran while one was open for 1% of the time, Pallas kernels for 4%

profile of v6, /device:TPU:1, one launch (start us, length us, event | category | flops | bytes accessed | tf_op | source)
XLA Modules:
  0.0 154.9 jit_solution(14502241245249411835)
XLA Ops:
  0.6 0.0 copy-start.13
  0.7 0.0 copy-start.7
  0.7 0.0 copy-start.14
  0.7 4.5 %first.1 = (bf16[128,8,128]{2,1,0:T(8,128)(2,1)}, f32[256,128]{1,0:T(8,128)S(1)}, bf16[25,4,16,128]{3,2,1,0:T(8,128)(2,1)}, bf16[25,4,16,128]{3,2,1,0:T(8,128)(2,1)}, f32[8,128]{1,0:T(8,128)}) custom-call(f32[12,8,32,128]{3,2,1,0:T(8,128)} %bitcast.11, s32[3,8,32,128]{3,2,1,0:T(8,128)} %masks.5, f32[8,32,128]{2,1,0:T(8,128)} %absorb.9, ...), custom_call_target="tpu_custom_call" | custom-call | tf_op jit(solution)/shard_map/first/pallas_call | solution.py:196
  5.2 11.5 %all-to-all-start = ((bf16[128,8,128]{2,1,0:T(8,128)(2,1)}), bf16[128,8,128]{2,1,0:T(8,128)(2,1)S(1)}, u32[]{:S(2)}, u32[]{:S(2)}) async-start(bf16[128,8,128]{2,1,0:T(8,128)(2,1)} %get-tuple-element.42), calls=%async_computation | async-start | bytes 524288 | tf_op jit(solution)/shard_map/all_to_all | solution.py:823
  16.8 2.7 %collective-permute-start.2 = (bf16[5,128,128]{2,1,0:T(8,128)(2,1)S(1)}, bf16[5,128,128]{2,1,0:T(8,128)(2,1)}, u32[]{:S(2)}, u32[]{:S(2)}) collective-permute-start(bf16[5,128,128]{2,1,0:T(8,128)(2,1)S(1)} %bitcast.18), channel_id=1, source_target_pairs={{0,96},{16,112},{32,0},{48,16},{64,32},{80,48},{96,64},{112,80},{1... | collective-permute-start | bytes 491528 | tf_op jit(solution)/shard_map/ppermute | solution.py:836
  19.4 0.6 collective-permute-start.1
  20.0 0.6 collective-permute-start
  20.6 1.2 collective-permute-start.3
  21.8 0.7 collective-permute-start.4
  22.5 0.7 copy.10
  23.2 1.0 reshape.30.index
  24.2 3.9 %all-to-all-done.every.y0.before = bf16[128,8,128]{2,1,0:T(8,128)(2,1)S(1)} async-done(((bf16[128,8,128]{2,1,0:T(8,128)(2,1)}), bf16[128,8,128]{2,1,0:T(8,128)(2,1)S(1)}, u32[]{:S(2)}, u32[]{:S(2)}) %all-to-all-start) | async-done | bytes 262176 | tf_op jit(solution)/shard_map/all_to_all | solution.py:823
  28.2 0.7 copy-done.28
  28.9 0.8 tile_sweep.1
  29.7 0.0 collective-permute-done.2.b3
  29.7 1.0 collective-permute-done.b1
  30.7 18.8 %all_to_all.41.every = bf16[128,8,128]{2,1,0:T(8,128)(2,1)S(1)} all-to-all(bf16[128,8,128]{2,1,0:T(8,128)(2,1)S(1)} %tile_sweep.1), channel_id=1, replica_groups=mesh['gx'=8,'gy'=16] {'gx','gy'}, dimensions={0} | all-to-all | bytes 524288 | tf_op jit(solution)/shard_map/all_to_all | solution.py:823
  49.5 1.6 %slabs.1 = (bf16[59,80,128]{2,1,0:T(8,128)(2,1)S(1)}, bf16[27,80,128]{2,1,0:T(8,128)(2,1)S(1)}, f32[17,4,8,128]{3,2,1,0:T(8,128)S(1)}, f32[17,4,8,128]{3,2,1,0:T(8,128)S(1)}) custom-call(f32[12,8,32,128]{3,2,1,0:T(8,128)S(1)} %bitcast.12, s32[3,8,32,128]{3,2,1,0:T(8,128)S(1)} %copy-done.7, f32[8,32,128]{2,1,0:T(8,128)S(1)} %copy-done.14, ...), custom_call_target="tpu_custom_call" | custom-call | tf_op jit(solution)/shard_map/slabs/pallas_call | solution.py:296
  51.2 0.6 collective-permute-start.5
  51.8 2.3 %collective-permute-start.6 = (bf16[27,80,128]{2,1,0:T(8,128)(2,1)S(1)}, bf16[27,80,128]{2,1,0:T(8,128)(2,1)S(1)}, u32[]{:S(2)}, u32[]{:S(2)}) collective-permute-start(bf16[27,80,128]{2,1,0:T(8,128)(2,1)S(1)} %get-tuple-element.53), channel_id=1, source_target_pairs={{16,32},{48,64},{80,96},{32,16},{64,48},{96,80},{17,33},{49,65},{8... | collective-permute-start | bytes 1658888 | tf_op jit(solution)/shard_map/ppermute | solution.py:832
  54.1 0.2 collective-permute-done.5.by_core.left.mleft.aleft
  54.3 0.9 copy-done.11
  55.3 2.3 %column_sweep.2 = bf16[16,8,8,128]{3,2,1,0:T(8,128)(2,1)S(1)} custom-call(s32[640]{0:T(1024)S(1)} %reshape.30.index, bf16[128,8,128]{2,1,0:T(8,128)(2,1)S(1)} %all_to_all.41.every, bf16[128,8,128]{2,1,0:T(8,128)(2,1)S(1)} %copy-done.11, f32[8,128]{1,0:T(8,128)S(1)} %copy-done.29, bf16[5,128,128]{2,1,0:T(8,128)(2,1)S(1)} %bitcast.23, ...), custom_call_target="tpu_custom_call" | custom-call | tf_op jit(solution)/shard_map/column_sweep/pallas_call | solution.py:510
  57.6 10.9 %all_to_all.42 = bf16[16,8,8,128]{3,2,1,0:T(8,128)(2,1)S(1)} all-to-all(bf16[16,8,8,128]{3,2,1,0:T(8,128)(2,1)S(1)} %column_sweep.2), channel_id=1, replica_groups=mesh['gx'=8,'gy'=16] {'gy'}, dimensions={0} | all-to-all | bytes 524288 | tf_op jit(solution)/shard_map/all_to_all | solution.py:823
  68.5 0.0 collective-permute-done.6.right.mright.aright.by_chip
  68.6 4.7 %local.2 = (f32[12,8,32,128]{3,2,1,0:T(8,128)S(1)}, f32[12,8,32,128]{3,2,1,0:T(8,128)S(1)}) custom-call(f32[12,8,32,128]{3,2,1,0:T(8,128)S(1)} %bitcast.13, f32[17,4,8,128]{3,2,1,0:T(8,128)S(1)} %get-tuple-element.50.low.mlow.alow.elow.low0, f32[17,4,8,128]{3,2,1,0:T(8,128)S(1)} %get-tuple-element.51.high.mhigh.ahigh.ehigh.high0, ...), custom_call_target="tpu_custom_call" | custom-call | tf_op jit(solution)/shard_map/local/pallas_call | solution.py:433
  73.3 0.0 copy-start.30
  73.3 1.3 last_sweep.2.ys
  74.6 0.0 copy-done
  74.7 3.9 %image.2 = (f32[12,8,32,128]{3,2,1,0:T(8,128)}, f32[12,8,32,128]{3,2,1,0:T(8,128)}, f32[128,8,128]{2,1,0:T(8,128)}, f32[12,4,8,128]{3,2,1,0:T(8,128)}, f32[12,4,8,128]{3,2,1,0:T(8,128)}) custom-call(f32[5,8,128]{2,1,0:T(8,128)S(1)} %last_sweep.2.ys, f32[256,128]{1,0:T(8,128)S(1)} %copy-done.26, ...), custom_call_target="tpu_custom_call" | custom-call | tf_op jit(solution)/shard_map/image/pallas_call | solution.py:768
  78.6 5.2 %all-to-all-start.3 = ((f32[128,8,128]{2,1,0:T(8,128)}), f32[128,8,128]{2,1,0:T(8,128)S(1)}, u32[]{:S(2)}, u32[]{:S(2)}) async-start(f32[128,8,128]{2,1,0:T(8,128)} %get-tuple-element.57), calls=%async_computation.3 | async-start | bytes 1048576 | tf_op jit(solution)/shard_map/all_to_all | solution.py:823
  83.8 1.5 collective-permute-start.7
  85.2 1.3 collective-permute-start.8
  86.6 11.3 %all-to-all-done.3.every = f32[128,8,128]{2,1,0:T(8,128)S(1)} async-done(((f32[128,8,128]{2,1,0:T(8,128)}), f32[128,8,128]{2,1,0:T(8,128)S(1)}, u32[]{:S(2)}, u32[]{:S(2)}) %all-to-all-start.3) | async-done | bytes 524320 | tf_op jit(solution)/shard_map/all_to_all | solution.py:823
  97.8 0.9 copy-done.12
  98.8 2.8 %restart.1 = (bf16[16,8,8,128]{3,2,1,0:T(8,128)(2,1)S(1)}, f32[128,8,128]{2,1,0:T(8,128)S(1)}, f32[16,128]{1,0:T(8,128)S(1)}, bf16[4,5,128,128]{3,2,1,0:T(8,128)(2,1)S(1)}, bf16[32,80,128]{2,1,0:T(8,128)(2,1)S(1)}) custom-call(s32[640]{0:T(1024)S(1)} %reshape.30.index, f32[128,8,128]{2,1,0:T(8,128)S(1)} %all-to-all-done.3.every, ...), custom_call_target="tpu_custom_call" | custom-call | tf_op jit(solution)/shard_map/restart/pallas_call | solution.py:644
  101.6 1.5 update.1
  103.1 0.7 collective-permute-start.9
  103.8 2.1 %collective-permute-start.10 = (bf16[18,80,128]{2,1,0:T(8,128)(2,1)S(1)}, bf16[18,80,128]{2,1,0:T(8,128)(2,1)S(1)}, u32[]{:S(2)}, u32[]{:S(2)}) collective-permute-start(bf16[18,80,128]{2,1,0:T(8,128)(2,1)S(1)} %get-tuple-element.64), channel_id=1, source_target_pairs={{16,32},{48,64},{80,96},{32,16},{64,48},{96,80},{17,33},{49,65},{8... | collective-permute-start | bytes 1105928 | tf_op jit(solution)/shard_map/ppermute | solution.py:832
  105.9 10.8 %all_to_all.43 = bf16[16,8,8,128]{3,2,1,0:T(8,128)(2,1)S(1)} all-to-all(bf16[16,8,8,128]{3,2,1,0:T(8,128)(2,1)S(1)} %get-tuple-element.58), channel_id=1, replica_groups=mesh['gx'=8,'gy'=16] {'gy'}, dimensions={0} | all-to-all | bytes 524288 | tf_op jit(solution)/shard_map/all_to_all | solution.py:823
  116.7 1.4 column_sweep.3
  118.1 11.1 %all_to_all.44 = bf16[16,8,8,128]{3,2,1,0:T(8,128)(2,1)S(1)} all-to-all(bf16[16,8,8,128]{3,2,1,0:T(8,128)(2,1)S(1)} %column_sweep.3), channel_id=1, replica_groups=mesh['gx'=8,'gy'=16] {'gy'}, dimensions={0} | all-to-all | bytes 524288 | tf_op jit(solution)/shard_map/all_to_all | solution.py:823
  129.3 4.6 %local.3 = (f32[12,8,32,128]{3,2,1,0:T(8,128)S(1)}, f32[12,8,32,128]{3,2,1,0:T(8,128)S(1)}) custom-call(f32[12,8,32,128]{3,2,1,0:T(8,128)S(1)} %get-tuple-element.69.src.res, f32[12,4,8,128]{3,2,1,0:T(8,128)S(1)} %get-tuple-element.70.low, f32[12,4,8,128]{3,2,1,0:T(8,128)S(1)} %get-tuple-element.71.high, ...), custom_call_target="tpu_custom_call" | custom-call | tf_op jit(solution)/shard_map/local/pallas_call | solution.py:433
  133.9 1.3 last_sweep.3.ys
  135.2 1.8 %image.3 = (f32[12,8,32,128]{3,2,1,0:T(8,128)S(1)}, f32[12,8,32,128]{3,2,1,0:T(8,128)S(1)}, f32[128,128]{1,0:T(8,128)S(1)}) custom-call(f32[5,8,128]{2,1,0:T(8,128)S(1)} %last_sweep.3.ys, f32[256,128]{1,0:T(8,128)S(1)} %copy-done.27, f32[17,4,8,128]{3,2,1,0:T(8,128)S(1)} %copy-done.4, f32[17,4,8,128]{3,2,1,0:T(8,128)S(1)} %copy-done.6, ...), custom_call_target="tpu_custom_call" | custom-call | tf_op jit(solution)/shard_map/image/pallas_call | solution.py:768
  137.0 15.5 %all_to_all.45 = f32[128,1,128]{2,1,0:T(1,128)S(1)} all-to-all(f32[128,1,128]{2,1,0:T(1,128)S(1)} %bitcast.29), channel_id=1, replica_groups=mesh['gx'=8,'gy'=16] {'gx','gy'}, dimensions={0} | all-to-all | bytes 131072 | tf_op jit(solution)/shard_map/all_to_all | solution.py:823
  152.6 2.2 %finish.1 = (f32[12,8,32,128]{3,2,1,0:T(8,128)}, f32[12,8,32,128]{3,2,1,0:T(8,128)}) custom-call(f32[128,128]{1,0:T(8,128)S(1)} %bitcast.28, f32[16,128]{1,0:T(8,128)S(1)} %get-tuple-element.60.alpha, f32[12,8,32,128]{3,2,1,0:T(8,128)S(1)} %copy-done.23, f32[12,8,32,128]{3,2,1,0:T(8,128)S(1)} %get-tuple-element.78.dir2, ...), custom_call_target="tpu_custom_call" | custom-call | tf_op jit(solution)/shard_map/finish/pallas_call | solution.py:802
  (63 shorter events, 0.1 us)
Async XLA Ops:
  0.6 16.1 %copy-start.13 = (bf16[1,1,5,128,128]{4,3,2,1,0:T(8,128)(2,1)S(1)}, bf16[1,1,5,128,128]{4,3,2,1,0:T(8,128)(2,1)}, u32[]{:S(2)}) copy-start(bf16[1,1,5,128,128]{4,3,2,1,0:T(8,128)(2,1)} %param.12) | copy-start | bytes 491524
  0.6 21.8 %copy-start.31 = (s32[8,16,5]{1,0,2:T(8,128)S(1)}, s32[8,16,5]{1,0,2:T(8,128)}, u32[]{:S(2)}) copy-start(s32[8,16,5]{1,0,2:T(8,128)} %param.13) | copy-start | bytes 7684
  0.7 48.8 %copy-start.2 = (f32[3,2,2,8,32,128]{5,4,3,2,1,0:T(8,128)S(1)}, f32[3,2,2,8,32,128]{5,4,3,2,1,0:T(8,128)}, u32[]{:S(2)}) copy-start(f32[3,2,2,8,32,128]{5,4,3,2,1,0:T(8,128)} %param.7) | copy-start | bytes 4718596
  0.7 48.8 %copy-start.7 = (s32[3,8,32,128]{3,2,1,0:T(8,128)S(1)}, s32[3,8,32,128]{3,2,1,0:T(8,128)}, u32[]{:S(2)}) copy-start(s32[3,8,32,128]{3,2,1,0:T(8,128)} %masks.5) | copy-start | bytes 1179652
  0.7 48.8 %copy-start.14 = (f32[8,32,128]{2,1,0:T(8,128)S(1)}, f32[8,32,128]{2,1,0:T(8,128)}, u32[]{:S(2)}) copy-start(f32[8,32,128]{2,1,0:T(8,128)} %absorb.9) | copy-start | bytes 393220
  5.2 45.9 %copy-start.25 = (f32[256,128]{1,0:T(8,128)}, f32[256,128]{1,0:T(8,128)S(1)}, u32[]{:S(2)}) copy-start(f32[256,128]{1,0:T(8,128)S(1)} %get-tuple-element.46.pe) | copy-start | bytes 393220
  5.2 23.0 %all-to-all-start = ((bf16[128,8,128]{2,1,0:T(8,128)(2,1)}), bf16[128,8,128]{2,1,0:T(8,128)(2,1)S(1)}, u32[]{:S(2)}, u32[]{:S(2)}) async-start(bf16[128,8,128]{2,1,0:T(8,128)(2,1)} %get-tuple-element.42), calls=%async_computation | async-start | bytes 524288 | tf_op jit(solution)/shard_map/all_to_all | solution.py:823
  16.8 12.9 %collective-permute-start.2 = (bf16[5,128,128]{2,1,0:T(8,128)(2,1)S(1)}, bf16[5,128,128]{2,1,0:T(8,128)(2,1)}, u32[]{:S(2)}, u32[]{:S(2)}) collective-permute-start(bf16[5,128,128]{2,1,0:T(8,128)(2,1)S(1)} %bitcast.18), channel_id=1, source_target_pairs={{0,96},{16,112},{32,0},{48,16},{64,32},{80,48},{96,64},{112,80},{1... | collective-permute-start | bytes 491528 | tf_op jit(solution)/shard_map/ppermute | solution.py:836
  19.4 10.3 %collective-permute-start.1 = (bf16[5,128,128]{2,1,0:T(8,128)(2,1)S(1)}, bf16[5,128,128]{2,1,0:T(8,128)(2,1)}, u32[]{:S(2)}, u32[]{:S(2)}) collective-permute-start(bf16[5,128,128]{2,1,0:T(8,128)(2,1)S(1)} %bitcast.19), channel_id=1, source_target_pairs={{0,64},{16,80},{32,96},{48,112},{64,0},{80,16},{96,32},{112,48},{1... | collective-permute-start | bytes 491528 | tf_op jit(solution)/shard_map/ppermute | solution.py:836
  20.0 10.7 %collective-permute-start = (bf16[5,128,128]{2,1,0:T(8,128)(2,1)S(1)}, bf16[5,128,128]{2,1,0:T(8,128)(2,1)}, u32[]{:S(2)}, u32[]{:S(2)}) collective-permute-start(bf16[5,128,128]{2,1,0:T(8,128)(2,1)S(1)} %bitcast.20), channel_id=1, source_target_pairs={{0,32},{16,48},{32,64},{48,80},{64,96},{80,112},{96,0},{112,16},{1... | collective-permute-start | bytes 491528 | tf_op jit(solution)/shard_map/ppermute | solution.py:836
  20.6 28.9 %collective-permute-start.3 = (bf16[25,4,16,128]{3,2,1,0:T(8,128)(2,1)}, bf16[25,4,16,128]{3,2,1,0:T(8,128)(2,1)S(1)}, u32[]{:S(2)}, u32[]{:S(2)}) collective-permute-start(bf16[25,4,16,128]{3,2,1,0:T(8,128)(2,1)} %get-tuple-element.47), channel_id=1, source_target_pairs={{0,1},{1,0},{2,3},{3,2},{4,5},{5,4},{6,7},{7,6},{8,9},{9,8},{10,11... | collective-permute-start | bytes 1228808 | tf_op jit(solution)/shard_map/ppermute | solution.py:814
  21.8 27.7 %collective-permute-start.4 = (bf16[25,4,16,128]{3,2,1,0:T(8,128)(2,1)}, bf16[25,4,16,128]{3,2,1,0:T(8,128)(2,1)S(1)}, u32[]{:S(2)}, u32[]{:S(2)}) collective-permute-start(bf16[25,4,16,128]{3,2,1,0:T(8,128)(2,1)} %get-tuple-element.48), channel_id=1, source_target_pairs={{1,2},{3,4},{5,6},{7,8},{9,10},{11,12},{13,14},{2,1},{4,3},{6,5},{... | collective-permute-start | bytes 1228808 | tf_op jit(solution)/shard_map/ppermute | solution.py:819
  28.2 23.0 %copy-start.10 = (bf16[128,8,128]{2,1,0:T(8,128)(2,1)}, bf16[128,8,128]{2,1,0:T(8,128)(2,1)S(1)}, u32[]{:S(2)}) copy-start(bf16[128,8,128]{2,1,0:T(8,128)(2,1)S(1)} %all-to-all-done.every.y0.before) | copy-start | bytes 786436
  28.2 0.7 copy-start.28
  49.5 4.8 %copy-start.29 = (f32[8,128]{1,0:T(8,128)S(1)}, f32[8,128]{1,0:T(8,128)}, u32[]{:S(2)}) copy-start(f32[8,128]{1,0:T(8,128)} %get-tuple-element.43.y0.y0_own.y0_far) | copy-start | bytes 12292
  49.5 1.7 %copy-start.17 = (bf16[25,4,16,128]{3,2,1,0:T(8,128)(2,1)}, bf16[25,4,16,128]{3,2,1,0:T(8,128)(2,1)S(1)}, u32[]{:S(2)}) copy-start(bf16[25,4,16,128]{3,2,1,0:T(8,128)(2,1)S(1)} %collective-permute-done.3.inner) | copy-start | bytes 1228804
  49.5 1.6 %copy-start.20 = (bf16[25,4,16,128]{3,2,1,0:T(8,128)(2,1)}, bf16[25,4,16,128]{3,2,1,0:T(8,128)(2,1)S(1)}, u32[]{:S(2)}) copy-start(bf16[25,4,16,128]{3,2,1,0:T(8,128)(2,1)S(1)} %collective-permute-done.4.outer) | copy-start | bytes 1228804
  51.2 23.4 %copy-start.3 = (f32[17,4,8,128]{3,2,1,0:T(8,128)}, f32[17,4,8,128]{3,2,1,0:T(8,128)S(1)}, u32[]{:S(2)}) copy-start(f32[17,4,8,128]{3,2,1,0:T(8,128)S(1)} %get-tuple-element.50.low.mlow.alow.elow.low0) | copy-start | bytes 835588
  51.2 23.4 %copy-start.5 = (f32[17,4,8,128]{3,2,1,0:T(8,128)}, f32[17,4,8,128]{3,2,1,0:T(8,128)S(1)}, u32[]{:S(2)}) copy-start(f32[17,4,8,128]{3,2,1,0:T(8,128)S(1)} %get-tuple-element.51.high.mhigh.ahigh.ehigh.high0) | copy-start | bytes 835588
  51.2 3.1 %collective-permute-start.5 = (bf16[59,80,128]{2,1,0:T(8,128)(2,1)S(1)}, bf16[59,80,128]{2,1,0:T(8,128)(2,1)S(1)}, u32[]{:S(2)}, u32[]{:S(2)}) collective-permute-start(bf16[59,80,128]{2,1,0:T(8,128)(2,1)S(1)} %get-tuple-element.49), channel_id=1, source_target_pairs={{0,16},{16,0},{32,48},{48,32},{64,80},{80,64},{96,112},{112,96},{1... | collective-permute-start | bytes 3624968 | tf_op jit(solution)/shard_map/ppermute | solution.py:827
  51.8 16.8 %copy-start.8 = (s32[3,8,32,128]{3,2,1,0:T(8,128)S(1)}, s32[3,8,32,128]{3,2,1,0:T(8,128)}, u32[]{:S(2)}) copy-start(s32[3,8,32,128]{3,2,1,0:T(8,128)} %masks.5) | copy-start | bytes 1179652
  51.8 16.8 %collective-permute-start.6 = (bf16[27,80,128]{2,1,0:T(8,128)(2,1)S(1)}, bf16[27,80,128]{2,1,0:T(8,128)(2,1)S(1)}, u32[]{:S(2)}, u32[]{:S(2)}) collective-permute-start(bf16[27,80,128]{2,1,0:T(8,128)(2,1)S(1)} %get-tuple-element.53), channel_id=1, source_target_pairs={{16,32},{48,64},{80,96},{32,16},{64,48},{96,80},{17,33},{49,65},{8... | collective-permute-start | bytes 1658888 | tf_op jit(solution)/shard_map/ppermute | solution.py:832
  54.3 1.0 copy-start.11
  55.3 19.4 %copy-start = (bf16[59,80,128]{2,1,0:T(8,128)(2,1)}, bf16[59,80,128]{2,1,0:T(8,128)(2,1)S(1)}, u32[]{:S(2)}) copy-start(bf16[59,80,128]{2,1,0:T(8,128)(2,1)S(1)} %collective-permute-done.5.by_core.left.mleft.aleft) | copy-start | bytes 3624964
  55.3 13.3 %copy-start.15 = (f32[8,32,128]{2,1,0:T(8,128)S(1)}, f32[8,32,128]{2,1,0:T(8,128)}, u32[]{:S(2)}) copy-start(f32[8,32,128]{2,1,0:T(8,128)} %absorb.9) | copy-start | bytes 393220
  68.6 4.7 %copy-start.18 = (bf16[25,4,16,128]{3,2,1,0:T(8,128)(2,1)S(1)}, bf16[25,4,16,128]{3,2,1,0:T(8,128)(2,1)}, u32[]{:S(2)}) copy-start(bf16[25,4,16,128]{3,2,1,0:T(8,128)(2,1)} %copy-done.17) | copy-start | bytes 1228804
  68.6 4.7 %copy-start.21 = (bf16[25,4,16,128]{3,2,1,0:T(8,128)(2,1)S(1)}, bf16[25,4,16,128]{3,2,1,0:T(8,128)(2,1)}, u32[]{:S(2)}) copy-start(bf16[25,4,16,128]{3,2,1,0:T(8,128)(2,1)} %copy-done.20) | copy-start | bytes 1228804
  73.2 1.4 copy-start.26
  73.3 1.4 copy-start.30
  78.6 19.2 %all-to-all-start.3 = ((f32[128,8,128]{2,1,0:T(8,128)}), f32[128,8,128]{2,1,0:T(8,128)S(1)}, u32[]{:S(2)}, u32[]{:S(2)}) async-start(f32[128,8,128]{2,1,0:T(8,128)} %get-tuple-element.57), calls=%async_computation.3 | async-start | bytes 1048576 | tf_op jit(solution)/shard_map/all_to_all | solution.py:823
  83.8 17.9 %copy-start.4 = (f32[17,4,8,128]{3,2,1,0:T(8,128)S(1)}, f32[17,4,8,128]{3,2,1,0:T(8,128)}, u32[]{:S(2)}) copy-start(f32[17,4,8,128]{3,2,1,0:T(8,128)} %copy-done.3) | copy-start | bytes 835588
  83.8 17.9 %copy-start.6 = (f32[17,4,8,128]{3,2,1,0:T(8,128)S(1)}, f32[17,4,8,128]{3,2,1,0:T(8,128)}, u32[]{:S(2)}) copy-start(f32[17,4,8,128]{3,2,1,0:T(8,128)} %copy-done.5) | copy-start | bytes 835588
  83.8 17.8 %collective-permute-start.7 = (f32[12,4,8,128]{3,2,1,0:T(8,128)}, f32[12,4,8,128]{3,2,1,0:T(8,128)}, u32[]{:S(2)}, u32[]{:S(2)}) collective-permute-start(f32[12,4,8,128]{3,2,1,0:T(8,128)} %get-tuple-element.61), channel_id=1, source_target_pairs={{0,1},{1,0},{2,3},{3,2},{4,5},{5,4},{6,7},{7,6},{8,9},{9,8},{10,11... | collective-permute-start | bytes 589832 | tf_op jit(solution)/shard_map/ppermute | solution.py:814
  85.2 16.4 %collective-permute-start.8 = (f32[12,4,8,128]{3,2,1,0:T(8,128)}, f32[12,4,8,128]{3,2,1,0:T(8,128)}, u32[]{:S(2)}, u32[]{:S(2)}) collective-permute-start(f32[12,4,8,128]{3,2,1,0:T(8,128)} %get-tuple-element.62), channel_id=1, source_target_pairs={{1,2},{3,4},{5,6},{7,8},{9,10},{11,12},{13,14},{2,1},{4,3},{6,5},{... | collective-permute-start | bytes 589832 | tf_op jit(solution)/shard_map/ppermute | solution.py:819
  97.8 1.0 copy-start.12
  98.8 2.8 %copy-start.24 = (f32[12,8,32,128]{3,2,1,0:T(8,128)S(1)}, f32[12,8,32,128]{3,2,1,0:T(8,128)}, u32[]{:S(2)}) copy-start(f32[12,8,32,128]{3,2,1,0:T(8,128)} %get-tuple-element.59.img) | copy-start | bytes 4718596
  103.1 13.6 %collective-permute-start.9 = (bf16[18,80,128]{2,1,0:T(8,128)(2,1)S(1)}, bf16[18,80,128]{2,1,0:T(8,128)(2,1)S(1)}, u32[]{:S(2)}, u32[]{:S(2)}) collective-permute-start(bf16[18,80,128]{2,1,0:T(8,128)(2,1)S(1)} %get-tuple-element.63), channel_id=1, source_target_pairs={{0,16},{16,0},{32,48},{48,32},{64,80},{80,64},{96,112},{112,96},{1... | collective-permute-start | bytes 1105928 | tf_op jit(solution)/shard_map/ppermute | solution.py:827
  103.8 12.9 %collective-permute-start.10 = (bf16[18,80,128]{2,1,0:T(8,128)(2,1)S(1)}, bf16[18,80,128]{2,1,0:T(8,128)(2,1)S(1)}, u32[]{:S(2)}, u32[]{:S(2)}) collective-permute-start(bf16[18,80,128]{2,1,0:T(8,128)(2,1)S(1)} %get-tuple-element.64), channel_id=1, source_target_pairs={{16,32},{48,64},{80,96},{32,16},{64,48},{96,80},{17,33},{49,65},{8... | collective-permute-start | bytes 1105928 | tf_op jit(solution)/shard_map/ppermute | solution.py:832
  116.7 12.6 %copy-start.1 = (bf16[59,80,128]{2,1,0:T(8,128)(2,1)S(1)}, bf16[59,80,128]{2,1,0:T(8,128)(2,1)}, u32[]{:S(2)}) copy-start(bf16[59,80,128]{2,1,0:T(8,128)(2,1)} %copy-done) | copy-start | bytes 3624964
  116.7 12.6 %copy-start.9 = (s32[3,8,32,128]{3,2,1,0:T(8,128)S(1)}, s32[3,8,32,128]{3,2,1,0:T(8,128)}, u32[]{:S(2)}) copy-start(s32[3,8,32,128]{3,2,1,0:T(8,128)} %masks.5) | copy-start | bytes 1179652
  116.7 12.6 %copy-start.16 = (f32[8,32,128]{2,1,0:T(8,128)S(1)}, f32[8,32,128]{2,1,0:T(8,128)}, u32[]{:S(2)}) copy-start(f32[8,32,128]{2,1,0:T(8,128)} %absorb.9) | copy-start | bytes 393220
  129.3 4.6 %copy-start.19 = (bf16[25,4,16,128]{3,2,1,0:T(8,128)(2,1)S(1)}, bf16[25,4,16,128]{3,2,1,0:T(8,128)(2,1)}, u32[]{:S(2)}) copy-start(bf16[25,4,16,128]{3,2,1,0:T(8,128)(2,1)} %copy-done.17) | copy-start | bytes 1228804
  129.3 4.6 %copy-start.22 = (bf16[25,4,16,128]{3,2,1,0:T(8,128)(2,1)S(1)}, bf16[25,4,16,128]{3,2,1,0:T(8,128)(2,1)}, u32[]{:S(2)}) copy-start(bf16[25,4,16,128]{3,2,1,0:T(8,128)(2,1)} %copy-done.20) | copy-start | bytes 1228804
  133.9 1.3 copy-start.27
  135.2 17.4 %copy-start.23 = (f32[12,8,32,128]{3,2,1,0:T(8,128)S(1)}, f32[12,8,32,128]{3,2,1,0:T(8,128)}, u32[]{:S(2)}) copy-start(f32[12,8,32,128]{3,2,1,0:T(8,128)} %get-tuple-element.77.dir1) | copy-start | bytes 4718596
